TPU v7x, 512 devices: a whole 4x8x8 slice. The times are simulated.
512 devices in a mesh: dp: 64 (over z, x, core), tp: 8 (over y).
Axes of the slice: x: 4, y: 8, z: 8, core: 2. Of those that a mesh axis runs over, the one named last changes fastest.
Arguments:
- queries: bfloat16 [64, 4, 128, 576], P('dp', None, 'tp')
- new_latents: bfloat16 [64, 4, 576], P('dp'), may hold values from -6 to 6
- latent_cache: bfloat16 [64, 512, 576], P('dp')
- lengths: int32 [64], P('dp'), may hold values from 32 to 512, as said below
- slot_of: int32 [64], replicated, may hold values from 0 to 63, each once
- value_maps: bfloat16 [128, 512, 128], P('tp'), may hold values from -0.25 to 0.25
- out_proj: bfloat16 [16384, 7168], P('tp', 'dp'), may hold values from -0.046875 to 0.046875
- residual: bfloat16 [256, 7168], P(None, 'dp'), may hold values from -6 to 6
- norm_gain: bfloat16 [7168], P('dp'), may hold values from 0.25 to 1.75
- w_gate: bfloat16 [7168, 18432], P('dp', 'tp'), may hold values from -0.0625 to 0.0625
- w_up: bfloat16 [7168, 18432], P('dp', 'tp'), may hold values from -0.0625 to 0.0625
- w_down: bfloat16 [18432, 7168], P('tp', 'dp'), may hold values from -0.046875 to 0.046875
Outputs:
- layer_out: bfloat16 [256, 7168], P('tp', 'dp')
Inputs may be any that keep to these rules, and one draw needn't show every extreme that they name: `lengths`: lengths differ widely between requests; some request has a full cache of 512 positions.
All inputs are finite; a program needn't handle non-finite values.
Results may differ from a plain program's by a relative error of at most 0.013.
Values may be sent and summed in bfloat16 or wider, within the bound.
No kernel may reach another device: no remote copies, remote signals or barrier semaphores. Data moves between devices by JAX's collectives and lax.ppermute only.
A program may use at most 64 MiB of HBM per device.

v0:
```python
import jax
import jax.numpy as jnp
from jax import lax
from jax.sharding import PartitionSpec as P

D = 7168


score_scale = 192.0 ** (-0.5)
norm_eps = 1e-06


def local(
    queries,
    new_latents,
    latent_cache,
    lengths,
    slot_of,
    value_maps,
    out_proj,
    residual,
    norm_gain,
    w_gate,
    w_up,
    w_down,
):
    step_count = queries.shape[1]
    cache_len = latent_cache.shape[1]
    latent_width = value_maps.shape[1]
    score_cache = (
        jnp.einsum("rshc,rlc->rshl", queries, latent_cache, preferred_element_type=jnp.float32)
        * score_scale
    )
    score_new = (
        jnp.einsum("rshc,ruc->rshu", queries, new_latents, preferred_element_type=jnp.float32)
        * score_scale
    )
    position = jnp.arange(cache_len, dtype=jnp.int32)
    keep_cache = (position[None, :] < lengths[:, None])[:, None, None, :]
    step_ids = jnp.arange(step_count, dtype=jnp.int32)
    keep_new = (step_ids[None, :] <= step_ids[:, None])[None, :, None, :]
    row_max = jnp.maximum(
        jnp.max(jnp.where(keep_cache, score_cache, -1e30), axis=3, keepdims=True),
        jnp.max(jnp.where(keep_new, score_new, -1e30), axis=3, keepdims=True),
    )
    weight_cache = jnp.where(keep_cache, jnp.exp(score_cache - row_max), 0.0)
    weight_new = jnp.where(keep_new, jnp.exp(score_new - row_max), 0.0)
    softmax_total = jnp.sum(weight_cache, axis=3, keepdims=True) + jnp.sum(
        weight_new, axis=3, keepdims=True
    )
    prob_cache = (weight_cache / softmax_total).astype(jnp.bfloat16)
    prob_new = (weight_new / softmax_total).astype(jnp.bfloat16)
    context = jnp.einsum(
        "rshl,rlc->rshc",
        prob_cache,
        latent_cache[:, :, :latent_width],
        preferred_element_type=jnp.float32,
    )
    context = context + jnp.einsum(
        "rshu,ruc->rshc",
        prob_new,
        new_latents[:, :, :latent_width],
        preferred_element_type=jnp.float32,
    )
    context = context.astype(jnp.bfloat16)
    head_values = jnp.einsum(
        "rshc,hcd->rshd", context, value_maps, preferred_element_type=jnp.float32
    ).astype(jnp.bfloat16)
    head_values = head_values.reshape(
        head_values.shape[0] * step_count, head_values.shape[2] * head_values.shape[3]
    )
    projected = jnp.dot(
        lax.all_gather(head_values, "dp", axis=0, tiled=True),
        out_proj,
        preferred_element_type=jnp.float32,
    )
    row_order = (slot_of[:, None] * step_count + step_ids[None, :]).reshape(-1)
    projected = jnp.take(projected, row_order, axis=0)
    total_rows = projected.shape[0]
    share_rows = total_rows // lax.axis_size("tp")
    tp_index = lax.axis_index("tp")
    gain_float = norm_gain.astype(jnp.float32)
    attended = lax.psum(projected, "tp")
    hidden = residual.astype(jnp.float32) + attended
    square_sums = lax.psum(jnp.sum(hidden * hidden, axis=1), "dp")
    normed = (hidden * lax.rsqrt(square_sums[:, None] / D + norm_eps) * gain_float).astype(
        jnp.bfloat16
    )
    kept_rows = lax.dynamic_slice_in_dim(hidden, tp_index * share_rows, share_rows, 0)
    gate_part = jnp.dot(normed, w_gate, preferred_element_type=jnp.float32)
    up_part = jnp.dot(normed, w_up, preferred_element_type=jnp.float32)
    gate_sum, up_sum = (
        lax.psum_scatter(gate_part, "dp", scatter_dimension=1, tiled=True),
        lax.psum_scatter(up_part, "dp", scatter_dimension=1, tiled=True),
    )
    hidden_units = (jax.nn.silu(gate_sum) * up_sum).astype(jnp.bfloat16)
    down_term = jnp.dot(
        lax.all_gather(hidden_units, "dp", axis=1, tiled=True),
        w_down,
        preferred_element_type=jnp.float32,
    )
    ffn_share = lax.psum_scatter(
        down_term.astype(jnp.bfloat16), "tp", scatter_dimension=0, tiled=True
    ).astype(jnp.float32)
    return (kept_rows + ffn_share).astype(jnp.bfloat16)


def solution(mesh):
    placed = (
        P("dp", None, "tp", None),
        P("dp", None, None),
        P("dp", None, None),
        P("dp"),
        P(),
        P("tp", None, None),
        P("tp", "dp"),
        P(None, "dp"),
        P("dp"),
        P("dp", "tp"),
        P("dp", "tp"),
        P("tp", "dp"),
    )
    return jax.shard_map(
        local, mesh=mesh, in_specs=placed, out_specs=P("tp", "dp"), check_vma=False
    )
```

profile of v0, /device:TPU:2, one launch (start us, length us, event | category | flops | bytes accessed | tf_op | source)
XLA Modules:
  0.0 696.9 jit_solution(16247497361390380140)
XLA Ops:
  7.4 1.4 select_reduce_fusion
  11.2 1.3 fusion.2
  14.0 86.0 %all-gather.5.cloned.1.call-done = bf16[64,4,2048]{2,1,0:T(4,128)(2,1)} async-done(((bf16[1,4,2048]{2,1,0:T(4,128)(2,1)}), bf16[64,4,2048]{2,1,0:T(4,128)(2,1)}) %all-gather.5.cloned.1.call-update) | async-done | bytes 1048592 | tf_op jit(solution)/shard_map/all_gather | solution.py:73
  100.0 1.3 reshape.165
  101.3 1.5 fusion.31
  104.5 75.0 %all-reduce.7.cloned.1.call-done = f32[256,112]{1,0:T(8,128)} async-done(((f32[256,112]{1,0:T(8,128)}), f32[256,112]{1,0:T(8,128)}) %all-reduce.7.cloned.1.call-update) | async-done | bytes 114704 | tf_op jit(solution)/shard_map/psum | solution.py:83
  180.6 119.7 %psum.15 = f32[256]{0:T(256)S(1)} all-reduce(f32[256]{0:T(256)S(1)} %get-tuple-element.9), channel_id=1, replica_groups=mesh['dp'=64,'tp'=8] {'dp'}, use_global_device_ids=true, to_apply=%region_6.7 | all-reduce | flops 256 | bytes 2048 | tf_op jit(solution)/shard_map/psum | solution.py:85
  300.3 2.0 fusion.29
  302.3 2.0 fusion.28
  304.3 146.6 %fusion.30 = (f32[256,48]{0,1:T(8,128)S(1)}, f32[256,48]{0,1:T(8,128)S(1)}) fusion(f32[256,2304]{0,1:T(8,128)} %fusion.28, f32[256,2304]{0,1:T(8,128)} %fusion.29), kind=kCustom, calls=%all-reduce-scatter.2 | all-reduce-scatter fusion | flops 1572865 | bytes 4818944
  450.9 1.3 collective-permute-start.15
  452.2 8.2 %collective-permute-start.31 = (f32[256,36]{0,1:T(8,128)S(1)}, f32[256,36]{0,1:T(8,128)S(1)}, u32[]{:S(2)}, u32[]{:S(2)}) collective-permute-start(f32[256,36]{0,1:T(8,128)S(1)} %slice.11), channel_id=1, source_target_pairs={{0,128},{8,136},{16,144},{24,152},{32,160},{40,168},{48,176},{56,1... | collective-permute-start | bytes 110600
  460.5 1.9 collective-permute-start
  462.4 1.9 collective-permute-start.1
  464.3 9.6 %collective-permute-start.10 = (f32[256,48]{0,1:T(8,128)S(1)}, f32[256,48]{0,1:T(8,128)S(1)}, u32[]{:S(2)}, u32[]{:S(2)}) collective-permute-start(f32[256,48]{0,1:T(8,128)S(1)} %get-tuple-element.8), channel_id=1, source_target_pairs={{0,88},{8,96},{16,104},{24,112},{32,120},{40,128},{48,136},{56,144... | collective-permute-start | bytes 147464
  473.9 1.9 collective-permute-start.11
  475.9 1.6 collective-permute-start.12
  477.5 3.7 collective-permute-start.13
  481.3 1.6 collective-permute-start.14
  484.2 2.7 collective-permute-start.3
  487.0 4.3 collective-permute-start.4
  491.4 2.8 collective-permute-start.5
  494.2 1.6 collective-permute-start.6
  495.8 1.9 collective-permute-start.7
  497.7 1.7 collective-permute-start.8
  499.4 2.8 collective-permute-start.9
  502.2 2.9 collective-permute-start.16
  505.2 3.4 collective-permute-start.17
  508.6 2.4 collective-permute-start.18
  511.0 3.6 collective-permute-start.19
  514.7 3.0 collective-permute-start.20
  517.7 2.4 collective-permute-start.21
  520.1 2.3 collective-permute-start.22
  523.7 1.3 collective-permute-start.24
  525.0 2.0 collective-permute-start.25
  527.1 1.9 collective-permute-start.26
  529.0 2.9 collective-permute-start.27
  531.8 1.9 collective-permute-start.28
  533.7 1.9 collective-permute-start.29
  535.6 1.9 collective-permute-start.30
  539.6 7.9 %concatenate = f32[256,804]{0,1:T(8,128)S(1)} concatenate(f32[256,36]{0,1:T(8,128)} %copy-done.22, f32[256,48]{0,1:T(8,128)S(1)} %collective-permute-done.14, f32[256,48]{0,1:T(8,128)S(1)} %collective-permute-done.13, f32[256,48]{0,1:T(8,128)S(1)} %collective-permute-done.12, f32[256,48]{0,1:T(8,128)S(1)} %collective-permute-done.11, f32[256,48]{0,1:T(8,128)S(1)} %collective-permute-done.10, ...), dimensions={1} | concatenate | bytes 1646592
  547.6 24.2 %concatenate.1 = f32[256,804]{0,1:T(8,128)} concatenate(f32[256,36]{0,1:T(8,128)} %copy-done.21, f32[256,48]{0,1:T(8,128)} %collective-permute-done.30, f32[256,48]{0,1:T(8,128)} %collective-permute-done.29, f32[256,48]{0,1:T(8,128)} %collective-permute-done.28, f32[256,48]{0,1:T(8,128)} %collective-permute-done.27, f32[256,48]{0,1:T(8,128)} %collective-permute-done.26, ...), dimensions={1} | concatenate | bytes 1646592
  571.8 1.4 fusion.16
  573.3 74.4 %all-gather.7.cloned.1.call-done = bf16[64,36,256]{2,1,0:T(8,128)(2,1)} async-done(((bf16[1,36,256]{2,1,0:T(8,128)(2,1)}), bf16[64,36,256]{2,1,0:T(8,128)(2,1)}) %all-gather.7.cloned.1.call-update) | async-done | bytes 1179664 | tf_op jit(solution)/shard_map/all_gather | solution.py:98
  647.8 2.1 reshape.167
  649.9 2.2 convolution_convert_fusion
  652.1 36.9 %reduce-scatter.6.cloned.1.call-done = bf16[32,112]{1,0:T(8,128)(2,1)} async-done(((bf16[256,112]{1,0:T(8,128)(2,1)}), bf16[32,112]{1,0:T(8,128)(2,1)}) %reduce-scatter.6.cloned.1.call-update) | async-done | bytes 7184 | tf_op jit(solution)/shard_map/reduce_scatter | solution.py:102
  689.0 1.3 add_convert_fusion
  (117 shorter events, 10.6 us)
Async XLA Ops:
  6.5 93.5 %all-gather.5.cloned.1.call-start = ((), (), s32[]{:S(2)}) async-start(), calls=%async_computation.3 | async-start | bytes 1064960 | tf_op jit(solution)/shard_map/all_gather | solution.py:73
  13.6 166.0 %all-reduce.7.cloned.1.call-start = ((), (), s32[]{:S(2)}) async-start(), calls=%async_computation.1 | async-start | bytes 262144 | tf_op jit(solution)/shard_map/psum | solution.py:83
  14.0 90.4 %copy-start.3 = (bf16[256,112]{0,1:T(8,128)(2,1)S(1)}, bf16[256,112]{0,1:T(8,128)(2,1)}, u32[]{:S(2)}) copy-start(bf16[256,112]{0,1:T(8,128)(2,1)} %param.19) | copy-start | bytes 172036
  14.0 90.5 %copy-start.24 = (bf16[112]{0:T(256)(128)(2,1)S(1)}, bf16[112]{0:T(256)(128)(2,1)}, u32[]{:S(2)}) copy-start(bf16[112]{0:T(256)(128)(2,1)} %param.20) | copy-start | bytes 676
  102.8 197.5 %copy-start.1 = (bf16[112,2304]{1,0:T(8,128)(2,1)S(1)}, bf16[112,2304]{1,0:T(8,128)(2,1)}, u32[]{:S(2)}) copy-start(bf16[112,2304]{1,0:T(8,128)(2,1)} %param.21) | copy-start | bytes 1548292
  102.8 199.5 %copy-start.2 = (bf16[112,2304]{1,0:T(8,128)(2,1)S(1)}, bf16[112,2304]{1,0:T(8,128)(2,1)}, u32[]{:S(2)}) copy-start(bf16[112,2304]{1,0:T(8,128)(2,1)} %param.22) | copy-start | bytes 1548292
  104.3 543.4 %all-gather.7.cloned.1.call-start = ((), (), s32[]{:S(2)}) async-start(), calls=%async_computation.4 | async-start | bytes 1331200 | tf_op jit(solution)/shard_map/all_gather | solution.py:98
  450.9 23.0 %collective-permute-start.15 = (f32[256,36]{0,1:T(8,128)S(1)}, f32[256,36]{0,1:T(8,128)S(1)}, u32[]{:S(2)}, u32[]{:S(2)}) collective-permute-start(f32[256,36]{0,1:T(8,128)S(1)} %slice.10), channel_id=1, source_target_pairs={{0,128},{8,136},{16,144},{24,152},{32,160},{40,168},{48,176},{56,1... | collective-permute-start | bytes 110600
  452.2 23.6 %collective-permute-start.31 = (f32[256,36]{0,1:T(8,128)S(1)}, f32[256,36]{0,1:T(8,128)S(1)}, u32[]{:S(2)}, u32[]{:S(2)}) collective-permute-start(f32[256,36]{0,1:T(8,128)S(1)} %slice.11), channel_id=1, source_target_pairs={{0,128},{8,136},{16,144},{24,152},{32,160},{40,168},{48,176},{56,1... | collective-permute-start | bytes 110600
  460.5 17.1 %collective-permute-start = (f32[256,48]{0,1:T(8,128)S(1)}, f32[256,48]{0,1:T(8,128)S(1)}, u32[]{:S(2)}, u32[]{:S(2)}) collective-permute-start(f32[256,48]{0,1:T(8,128)S(1)} %get-tuple-element.8), channel_id=1, source_target_pairs={{0,8},{8,16},{16,24},{24,32},{32,40},{40,48},{48,56},{56,64},{64,7... | collective-permute-start | bytes 147464
  462.4 18.8 %collective-permute-start.1 = (f32[256,48]{0,1:T(8,128)S(1)}, f32[256,48]{0,1:T(8,128)S(1)}, u32[]{:S(2)}, u32[]{:S(2)}) collective-permute-start(f32[256,48]{0,1:T(8,128)S(1)} %get-tuple-element.8), channel_id=1, source_target_pairs={{0,16},{8,24},{16,32},{24,40},{32,48},{40,56},{48,64},{56,72},{64,... | collective-permute-start | bytes 147464
  464.3 18.6 %collective-permute-start.10 = (f32[256,48]{0,1:T(8,128)S(1)}, f32[256,48]{0,1:T(8,128)S(1)}, u32[]{:S(2)}, u32[]{:S(2)}) collective-permute-start(f32[256,48]{0,1:T(8,128)S(1)} %get-tuple-element.8), channel_id=1, source_target_pairs={{0,88},{8,96},{16,104},{24,112},{32,120},{40,128},{48,136},{56,144... | collective-permute-start | bytes 147464
  473.9 63.8 %copy-start.22 = (f32[256,36]{0,1:T(8,128)}, f32[256,36]{0,1:T(8,128)S(1)}, u32[]{:S(2)}) copy-start(f32[256,36]{0,1:T(8,128)S(1)} %collective-permute-done.15) | copy-start | bytes 110596
  473.9 10.3 %collective-permute-start.11 = (f32[256,48]{0,1:T(8,128)S(1)}, f32[256,48]{0,1:T(8,128)S(1)}, u32[]{:S(2)}, u32[]{:S(2)}) collective-permute-start(f32[256,48]{0,1:T(8,128)S(1)} %get-tuple-element.8), channel_id=1, source_target_pairs={{0,96},{8,104},{16,112},{24,120},{32,128},{40,136},{48,144},{56,15... | collective-permute-start | bytes 147464
  475.9 11.1 %collective-permute-start.12 = (f32[256,48]{0,1:T(8,128)S(1)}, f32[256,48]{0,1:T(8,128)S(1)}, u32[]{:S(2)}, u32[]{:S(2)}) collective-permute-start(f32[256,48]{0,1:T(8,128)S(1)} %get-tuple-element.8), channel_id=1, source_target_pairs={{0,104},{8,112},{16,120},{24,128},{32,136},{40,144},{48,152},{56,1... | collective-permute-start | bytes 147464
  477.5 13.8 %collective-permute-start.13 = (f32[256,48]{0,1:T(8,128)S(1)}, f32[256,48]{0,1:T(8,128)S(1)}, u32[]{:S(2)}, u32[]{:S(2)}) collective-permute-start(f32[256,48]{0,1:T(8,128)S(1)} %get-tuple-element.8), channel_id=1, source_target_pairs={{0,112},{8,120},{16,128},{24,136},{32,144},{40,152},{48,160},{56,1... | collective-permute-start | bytes 147464
  481.3 13.0 %collective-permute-start.14 = (f32[256,48]{0,1:T(8,128)S(1)}, f32[256,48]{0,1:T(8,128)S(1)}, u32[]{:S(2)}, u32[]{:S(2)}) collective-permute-start(f32[256,48]{0,1:T(8,128)S(1)} %get-tuple-element.8), channel_id=1, source_target_pairs={{0,120},{8,128},{16,136},{24,144},{32,152},{40,160},{48,168},{56,1... | collective-permute-start | bytes 147464
  482.9 12.9 %collective-permute-start.2 = (f32[256,48]{0,1:T(8,128)S(1)}, f32[256,48]{0,1:T(8,128)S(1)}, u32[]{:S(2)}, u32[]{:S(2)}) collective-permute-start(f32[256,48]{0,1:T(8,128)S(1)} %get-tuple-element.8), channel_id=1, source_target_pairs={{0,24},{8,32},{16,40},{24,48},{32,56},{40,64},{48,72},{56,80},{64,... | collective-permute-start | bytes 147464
  484.2 13.5 %collective-permute-start.3 = (f32[256,48]{0,1:T(8,128)S(1)}, f32[256,48]{0,1:T(8,128)S(1)}, u32[]{:S(2)}, u32[]{:S(2)}) collective-permute-start(f32[256,48]{0,1:T(8,128)S(1)} %get-tuple-element.8), channel_id=1, source_target_pairs={{0,32},{8,40},{16,48},{24,56},{32,64},{40,72},{48,80},{56,88},{64,... | collective-permute-start | bytes 147464
  487.0 12.4 %collective-permute-start.4 = (f32[256,48]{0,1:T(8,128)S(1)}, f32[256,48]{0,1:T(8,128)S(1)}, u32[]{:S(2)}, u32[]{:S(2)}) collective-permute-start(f32[256,48]{0,1:T(8,128)S(1)} %get-tuple-element.8), channel_id=1, source_target_pairs={{0,40},{8,48},{16,56},{24,64},{32,72},{40,80},{48,88},{56,96},{64,... | collective-permute-start | bytes 147464
  491.4 10.8 %collective-permute-start.5 = (f32[256,48]{0,1:T(8,128)S(1)}, f32[256,48]{0,1:T(8,128)S(1)}, u32[]{:S(2)}, u32[]{:S(2)}) collective-permute-start(f32[256,48]{0,1:T(8,128)S(1)} %get-tuple-element.8), channel_id=1, source_target_pairs={{0,48},{8,56},{16,64},{24,72},{32,80},{40,88},{48,96},{56,104},{64... | collective-permute-start | bytes 147464
  494.2 10.9 %collective-permute-start.6 = (f32[256,48]{0,1:T(8,128)S(1)}, f32[256,48]{0,1:T(8,128)S(1)}, u32[]{:S(2)}, u32[]{:S(2)}) collective-permute-start(f32[256,48]{0,1:T(8,128)S(1)} %get-tuple-element.8), channel_id=1, source_target_pairs={{0,56},{8,64},{16,72},{24,80},{32,88},{40,96},{48,104},{56,112},{6... | collective-permute-start | bytes 147464
  495.8 12.8 %collective-permute-start.7 = (f32[256,48]{0,1:T(8,128)S(1)}, f32[256,48]{0,1:T(8,128)S(1)}, u32[]{:S(2)}, u32[]{:S(2)}) collective-permute-start(f32[256,48]{0,1:T(8,128)S(1)} %get-tuple-element.8), channel_id=1, source_target_pairs={{0,64},{8,72},{16,80},{24,88},{32,96},{40,104},{48,112},{56,120},{... | collective-permute-start | bytes 147464
  497.7 37.9 %copy-start.4 = (f32[256,48]{0,1:T(8,128)}, f32[256,48]{0,1:T(8,128)S(1)}, u32[]{:S(2)}) copy-start(f32[256,48]{0,1:T(8,128)S(1)} %collective-permute-done.3) | copy-start | bytes 147460
  497.7 13.3 %collective-permute-start.8 = (f32[256,48]{0,1:T(8,128)S(1)}, f32[256,48]{0,1:T(8,128)S(1)}, u32[]{:S(2)}, u32[]{:S(2)}) collective-permute-start(f32[256,48]{0,1:T(8,128)S(1)} %get-tuple-element.8), channel_id=1, source_target_pairs={{0,72},{8,80},{16,88},{24,96},{32,104},{40,112},{48,120},{56,128},... | collective-permute-start | bytes 147464
  499.4 38.1 %copy-start.5 = (f32[256,48]{0,1:T(8,128)}, f32[256,48]{0,1:T(8,128)S(1)}, u32[]{:S(2)}) copy-start(f32[256,48]{0,1:T(8,128)S(1)} %collective-permute-done.4) | copy-start | bytes 147460
  499.4 15.3 %collective-permute-start.9 = (f32[256,48]{0,1:T(8,128)S(1)}, f32[256,48]{0,1:T(8,128)S(1)}, u32[]{:S(2)}, u32[]{:S(2)}) collective-permute-start(f32[256,48]{0,1:T(8,128)S(1)} %get-tuple-element.8), channel_id=1, source_target_pairs={{0,80},{8,88},{16,96},{24,104},{32,112},{40,120},{48,128},{56,136}... | collective-permute-start | bytes 147464
  502.2 35.3 %copy-start.6 = (f32[256,48]{0,1:T(8,128)}, f32[256,48]{0,1:T(8,128)S(1)}, u32[]{:S(2)}) copy-start(f32[256,48]{0,1:T(8,128)S(1)} %collective-permute-done.5) | copy-start | bytes 147460
  502.2 15.5 %collective-permute-start.16 = (f32[256,48]{0,1:T(8,128)S(1)}, f32[256,48]{0,1:T(8,128)S(1)}, u32[]{:S(2)}, u32[]{:S(2)}) collective-permute-start(f32[256,48]{0,1:T(8,128)S(1)} %get-tuple-element.7), channel_id=1, source_target_pairs={{0,8},{8,16},{16,24},{24,32},{32,40},{40,48},{48,56},{56,64},{64,7... | collective-permute-start | bytes 147464
  505.2 32.4 %copy-start.7 = (f32[256,48]{0,1:T(8,128)}, f32[256,48]{0,1:T(8,128)S(1)}, u32[]{:S(2)}) copy-start(f32[256,48]{0,1:T(8,128)S(1)} %collective-permute-done.6) | copy-start | bytes 147460
  505.2 14.9 %collective-permute-start.17 = (f32[256,48]{0,1:T(8,128)S(1)}, f32[256,48]{0,1:T(8,128)S(1)}, u32[]{:S(2)}, u32[]{:S(2)}) collective-permute-start(f32[256,48]{0,1:T(8,128)S(1)} %get-tuple-element.7), channel_id=1, source_target_pairs={{0,16},{8,24},{16,32},{24,40},{32,48},{40,56},{48,64},{56,72},{64,... | collective-permute-start | bytes 147464
  508.6 28.9 %copy-start.8 = (f32[256,48]{0,1:T(8,128)}, f32[256,48]{0,1:T(8,128)S(1)}, u32[]{:S(2)}) copy-start(f32[256,48]{0,1:T(8,128)S(1)} %collective-permute-done.7) | copy-start | bytes 147460
  508.6 13.7 %collective-permute-start.18 = (f32[256,48]{0,1:T(8,128)S(1)}, f32[256,48]{0,1:T(8,128)S(1)}, u32[]{:S(2)}, u32[]{:S(2)}) collective-permute-start(f32[256,48]{0,1:T(8,128)S(1)} %get-tuple-element.7), channel_id=1, source_target_pairs={{0,24},{8,32},{16,40},{24,48},{32,56},{40,64},{48,72},{56,80},{64,... | collective-permute-start | bytes 147464
  511.0 26.5 %copy-start.10 = (f32[256,48]{0,1:T(8,128)}, f32[256,48]{0,1:T(8,128)S(1)}, u32[]{:S(2)}) copy-start(f32[256,48]{0,1:T(8,128)S(1)} %collective-permute-done.8) | copy-start | bytes 147460
  511.0 12.7 %collective-permute-start.19 = (f32[256,48]{0,1:T(8,128)S(1)}, f32[256,48]{0,1:T(8,128)S(1)}, u32[]{:S(2)}, u32[]{:S(2)}) collective-permute-start(f32[256,48]{0,1:T(8,128)S(1)} %get-tuple-element.7), channel_id=1, source_target_pairs={{0,32},{8,40},{16,48},{24,56},{32,64},{40,72},{48,80},{56,88},{64,... | collective-permute-start | bytes 147464
  514.7 22.9 %copy-start.12 = (f32[256,48]{0,1:T(8,128)}, f32[256,48]{0,1:T(8,128)S(1)}, u32[]{:S(2)}) copy-start(f32[256,48]{0,1:T(8,128)S(1)} %collective-permute-done.9) | copy-start | bytes 147460
  514.7 10.3 %collective-permute-start.20 = (f32[256,48]{0,1:T(8,128)S(1)}, f32[256,48]{0,1:T(8,128)S(1)}, u32[]{:S(2)}, u32[]{:S(2)}) collective-permute-start(f32[256,48]{0,1:T(8,128)S(1)} %get-tuple-element.7), channel_id=1, source_target_pairs={{0,40},{8,48},{16,56},{24,64},{32,72},{40,80},{48,88},{56,96},{64,... | collective-permute-start | bytes 147464
  517.7 9.3 %collective-permute-start.21 = (f32[256,48]{0,1:T(8,128)S(1)}, f32[256,48]{0,1:T(8,128)S(1)}, u32[]{:S(2)}, u32[]{:S(2)}) collective-permute-start(f32[256,48]{0,1:T(8,128)S(1)} %get-tuple-element.7), channel_id=1, source_target_pairs={{0,48},{8,56},{16,64},{24,72},{32,80},{40,88},{48,96},{56,104},{64... | collective-permute-start | bytes 147464
  520.1 8.9 %collective-permute-start.22 = (f32[256,48]{0,1:T(8,128)S(1)}, f32[256,48]{0,1:T(8,128)S(1)}, u32[]{:S(2)}, u32[]{:S(2)}) collective-permute-start(f32[256,48]{0,1:T(8,128)S(1)} %get-tuple-element.7), channel_id=1, source_target_pairs={{0,56},{8,64},{16,72},{24,80},{32,88},{40,96},{48,104},{56,112},{6... | collective-permute-start | bytes 147464
  522.4 9.5 %collective-permute-start.23 = (f32[256,48]{0,1:T(8,128)S(1)}, f32[256,48]{0,1:T(8,128)S(1)}, u32[]{:S(2)}, u32[]{:S(2)}) collective-permute-start(f32[256,48]{0,1:T(8,128)S(1)} %get-tuple-element.7), channel_id=1, source_target_pairs={{0,64},{8,72},{16,80},{24,88},{32,96},{40,104},{48,112},{56,120},{... | collective-permute-start | bytes 147464
  523.7 10.0 %collective-permute-start.24 = (f32[256,48]{0,1:T(8,128)S(1)}, f32[256,48]{0,1:T(8,128)S(1)}, u32[]{:S(2)}, u32[]{:S(2)}) collective-permute-start(f32[256,48]{0,1:T(8,128)S(1)} %get-tuple-element.7), channel_id=1, source_target_pairs={{0,72},{8,80},{16,88},{24,96},{32,104},{40,112},{48,120},{56,128},... | collective-permute-start | bytes 147464
  525.0 10.6 %collective-permute-start.25 = (f32[256,48]{0,1:T(8,128)S(1)}, f32[256,48]{0,1:T(8,128)S(1)}, u32[]{:S(2)}, u32[]{:S(2)}) collective-permute-start(f32[256,48]{0,1:T(8,128)S(1)} %get-tuple-element.7), channel_id=1, source_target_pairs={{0,80},{8,88},{16,96},{24,104},{32,112},{40,120},{48,128},{56,136}... | collective-permute-start | bytes 147464
  527.1 20.5 %collective-permute-start.26 = (f32[256,48]{0,1:T(8,128)S(1)}, f32[256,48]{0,1:T(8,128)}, u32[]{:S(2)}, u32[]{:S(2)}) collective-permute-start(f32[256,48]{0,1:T(8,128)S(1)} %get-tuple-element.7), channel_id=1, source_target_pairs={{0,88},{8,96},{16,104},{24,112},{32,120},{40,128},{48,136},{56,144... | collective-permute-start | bytes 147464
  529.0 18.6 %collective-permute-start.27 = (f32[256,48]{0,1:T(8,128)S(1)}, f32[256,48]{0,1:T(8,128)}, u32[]{:S(2)}, u32[]{:S(2)}) collective-permute-start(f32[256,48]{0,1:T(8,128)S(1)} %get-tuple-element.7), channel_id=1, source_target_pairs={{0,96},{8,104},{16,112},{24,120},{32,128},{40,136},{48,144},{56,15... | collective-permute-start | bytes 147464
  531.8 15.8 %collective-permute-start.28 = (f32[256,48]{0,1:T(8,128)S(1)}, f32[256,48]{0,1:T(8,128)}, u32[]{:S(2)}, u32[]{:S(2)}) collective-permute-start(f32[256,48]{0,1:T(8,128)S(1)} %get-tuple-element.7), channel_id=1, source_target_pairs={{0,104},{8,112},{16,120},{24,128},{32,136},{40,144},{48,152},{56,1... | collective-permute-start | bytes 147464
  533.7 13.9 %collective-permute-start.29 = (f32[256,48]{0,1:T(8,128)S(1)}, f32[256,48]{0,1:T(8,128)}, u32[]{:S(2)}, u32[]{:S(2)}) collective-permute-start(f32[256,48]{0,1:T(8,128)S(1)} %get-tuple-element.7), channel_id=1, source_target_pairs={{0,112},{8,120},{16,128},{24,136},{32,144},{40,152},{48,160},{56,1... | collective-permute-start | bytes 147464
  535.6 12.0 %collective-permute-start.30 = (f32[256,48]{0,1:T(8,128)S(1)}, f32[256,48]{0,1:T(8,128)}, u32[]{:S(2)}, u32[]{:S(2)}) collective-permute-start(f32[256,48]{0,1:T(8,128)S(1)} %get-tuple-element.7), channel_id=1, source_target_pairs={{0,120},{8,128},{16,136},{24,144},{32,152},{40,160},{48,168},{56,1... | collective-permute-start | bytes 147464
  573.3 115.8 %reduce-scatter.6.cloned.1.call-start = ((), (), s32[]{:S(2)}) async-start(), calls=%async_computation.2 | async-start | bytes 73728 | tf_op jit(solution)/shard_map/reduce_scatter | solution.py:102
  (13 other events, 131.5 us)
Sparse Core Ops, SparseCore 0:
  13.7 86.2 all-gather.4
  104.5 75.0 all-reduce.6
  573.4 74.3 all-gather.6
  652.2 36.7 reduce-scatter.5
where the time goes:
time: 700 us; the launch traced here: 697 us
  waiting for transfers between devices  273 us (39%)
  blocking collectives  266 us (38%)
  starting transfers between devices  86.1 us (12%)
  local copies, waits for them, and re-layouts  38.1 us (5%)
  between operations  15.5 us (2%)
  matrix products  13.5 us (2%)
    unnamed x1, blocking collectives  147 us
    psum x1, blocking collectives, local(): square_sums = lax.psum(jnp.sum(hidden * hidden, axis=1), 'dp')  120 us
    all_gather x1, waiting for transfers between devices, local(): lax.all_gather(head_values, 'dp', axis=0, tiled=True)  86 us
    unnamed x32, starting transfers between devices  86 us
    psum x1, waiting for transfers between devices, local(): attended = lax.psum(projected, 'tp')  75 us
    all_gather x1, waiting for transfers between devices, local(): lax.all_gather(hidden_units, 'dp', axis=1, tiled=True)  74.4 us
    unnamed x58, local copies, waits for them, and re-layouts  37.1 us
    reduce_scatter x1, waiting for transfers between devices, local(): lax.psum_scatter(down_term.astype(jnp.bfloat16), 'tp', scatter_dimension=...  36.9 us
  transfers between devices with their start and end apart: 36, of which 4 were waited for; matrix products, arithmetic and copies ran while one was open for 1% of the time, Pallas kernels for 0%

commit v1 on v0

v1 whole, which is shorter than its diff:
```python
import jax
import jax.numpy as jnp
from jax import lax
from jax.sharding import Mesh
from jax.sharding import PartitionSpec as P

D = 7168

score_scale = 192.0 ** (-0.5)
norm_eps = 1e-06

AXES = ("z", "xh", "xl", "c", "y")
DP = ("z", "xh", "xl", "c")
BF = jnp.bfloat16
F32 = jnp.float32


def attention(queries, new_latents, latent_cache, lengths, value_maps):
    step_count = queries.shape[1]
    cache_len = latent_cache.shape[1]
    latent_width = value_maps.shape[1]
    score_cache = (
        jnp.einsum("rshc,rlc->rshl", queries, latent_cache, preferred_element_type=F32)
        * score_scale
    )
    score_new = (
        jnp.einsum("rshc,ruc->rshu", queries, new_latents, preferred_element_type=F32)
        * score_scale
    )
    position = jnp.arange(cache_len, dtype=jnp.int32)
    keep_cache = (position[None, :] < lengths[:, None])[:, None, None, :]
    step_ids = jnp.arange(step_count, dtype=jnp.int32)
    keep_new = (step_ids[None, :] <= step_ids[:, None])[None, :, None, :]
    row_max = jnp.maximum(
        jnp.max(jnp.where(keep_cache, score_cache, -1e30), axis=3, keepdims=True),
        jnp.max(jnp.where(keep_new, score_new, -1e30), axis=3, keepdims=True),
    )
    weight_cache = jnp.where(keep_cache, jnp.exp(score_cache - row_max), 0.0)
    weight_new = jnp.where(keep_new, jnp.exp(score_new - row_max), 0.0)
    softmax_total = jnp.sum(weight_cache, axis=3, keepdims=True) + jnp.sum(
        weight_new, axis=3, keepdims=True
    )
    prob_cache = (weight_cache / softmax_total).astype(BF)
    prob_new = (weight_new / softmax_total).astype(BF)
    context = jnp.einsum(
        "rshl,rlc->rshc",
        prob_cache,
        latent_cache[:, :, :latent_width],
        preferred_element_type=F32,
    )
    context = context + jnp.einsum(
        "rshu,ruc->rshc",
        prob_new,
        new_latents[:, :, :latent_width],
        preferred_element_type=F32,
    )
    context = context.astype(BF)
    head_values = jnp.einsum(
        "rshc,hcd->rshd", context, value_maps, preferred_element_type=F32
    ).astype(BF)
    return head_values.reshape(step_count, -1)


def swap(value, axis):
    return lax.ppermute(value, axis, [(0, 1), (1, 0)])


def exchange(blocks, axes):
    return lax.all_to_all(blocks, axes, 0, 0, tiled=True)


def gather(block, axes, count):
    return exchange(jnp.broadcast_to(block[None], (count,) + block.shape), axes)


def dot(a, b):
    return jnp.dot(a, b, preferred_element_type=F32)


def halves(weight, axis, index):
    size = weight.shape[axis] // 2
    keep = lax.dynamic_slice_in_dim(weight, index * size, size, axis)
    send = lax.dynamic_slice_in_dim(weight, (1 - index) * size, size, axis)
    return keep, send


def local(
    queries,
    new_latents,
    latent_cache,
    lengths,
    slot_of,
    value_maps,
    out_proj,
    residual,
    norm_gain,
    w_gate,
    w_up,
    w_down,
):
    xl, core, tp = lax.axis_index("xl"), lax.axis_index("c"), lax.axis_index("y")
    width = out_proj.shape[1]
    row_ids = jnp.arange(128, dtype=jnp.int32)
    out_ids = jnp.arange(256, dtype=jnp.int32)
    slot_rows = jnp.repeat(slot_of, 4) * 4 + out_ids % 4

    def placed(of_core):
        own = (row_ids // 4) * 8 + of_core * 4 + row_ids % 4
        return (slot_rows[:, None] == own[None, :]).astype(BF)

    mine, others = placed(core), placed(1 - core)
    block = lambda m: lax.dynamic_slice_in_dim(m, tp * 16, 16, 1)
    pick = lambda m: lax.dot_general(
        block(m), residual, (((0,), (0,)), ((), ())), preferred_element_type=F32
    ).astype(BF)
    head = pick(mine)
    other = swap(
        jnp.concatenate([pick(others), jnp.broadcast_to(norm_gain[None], (16, width))], axis=0), "c"
    )
    out_other = swap(out_proj, "c")

    head_values = attention(queries, new_latents, latent_cache, lengths, value_maps)

    gate_keep, gate_send = halves(w_gate, 1, xl)
    up_keep, up_send = halves(w_up, 1, xl)
    ff_own = jnp.concatenate([gate_keep, up_keep], axis=1)
    ff_next = swap(jnp.concatenate([gate_send, up_send], axis=1), "xl")
    ff_own_other = swap(ff_own, "c")
    ff_next_other = swap(ff_next, "c")
    down_own, down_send = halves(w_down, 0, xl)
    down_next = swap(down_send, "xl")
    down_own_other = swap(down_own, "c")
    down_next_other = swap(down_next, "c")

    rows = gather(head_values, ("z", "xh", "xl"), 32).reshape(128, -1)
    part = jnp.stack([dot(rows, out_proj), dot(rows, out_other)]).astype(BF)
    part = part.reshape(2, 8, 16, width).transpose(1, 0, 2, 3)
    attended = jnp.sum(exchange(part, "y").astype(F32), axis=0)
    start = jnp.stack([head, other[:16]]).astype(F32)
    gain = jnp.stack([norm_gain[None], other[16:17]]).astype(F32)
    hidden = start + attended
    squares = jnp.sum(hidden * hidden, axis=(0, 2))
    high = squares.astype(BF)
    low = (squares - high.astype(F32)).astype(BF)
    extra = jnp.stack([high, low], axis=1)
    extra = jnp.pad(extra[None], ((0, 1), (0, 0), (0, 128 - width - 2)))
    scaled = jnp.concatenate([(hidden * gain).astype(BF), extra], axis=2)

    full = gather(scaled, ("xl", "y"), 16).reshape(2, 8, 2, 16, 128)
    near = lax.dynamic_index_in_dim(full, xl, 0, False)
    far = lax.dynamic_index_in_dim(full, 1 - xl, 0, False)
    rows_of = lambda a, o: a[:, o, :, :width].reshape(128, width)
    ff = (
        dot(rows_of(near, 0), ff_own)
        + dot(rows_of(near, 1), ff_own_other)
        + dot(rows_of(far, 0), ff_next)
        + dot(rows_of(far, 1), ff_next_other)
    )
    sums = jnp.sum(full[:, :, 0, :, width : width + 2].astype(F32), axis=(0, 3)).reshape(128, 1)
    high = sums.astype(BF)
    low = (sums - high.astype(F32)).astype(BF)
    ff = jnp.concatenate([ff.astype(BF), high, low, jnp.zeros((128, 126), BF)], axis=1)
    total = jnp.sum(exchange(ff.reshape(16, 8, -1), ("z", "xh")).astype(F32), axis=0)
    half = w_gate.shape[1] // 2
    square_sums = total[:, 2 * half : 2 * half + 1] + total[:, 2 * half + 1 : 2 * half + 2]
    factor = lax.rsqrt(square_sums / D + norm_eps)
    units = (jax.nn.silu(total[:, :half] * factor) * (total[:, half : 2 * half] * factor)).astype(BF)

    units = gather(units, ("z", "xh"), 16).reshape(128, half)
    hidden_rows = lax.dynamic_update_slice_in_dim(
        jnp.zeros((2, 128, width), F32), hidden, tp * 16, 1
    )
    own = jnp.stack([dot(units, down_own), dot(units, down_own_other)]) + hidden_rows
    nxt = jnp.stack([dot(units, down_next), dot(units, down_next_other)])
    both = jnp.where(xl == 0, jnp.stack([own, nxt]), jnp.stack([nxt, own])).astype(BF)
    both = jnp.einsum("qr,xork->xoqk", mine, both, preferred_element_type=F32).astype(BF)
    both = both.reshape(2, 2, 8, 32, width).transpose(0, 2, 1, 3, 4).reshape(16, 2, 32, width)
    share = jnp.sum(exchange(both, ("xl", "y")).astype(F32), axis=0)
    return (share[0] + swap(share[1], "c")).astype(BF)


def solution(mesh):
    fine = Mesh(mesh.devices.reshape(8, 2, 2, 2, 8), AXES)
    placed = (
        P(DP, None, "y", None),
        P(DP, None, None),
        P(DP, None, None),
        P(DP),
        P(),
        P("y", None, None),
        P("y", DP),
        P(None, DP),
        P(DP),
        P(DP, "y"),
        P(DP, "y"),
        P("y", DP),
    )
    return jax.shard_map(
        local, mesh=fine, in_specs=placed, out_specs=P("y", DP), check_vma=False
    )
```

time: 700 us -> 143 us (0.20)
  the two profiles are of different devices: /device:TPU:2 before, /device:TPU:15 now
where the time goes in v1:
time: 143 us; the launch traced here: 142 us
  starting transfers between devices  65.8 us (46%)
  blocking collectives  38.4 us (27%)
  matrix products  12.9 us (9%)
  waiting for transfers between devices  12.1 us (8%)
  local copies, waits for them, and re-layouts  8.52 us (6%)
  other arithmetic  2.68 us (2%)
    all_to_all x2, blocking collectives, exchange(): return lax.all_to_all(blocks, axes, 0, 0, tiled=True)  38.4 us
    ppermute x9, starting transfers between devices, swap(): return lax.ppermute(value, axis, [(0, 1), (1, 0)])  34.3 us
    all_to_all x4, starting transfers between devices, exchange(): return lax.all_to_all(blocks, axes, 0, 0, tiled=True)  31.5 us
    all_to_all x4, waiting for transfers between devices, exchange(): return lax.all_to_all(blocks, axes, 0, 0, tiled=True)  11.2 us
    dot_general x10, matrix products, dot(): return jnp.dot(a, b, preferred_element_type=F32)  7.93 us
  transfers between devices with their start and end apart: 13, of which 3 were waited for; matrix products, arithmetic and copies ran while one was open for 10% of the time, Pallas kernels for 0%

profile of v1, /device:TPU:15, one launch (start us, length us, event | category | flops | bytes accessed | tf_op | source)
XLA Modules:
  0.0 141.8 jit_solution(11063272905955492186)
XLA Ops:
  0.8 1.4 %select_reduce_fusion = (f32[4,16]{1,0:T(4,128)S(1)}, f32[4,16,512]{2,1,0:T(8,128)S(1)}) fusion(pred[512]{0:T(512)(128)(4,1)S(1)} %iota_compare_fusion.2, bf16[1,512,576]{1,2,0:T(8,128)(2,1)} %param.14, bf16[1,4,16,576]{3,2,1,0:T(8,128)(2,1)} %param.12), kind=kOutput, calls=%fused_computation.45 | convolution fusion | flops 37846976 | bytes 795392 | tf_op jit(solution)/shard_map/rshc,rlc->rshl/dot_general | solution.py:23
  2.3 1.1 select_reduce_fusion.1
  3.7 1.0 fusion.43
  4.7 0.3 fusion.3
  5.0 0.4 fusion.6
  5.4 1.0 broadcast_in_dim.96
  6.4 12.9 %all-to-all-start = ((bf16[32,4,2048]{2,1,0:T(4,128)(2,1)}), bf16[32,4,2048]{2,1,0:T(4,128)(2,1)}, u32[]{:S(2)}, u32[]{:S(2)}) async-start(bf16[32,4,2048]{2,1,0:T(4,128)(2,1)} %broadcast_in_dim.96), calls=%async_computation | async-start | bytes 1048576 | tf_op jit(solution)/shard_map/all_to_all | solution.py:69
  19.3 3.1 %collective-permute-start.1 = (bf16[2048,112]{0,1:T(8,128)(2,1)}, bf16[2048,112]{0,1:T(8,128)(2,1)}, u32[]{:S(2)}, u32[]{:S(2)}) collective-permute-start(bf16[2048,112]{0,1:T(8,128)(2,1)} %param.18), channel_id=1, source_target_pairs={{0,8},{8,0},{1,9},{9,1},{2,10},{10,2},{3,11},{11,3},{4,12},{12,4},... | collective-permute-start | bytes 1376264 | tf_op jit(solution)/shard_map/ppermute | solution.py:65
  22.8 0.3 convolution_convert_fusion.4
  23.1 1.9 %collective-permute-start = (bf16[32,112]{1,0:T(8,128)(2,1)S(1)}, bf16[32,112]{1,0:T(8,128)(2,1)S(1)}, u32[]{:S(2)}, u32[]{:S(2)}) collective-permute-start(bf16[32,112]{1,0:T(8,128)(2,1)S(1)} %pad_maximum_fusion.3), channel_id=1, source_target_pairs={{0,8},{8,0},{1,9},{9,1},{2,10},{10,2},{3,11},{11,3},{4,12},{12,4},... | collective-permute-start | bytes 21512 | tf_op jit(solution)/shard_map/ppermute | solution.py:65
  25.0 1.2 constant_dynamic-slice_fusion.1
  26.2 0.8 pad_maximum_fusion.1
  27.0 2.5 %collective-permute-start.3 = (bf16[112,2304]{1,0:T(8,128)(2,1)}, bf16[112,2304]{1,0:T(8,128)(2,1)}, u32[]{:S(2)}, u32[]{:S(2)}) collective-permute-start(bf16[112,2304]{1,0:T(8,128)(2,1)} %pad_maximum_fusion.1), channel_id=1, source_target_pairs={{0,16},{16,0},{1,17},{17,1},{2,18},{18,2},{3,19},{19,3},{4,20},{20... | collective-permute-start | bytes 1548296 | tf_op jit(solution)/shard_map/ppermute | solution.py:65
  29.6 0.3 fusion.7
  30.0 5.2 %all-to-all-done = bf16[32,4,2048]{2,1,0:T(4,128)(2,1)} async-done(((bf16[32,4,2048]{2,1,0:T(4,128)(2,1)}), bf16[32,4,2048]{2,1,0:T(4,128)(2,1)}, u32[]{:S(2)}, u32[]{:S(2)}) %all-to-all-start) | async-done | bytes 524320 | tf_op jit(solution)/shard_map/all_to_all | solution.py:69
  35.2 1.2 reshape.279
  36.4 1.3 fusion.4
  37.7 1.3 fusion.5
  39.1 0.6 copy.117
  39.7 7.0 %all-to-all-start.1 = ((bf16[8,2,16,112]{3,2,1,0:T(8,128)(2,1)}), bf16[8,2,16,112]{3,2,1,0:T(8,128)(2,1)S(1)}, u32[]{:S(2)}, u32[]{:S(2)}) async-start(bf16[8,2,16,112]{3,2,1,0:T(8,128)(2,1)} %copy.117), calls=%async_computation.1 | async-start | bytes 131072 | tf_op jit(solution)/shard_map/all_to_all | solution.py:69
  46.7 6.0 %all-to-all-done.1 = bf16[8,2,16,112]{3,2,1,0:T(8,128)(2,1)S(1)} async-done(((bf16[8,2,16,112]{3,2,1,0:T(8,128)(2,1)}), bf16[8,2,16,112]{3,2,1,0:T(8,128)(2,1)S(1)}, u32[]{:S(2)}, u32[]{:S(2)}) %all-to-all-start.1) | async-done | bytes 57376 | tf_op jit(solution)/shard_map/all_to_all | solution.py:69
  53.2 0.7 broadcast_in_dim.98
  53.9 4.9 %all-to-all-start.2 = ((bf16[16,2,16,128]{3,2,1,0:T(8,128)(2,1)}), bf16[16,2,16,128]{3,2,1,0:T(8,128)(2,1)S(1)}, u32[]{:S(2)}, u32[]{:S(2)}) async-start(bf16[16,2,16,128]{3,2,1,0:T(8,128)(2,1)} %broadcast_in_dim.98), calls=%async_computation.2 | async-start | bytes 262144 | tf_op jit(solution)/shard_map/all_to_all | solution.py:69
  58.8 5.8 %collective-permute-start.2 = (bf16[112,2304]{1,0:T(8,128)(2,1)S(1)}, bf16[112,2304]{1,0:T(8,128)(2,1)}, u32[]{:S(2)}, u32[]{:S(2)}) collective-permute-start(bf16[112,2304]{1,0:T(8,128)(2,1)S(1)} %pad_maximum_fusion), channel_id=1, source_target_pairs={{0,8},{8,0},{1,9},{9,1},{2,10},{10,2},{3,11},{11,3},{4,12},{12,4},... | collective-permute-start | bytes 1548296 | tf_op jit(solution)/shard_map/ppermute | solution.py:65
  64.6 1.9 %collective-permute-start.4 = (bf16[112,2304]{1,0:T(8,128)(2,1)}, bf16[112,2304]{1,0:T(8,128)(2,1)}, u32[]{:S(2)}, u32[]{:S(2)}) collective-permute-start(bf16[112,2304]{1,0:T(8,128)(2,1)} %collective-permute-done.3), channel_id=1, source_target_pairs={{0,8},{8,0},{1,9},{9,1},{2,10},{10,2},{3,11},{11,3},{4,12},{12,4},... | collective-permute-start | bytes 1548296 | tf_op jit(solution)/shard_map/ppermute | solution.py:65
  67.1 0.7 copy.127
  67.9 0.3 fusion.61
  68.2 1.3 convolution_add_fusion.2
  69.6 1.3 convolution_add_fusion.1
  70.9 1.3 fusion.1
  72.3 0.3 concatenate.30
  72.6 19.7 %all_to_all.30 = bf16[16,8,2432]{2,1,0:T(8,128)(2,1)S(1)} all-to-all(bf16[16,8,2432]{2,1,0:T(8,128)(2,1)S(1)} %concatenate.30), channel_id=1, replica_groups=mesh['z'=8,'xh'=2,'xl'=2,'c'=2,'y'=8] {'z','xh'}, dimensions={0} | all-to-all | bytes 1245184 | tf_op jit(solution)/shard_map/all_to_all | solution.py:69
  92.4 0.2 fusion.47
  92.7 0.7 broadcast_in_dim.100
  93.4 6.7 %all-to-all-start.4 = ((bf16[16,8,1152]{2,1,0:T(8,128)(2,1)}), bf16[16,8,1152]{2,1,0:T(8,128)(2,1)S(1)}, u32[]{:S(2)}, u32[]{:S(2)}) async-start(bf16[16,8,1152]{2,1,0:T(8,128)(2,1)} %broadcast_in_dim.100), calls=%async_computation.4 | async-start | bytes 589824 | tf_op jit(solution)/shard_map/all_to_all | solution.py:69
  100.2 1.9 %collective-permute-start.6 = (bf16[1152,112]{0,1:T(8,128)(2,1)S(1)}, bf16[1152,112]{0,1:T(8,128)(2,1)S(1)}, u32[]{:S(2)}, u32[]{:S(2)}) collective-permute-start(bf16[1152,112]{0,1:T(8,128)(2,1)S(1)} %get-tuple-element.10), channel_id=1, source_target_pairs={{0,16},{16,0},{1,17},{17,1},{2,18},{18,2},{3,19},{19,3},{4,20},{20... | collective-permute-start | bytes 774152 | tf_op jit(solution)/shard_map/ppermute | solution.py:65
  102.2 7.0 %collective-permute-start.5 = (bf16[1152,112]{0,1:T(8,128)(2,1)S(1)}, bf16[1152,112]{0,1:T(8,128)(2,1)S(1)}, u32[]{:S(2)}, u32[]{:S(2)}) collective-permute-start(bf16[1152,112]{0,1:T(8,128)(2,1)S(1)} %get-tuple-element.9), channel_id=1, source_target_pairs={{0,8},{8,0},{1,9},{9,1},{2,10},{10,2},{3,11},{11,3},{4,12},{12,4},... | collective-permute-start | bytes 774152 | tf_op jit(solution)/shard_map/ppermute | solution.py:65
  109.2 6.7 %collective-permute-start.7 = (bf16[1152,112]{0,1:T(8,128)(2,1)S(1)}, bf16[1152,112]{0,1:T(8,128)(2,1)S(1)}, u32[]{:S(2)}, u32[]{:S(2)}) collective-permute-start(bf16[1152,112]{0,1:T(8,128)(2,1)S(1)} %collective-permute-done.6), channel_id=1, source_target_pairs={{0,8},{8,0},{1,9},{9,1},{2,10},{10,2},{3,11},{11,3},{4,12},{12,4},... | collective-permute-start | bytes 774152 | tf_op jit(solution)/shard_map/ppermute | solution.py:65
  115.9 0.2 convolution_bitcast_fusion.3
  116.2 0.2 convolution_bitcast_fusion.2
  116.5 0.6 add.165
  117.2 0.2 convolution_bitcast_fusion.1
  117.4 0.2 convolution_bitcast_fusion
  117.7 0.3 fusion.2
  118.2 18.6 %all_to_all.31 = bf16[16,2,32,112]{3,2,1,0:T(8,128)(2,1)S(1)} all-to-all(bf16[16,2,32,112]{3,2,1,0:T(8,128)(2,1)S(1)} %bitcast.135), channel_id=1, replica_groups=mesh['z'=8,'xh'=2,'xl'=2,'c'=2,'y'=8] {'xl','y'}, dimensions={0} | all-to-all | bytes 458752 | tf_op jit(solution)/shard_map/all_to_all | solution.py:69
  136.9 3.4 %collective-permute-start.8 = (f32[32,112]{1,0:T(8,128)S(1)}, f32[32,112]{1,0:T(8,128)S(1)}, u32[]{:S(2)}, u32[]{:S(2)}) collective-permute-start(f32[32,112]{1,0:T(8,128)S(1)} %slice_bitcast_fusion), channel_id=1, source_target_pairs={{0,8},{8,0},{1,9},{9,1},{2,10},{10,2},{3,11},{11,3},{4,12},{12,4},... | collective-permute-start | bytes 43016 | tf_op jit(solution)/shard_map/ppermute | solution.py:65
  140.3 0.8 collective-permute-done.8
  141.2 0.6 fusion.38
  (79 shorter events, 2.6 us)
Async XLA Ops:
  0.0 5.0 %copy-start = (bf16[16,512,128]{2,1,0:T(8,128)(2,1)S(1)}, bf16[16,512,128]{2,1,0:T(8,128)(2,1)}, u32[]{:S(2)}) copy-start(bf16[16,512,128]{2,1,0:T(8,128)(2,1)} %param.17) | copy-start | bytes 6291460
  0.0 4.7 %copy-start.1 = (bf16[1,512,576]{1,2,0:T(8,128)(2,1)S(1)}, bf16[1,512,576]{1,2,0:T(8,128)(2,1)}, u32[]{:S(2)}) copy-start(bf16[1,512,576]{1,2,0:T(8,128)(2,1)} %param.14) | copy-start | bytes 1769476
  5.4 17.1 %copy-start.7 = (s32[64]{0:T(128)S(1)}, s32[64]{0:T(128)}, u32[]{:S(2)}) copy-start(s32[64]{0:T(128)} %param.16) | copy-start | bytes 772
  5.4 17.4 %copy-start.5 = (bf16[256,112]{0,1:T(8,128)(2,1)S(1)}, bf16[256,112]{0,1:T(8,128)(2,1)}, u32[]{:S(2)}) copy-start(bf16[256,112]{0,1:T(8,128)(2,1)} %param.19) | copy-start | bytes 172036
  5.4 17.7 %copy-start.6 = (bf16[112]{0:T(256)(128)(2,1)S(1)}, bf16[112]{0:T(256)(128)(2,1)}, u32[]{:S(2)}) copy-start(bf16[112]{0:T(256)(128)(2,1)} %param.20) | copy-start | bytes 676
  5.4 19.6 %copy-start.2 = (bf16[112,2304]{1,0:T(8,128)(2,1)S(1)}, bf16[112,2304]{1,0:T(8,128)(2,1)}, u32[]{:S(2)}) copy-start(bf16[112,2304]{1,0:T(8,128)(2,1)} %param.22) | copy-start | bytes 1548292
  6.4 28.8 %all-to-all-start = ((bf16[32,4,2048]{2,1,0:T(4,128)(2,1)}), bf16[32,4,2048]{2,1,0:T(4,128)(2,1)}, u32[]{:S(2)}, u32[]{:S(2)}) async-start(bf16[32,4,2048]{2,1,0:T(4,128)(2,1)} %broadcast_in_dim.96), calls=%async_computation | async-start | bytes 1048576 | tf_op jit(solution)/shard_map/all_to_all | solution.py:69
  19.3 18.4 %collective-permute-start.1 = (bf16[2048,112]{0,1:T(8,128)(2,1)}, bf16[2048,112]{0,1:T(8,128)(2,1)}, u32[]{:S(2)}, u32[]{:S(2)}) collective-permute-start(bf16[2048,112]{0,1:T(8,128)(2,1)} %param.18), channel_id=1, source_target_pairs={{0,8},{8,0},{1,9},{9,1},{2,10},{10,2},{3,11},{11,3},{4,12},{12,4},... | collective-permute-start | bytes 1376264 | tf_op jit(solution)/shard_map/ppermute | solution.py:65
  23.1 6.8 %collective-permute-start = (bf16[32,112]{1,0:T(8,128)(2,1)S(1)}, bf16[32,112]{1,0:T(8,128)(2,1)S(1)}, u32[]{:S(2)}, u32[]{:S(2)}) collective-permute-start(bf16[32,112]{1,0:T(8,128)(2,1)S(1)} %pad_maximum_fusion.3), channel_id=1, source_target_pairs={{0,8},{8,0},{1,9},{9,1},{2,10},{10,2},{3,11},{11,3},{4,12},{12,4},... | collective-permute-start | bytes 21512 | tf_op jit(solution)/shard_map/ppermute | solution.py:65
  27.0 37.5 %collective-permute-start.3 = (bf16[112,2304]{1,0:T(8,128)(2,1)}, bf16[112,2304]{1,0:T(8,128)(2,1)}, u32[]{:S(2)}, u32[]{:S(2)}) collective-permute-start(bf16[112,2304]{1,0:T(8,128)(2,1)} %pad_maximum_fusion.1), channel_id=1, source_target_pairs={{0,16},{16,0},{1,17},{17,1},{2,18},{18,2},{3,19},{19,3},{4,20},{20... | collective-permute-start | bytes 1548296 | tf_op jit(solution)/shard_map/ppermute | solution.py:65
  39.7 13.0 %all-to-all-start.1 = ((bf16[8,2,16,112]{3,2,1,0:T(8,128)(2,1)}), bf16[8,2,16,112]{3,2,1,0:T(8,128)(2,1)S(1)}, u32[]{:S(2)}, u32[]{:S(2)}) async-start(bf16[8,2,16,112]{3,2,1,0:T(8,128)(2,1)} %copy.117), calls=%async_computation.1 | async-start | bytes 131072 | tf_op jit(solution)/shard_map/all_to_all | solution.py:69
  53.9 12.7 %all-to-all-start.2 = ((bf16[16,2,16,128]{3,2,1,0:T(8,128)(2,1)}), bf16[16,2,16,128]{3,2,1,0:T(8,128)(2,1)S(1)}, u32[]{:S(2)}, u32[]{:S(2)}) async-start(bf16[16,2,16,128]{3,2,1,0:T(8,128)(2,1)} %broadcast_in_dim.98), calls=%async_computation.2 | async-start | bytes 262144 | tf_op jit(solution)/shard_map/all_to_all | solution.py:69
  58.8 9.4 %collective-permute-start.2 = (bf16[112,2304]{1,0:T(8,128)(2,1)S(1)}, bf16[112,2304]{1,0:T(8,128)(2,1)}, u32[]{:S(2)}, u32[]{:S(2)}) collective-permute-start(bf16[112,2304]{1,0:T(8,128)(2,1)S(1)} %pad_maximum_fusion), channel_id=1, source_target_pairs={{0,8},{8,0},{1,9},{9,1},{2,10},{10,2},{3,11},{11,3},{4,12},{12,4},... | collective-permute-start | bytes 1548296 | tf_op jit(solution)/shard_map/ppermute | solution.py:65
  64.6 6.3 %collective-permute-start.4 = (bf16[112,2304]{1,0:T(8,128)(2,1)}, bf16[112,2304]{1,0:T(8,128)(2,1)}, u32[]{:S(2)}, u32[]{:S(2)}) collective-permute-start(bf16[112,2304]{1,0:T(8,128)(2,1)} %collective-permute-done.3), channel_id=1, source_target_pairs={{0,8},{8,0},{1,9},{9,1},{2,10},{10,2},{3,11},{11,3},{4,12},{12,4},... | collective-permute-start | bytes 1548296 | tf_op jit(solution)/shard_map/ppermute | solution.py:65
  70.9 1.4 copy-start.4
  92.3 7.9 %copy-start.3 = (bf16[2304,112]{0,1:T(8,128)(2,1)S(1)}, bf16[2304,112]{0,1:T(8,128)(2,1)}, u32[]{:S(2)}) copy-start(bf16[2304,112]{0,1:T(8,128)(2,1)} %param.23) | copy-start | bytes 1548292
  93.4 22.5 %all-to-all-start.4 = ((bf16[16,8,1152]{2,1,0:T(8,128)(2,1)}), bf16[16,8,1152]{2,1,0:T(8,128)(2,1)S(1)}, u32[]{:S(2)}, u32[]{:S(2)}) async-start(bf16[16,8,1152]{2,1,0:T(8,128)(2,1)} %broadcast_in_dim.100), calls=%async_computation.4 | async-start | bytes 589824 | tf_op jit(solution)/shard_map/all_to_all | solution.py:69
  100.2 9.0 %collective-permute-start.6 = (bf16[1152,112]{0,1:T(8,128)(2,1)S(1)}, bf16[1152,112]{0,1:T(8,128)(2,1)S(1)}, u32[]{:S(2)}, u32[]{:S(2)}) collective-permute-start(bf16[1152,112]{0,1:T(8,128)(2,1)S(1)} %get-tuple-element.10), channel_id=1, source_target_pairs={{0,16},{16,0},{1,17},{17,1},{2,18},{18,2},{3,19},{19,3},{4,20},{20... | collective-permute-start | bytes 774152 | tf_op jit(solution)/shard_map/ppermute | solution.py:65
  102.2 14.0 %collective-permute-start.5 = (bf16[1152,112]{0,1:T(8,128)(2,1)S(1)}, bf16[1152,112]{0,1:T(8,128)(2,1)S(1)}, u32[]{:S(2)}, u32[]{:S(2)}) collective-permute-start(bf16[1152,112]{0,1:T(8,128)(2,1)S(1)} %get-tuple-element.9), channel_id=1, source_target_pairs={{0,8},{8,0},{1,9},{9,1},{2,10},{10,2},{3,11},{11,3},{4,12},{12,4},... | collective-permute-start | bytes 774152 | tf_op jit(solution)/shard_map/ppermute | solution.py:65
  109.2 8.2 %collective-permute-start.7 = (bf16[1152,112]{0,1:T(8,128)(2,1)S(1)}, bf16[1152,112]{0,1:T(8,128)(2,1)S(1)}, u32[]{:S(2)}, u32[]{:S(2)}) collective-permute-start(bf16[1152,112]{0,1:T(8,128)(2,1)S(1)} %collective-permute-done.6), channel_id=1, source_target_pairs={{0,8},{8,0},{1,9},{9,1},{2,10},{10,2},{3,11},{11,3},{4,12},{12,4},... | collective-permute-start | bytes 774152 | tf_op jit(solution)/shard_map/ppermute | solution.py:65
  136.9 4.3 %collective-permute-start.8 = (f32[32,112]{1,0:T(8,128)S(1)}, f32[32,112]{1,0:T(8,128)S(1)}, u32[]{:S(2)}, u32[]{:S(2)}) collective-permute-start(f32[32,112]{1,0:T(8,128)S(1)} %slice_bitcast_fusion), channel_id=1, source_target_pairs={{0,8},{8,0},{1,9},{9,1},{2,10},{10,2},{3,11},{11,3},{4,12},{12,4},... | collective-permute-start | bytes 43016 | tf_op jit(solution)/shard_map/ppermute | solution.py:65

commit v2 on v1

--- a/solution.py
+++ b/solution.py
@@ -75,13 +75,6 @@
 
 def dot(a, b):
     return jnp.dot(a, b, preferred_element_type=F32)
-
-
-def halves(weight, axis, index):
-    size = weight.shape[axis] // 2
-    keep = lax.dynamic_slice_in_dim(weight, index * size, size, axis)
-    send = lax.dynamic_slice_in_dim(weight, (1 - index) * size, size, axis)
-    return keep, send
 
 
 def local(
@@ -98,7 +91,8 @@
     w_up,
     w_down,
 ):
-    xl, core, tp = lax.axis_index("xl"), lax.axis_index("c"), lax.axis_index("y")
+    xh, xl = lax.axis_index("xh"), lax.axis_index("xl")
+    core, tp = lax.axis_index("c"), lax.axis_index("y")
     width = out_proj.shape[1]
     row_ids = jnp.arange(128, dtype=jnp.int32)
     out_ids = jnp.arange(256, dtype=jnp.int32)
@@ -121,16 +115,28 @@
 
     head_values = attention(queries, new_latents, latent_cache, lengths, value_maps)
 
-    gate_keep, gate_send = halves(w_gate, 1, xl)
-    up_keep, up_send = halves(w_up, 1, xl)
-    ff_own = jnp.concatenate([gate_keep, up_keep], axis=1)
-    ff_next = swap(jnp.concatenate([gate_send, up_send], axis=1), "xl")
-    ff_own_other = swap(ff_own, "c")
-    ff_next_other = swap(ff_next, "c")
-    down_own, down_send = halves(w_down, 0, xl)
-    down_next = swap(down_send, "xl")
-    down_own_other = swap(down_own, "c")
-    down_next_other = swap(down_next, "c")
+    def piece(xh_to, xl_to):
+        quarter = 2 * xh_to + xl_to
+        cut = lambda w: lax.dynamic_slice_in_dim(w, quarter * size, size, 1)
+        return jnp.concatenate([cut(w_gate), cut(w_up)], axis=1)
+
+    def spread(mine, for_xh, for_xl, for_both):
+        from_xl = swap(jnp.stack([for_xl, for_both]), "xl")
+        from_xh = swap(jnp.stack([for_xh, from_xl[1]]), "xh")
+        held = jnp.concatenate([mine[None], from_xl[:1], from_xh], axis=0)
+        return held, swap(held, "c")
+
+    size = w_gate.shape[1] // 4
+    ff_own, ff_other = spread(
+        piece(xh, xl), piece(1 - xh, xl), piece(xh, 1 - xl), piece(1 - xh, 1 - xl)
+    )
+
+    def rows_piece(xh_to, xl_to):
+        return lax.dynamic_slice_in_dim(w_down, (2 * xh_to + xl_to) * size, size, 0)
+
+    down_own, down_other = spread(
+        rows_piece(xh, xl), rows_piece(1 - xh, xl), rows_piece(xh, 1 - xl), rows_piece(1 - xh, 1 - xl)
+    )
 
     rows = gather(head_values, ("z", "xh", "xl"), 32).reshape(128, -1)
     part = jnp.stack([dot(rows, out_proj), dot(rows, out_other)]).astype(BF)
@@ -146,37 +152,35 @@
     extra = jnp.pad(extra[None], ((0, 1), (0, 0), (0, 128 - width - 2)))
     scaled = jnp.concatenate([(hidden * gain).astype(BF), extra], axis=2)
 
-    full = gather(scaled, ("xl", "y"), 16).reshape(2, 8, 2, 16, 128)
-    near = lax.dynamic_index_in_dim(full, xl, 0, False)
-    far = lax.dynamic_index_in_dim(full, 1 - xl, 0, False)
-    rows_of = lambda a, o: a[:, o, :, :width].reshape(128, width)
-    ff = (
-        dot(rows_of(near, 0), ff_own)
-        + dot(rows_of(near, 1), ff_own_other)
-        + dot(rows_of(far, 0), ff_next)
-        + dot(rows_of(far, 1), ff_next_other)
-    )
+    full = gather(scaled, ("xh", "xl", "y"), 32).reshape(4, 8, 2, 16, 128)
+    order = [2 * xh + xl, 2 * xh + 1 - xl, 2 * (1 - xh) + xl, 2 * (1 - xh) + 1 - xl]
+    ff = jnp.zeros((128, 2 * size), F32)
+    for i in range(4):
+        held = lax.dynamic_index_in_dim(full, order[i], 0, False)
+        ff = ff + dot(held[:, 0, :, :width].reshape(128, width), ff_own[i])
+        ff = ff + dot(held[:, 1, :, :width].reshape(128, width), ff_other[i])
     sums = jnp.sum(full[:, :, 0, :, width : width + 2].astype(F32), axis=(0, 3)).reshape(128, 1)
     high = sums.astype(BF)
     low = (sums - high.astype(F32)).astype(BF)
     ff = jnp.concatenate([ff.astype(BF), high, low, jnp.zeros((128, 126), BF)], axis=1)
-    total = jnp.sum(exchange(ff.reshape(16, 8, -1), ("z", "xh")).astype(F32), axis=0)
-    half = w_gate.shape[1] // 2
-    square_sums = total[:, 2 * half : 2 * half + 1] + total[:, 2 * half + 1 : 2 * half + 2]
+    total = jnp.sum(exchange(ff.reshape(8, 16, -1), "z").astype(F32), axis=0)
+    square_sums = total[:, 2 * size : 2 * size + 1] + total[:, 2 * size + 1 : 2 * size + 2]
     factor = lax.rsqrt(square_sums / D + norm_eps)
-    units = (jax.nn.silu(total[:, :half] * factor) * (total[:, half : 2 * half] * factor)).astype(BF)
-
-    units = gather(units, ("z", "xh"), 16).reshape(128, half)
+    units = (jax.nn.silu(total[:, :size] * factor) * (total[:, size : 2 * size] * factor)).astype(BF)
+
+    units = gather(units, "z", 8).reshape(128, size)
+    product = lambda w: jnp.einsum("rk,bkn->brn", units, w, preferred_element_type=F32)
     hidden_rows = lax.dynamic_update_slice_in_dim(
         jnp.zeros((2, 128, width), F32), hidden, tp * 16, 1
     )
-    own = jnp.stack([dot(units, down_own), dot(units, down_own_other)]) + hidden_rows
-    nxt = jnp.stack([dot(units, down_next), dot(units, down_next_other)])
-    both = jnp.where(xl == 0, jnp.stack([own, nxt]), jnp.stack([nxt, own])).astype(BF)
-    both = jnp.einsum("qr,xork->xoqk", mine, both, preferred_element_type=F32).astype(BF)
-    both = both.reshape(2, 2, 8, 32, width).transpose(0, 2, 1, 3, 4).reshape(16, 2, 32, width)
-    share = jnp.sum(exchange(both, ("xl", "y")).astype(F32), axis=0)
-    return (share[0] + swap(share[1], "c")).astype(BF)
+    at_own = lambda a, o: jnp.concatenate([a[:1] + hidden_rows[o], a[1:]], axis=0).astype(BF)
+    for_own = at_own(product(down_own), 0)
+    for_other = swap(at_own(product(down_other), 1), "c")
+    ranks = jnp.stack([jnp.argmax(jnp.stack(order) == i) for i in range(4)])
+    place = lambda m, a: jnp.einsum("qr,xrk->xqk", m, a, preferred_element_type=F32)
+    both = (place(mine, for_own) + place(others, for_other)).astype(BF)
+    both = jnp.take(both, ranks, axis=0).reshape(32, 32, width)
+    return jnp.sum(exchange(both, ("xh", "xl", "y")).astype(F32), axis=0).astype(BF)
 
 
 def solution(mesh):

time: 143 us -> 155 us (1.084)
  the two profiles are of different devices: /device:TPU:15 before, /device:TPU:8 now
where the time goes in v2:
time: 155 us; the launch traced here: 154 us
  starting transfers between devices  63.7 us (41%)
  blocking collectives  22.5 us (15%)
  waiting for transfers between devices  18.3 us (12%)
  other arithmetic  18 us (12%)
  local copies, waits for them, and re-layouts  17.3 us (11%)
  matrix products  12.7 us (8%)
    all_to_all x5, starting transfers between devices, exchange(): return lax.all_to_all(blocks, axes, 0, 0, tiled=True)  39.1 us
    ppermute x9, starting transfers between devices, swap(): return lax.ppermute(value, axis, [(0, 1), (1, 0)])  24.6 us
    all_to_all x1, blocking collectives, exchange(): return lax.all_to_all(blocks, axes, 0, 0, tiled=True)  22.5 us
    all_to_all x5, waiting for transfers between devices, exchange(): return lax.all_to_all(blocks, axes, 0, 0, tiled=True)  12.7 us
    dot_general x10, matrix products, dot(): return jnp.dot(a, b, preferred_element_type=F32)  8.43 us
    ppermute x9, waiting for transfers between devices, swap(): return lax.ppermute(value, axis, [(0, 1), (1, 0)])  5.63 us
  transfers between devices with their start and end apart: 14, of which 6 were waited for; matrix products, arithmetic and copies ran while one was open for 22% of the time, Pallas kernels for 0%

profile of v2, /device:TPU:8, one launch (start us, length us, event | category | flops | bytes accessed | tf_op | source)
XLA Modules:
  0.0 153.9 jit_solution(16811212253584429580)
XLA Ops:
  0.0 2.8 %constant_dynamic-slice_fusion.6 = (bf16[112,576]{1,0:T(8,128)(2,1)S(1)}, bf16[112,576]{1,0:T(8,128)(2,1)S(1)}, bf16[112,576]{1,0:T(8,128)(2,1)}, bf16[112,576]{...) fusion(bf16[112,2304]{1,0:T(8,128)(2,1)} %param.22, ...), kind=kLoop, calls=%fused_computation.124 | loop fusion | bytes 2064400 | tf_op jit(solution)/shard_map/dynamic_slice | solution.py:120
  3.0 0.9 pad_maximum_fusion.2
  3.9 3.4 %collective-permute-start.4 = (bf16[2,112,1152]{2,1,0:T(8,128)(2,1)}, bf16[2,112,1152]{2,1,0:T(8,128)(2,1)S(1)}, u32[]{:S(2)}, u32[]{:S(2)}) collective-permute-start(bf16[2,112,1152]{2,1,0:T(8,128)(2,1)} %pad_maximum_fusion.2), channel_id=1, source_target_pairs={{0,16},{16,0},{1,17},{17,1},{2,18},{18,2},{3,19},{19,3},{4,20},{20... | collective-permute-start | bytes 1548296 | tf_op jit(solution)/shard_map/ppermute | solution.py:65
  9.8 1.0 broadcast_in_dim.122
  10.9 12.9 %all-to-all-start = ((bf16[32,4,2048]{2,1,0:T(4,128)(2,1)}), bf16[32,4,2048]{2,1,0:T(4,128)(2,1)S(1)}, u32[]{:S(2)}, u32[]{:S(2)}) async-start(bf16[32,4,2048]{2,1,0:T(4,128)(2,1)} %broadcast_in_dim.122), calls=%async_computation | async-start | bytes 1048576 | tf_op jit(solution)/shard_map/all_to_all | solution.py:69
  23.8 1.9 %collective-permute-start.3 = (bf16[2048,112]{0,1:T(8,128)(2,1)}, bf16[2048,112]{0,1:T(8,128)(2,1)}, u32[]{:S(2)}, u32[]{:S(2)}) collective-permute-start(bf16[2048,112]{0,1:T(8,128)(2,1)} %param.18), channel_id=1, source_target_pairs={{0,8},{8,0},{1,9},{9,1},{2,10},{10,2},{3,11},{11,3},{4,12},{12,4},... | collective-permute-start | bytes 1376264 | tf_op jit(solution)/shard_map/ppermute | solution.py:65
  26.6 2.4 %collective-permute-start.2 = (bf16[32,112]{1,0:T(8,128)(2,1)S(1)}, bf16[32,112]{1,0:T(8,128)(2,1)S(1)}, u32[]{:S(2)}, u32[]{:S(2)}) collective-permute-start(bf16[32,112]{1,0:T(8,128)(2,1)S(1)} %pad_maximum_fusion.9), channel_id=1, source_target_pairs={{0,8},{8,0},{1,9},{9,1},{2,10},{10,2},{3,11},{11,3},{4,12},{12,4},... | collective-permute-start | bytes 21512 | tf_op jit(solution)/shard_map/ppermute | solution.py:65
  29.0 2.1 %dynamic-slice_bitcast_fusion.3 = (bf16[1,576,112]{1,2,0:T(8,128)(2,1)}, bf16[1,576,112]{1,2,0:T(8,128)(2,1)S(1)}, bf16[1,576,112]{1,2,0:T(8,128)(2,1)}, bf16[1,576,112]{1,2,0:T(8,128)(2,1)S(1)}) fusion(bf16[2304,112]{0,1:T(8,128)(2,1)} %param.23, s32[]{:T(128)S(6)} %select_n.131, s32[]{:T(128)S(6)} %select_n.132, s32[]{:T(128)S(6)} %select_n.134, ...), kind=kLoop, calls=%fused_computation.63 | loop fusion | bytes 1032208 | tf_op jit(solution)/shard_map/broadcast_in_dim | solution.py:126
  31.2 0.8 pad_maximum_fusion.4
  31.9 3.7 %collective-permute-start = (bf16[2,576,112]{1,2,0:T(8,128)(2,1)}, bf16[2,576,112]{1,2,0:T(8,128)(2,1)}, u32[]{:S(2)}, u32[]{:S(2)}) collective-permute-start(bf16[2,576,112]{1,2,0:T(8,128)(2,1)} %pad_maximum_fusion.4), channel_id=1, source_target_pairs={{0,16},{16,0},{1,17},{17,1},{2,18},{18,2},{3,19},{19,3},{4,20},{20... | collective-permute-start | bytes 774152 | tf_op jit(solution)/shard_map/ppermute | solution.py:65
  35.6 1.8 %maximum_bitcast_fusion.2 = bf16[1,112,1152]{2,1,0:T(8,128)(2,1)} fusion(bf16[112,576]{1,0:T(8,128)(2,1)} %get-tuple-element.27, bf16[112,576]{1,0:T(8,128)(2,1)} %get-tuple-element.58), kind=kLoop, calls=%fused_computation.54 | loop fusion | flops 516096 | bytes 516096 | tf_op jit(solution)/shard_map/stack | solution.py:125
  37.4 0.8 fusion.24
  38.5 0.9 fusion.71
  39.5 1.8 %all-to-all-done = bf16[32,4,2048]{2,1,0:T(4,128)(2,1)S(1)} async-done(((bf16[32,4,2048]{2,1,0:T(4,128)(2,1)}), bf16[32,4,2048]{2,1,0:T(4,128)(2,1)S(1)}, u32[]{:S(2)}, u32[]{:S(2)}) %all-to-all-start) | async-done | bytes 524320 | tf_op jit(solution)/shard_map/all_to_all | solution.py:69
  41.4 1.4 fusion.9
  42.8 1.3 fusion.10
  44.8 7.5 %all-to-all-start.1 = ((bf16[8,2,16,112]{3,2,1,0:T(8,128)(2,1)}), bf16[8,2,16,112]{3,2,1,0:T(8,128)(2,1)S(1)}, u32[]{:S(2)}, u32[]{:S(2)}) async-start(bf16[8,2,16,112]{3,2,1,0:T(8,128)(2,1)} %copy.79), calls=%async_computation.1 | async-start | bytes 131072 | tf_op jit(solution)/shard_map/all_to_all | solution.py:69
  52.3 0.8 pad_maximum_fusion.3
  53.2 4.2 %collective-permute-start.5 = (bf16[2,112,1152]{2,1,0:T(8,128)(2,1)}, bf16[2,112,1152]{2,1,0:T(8,128)(2,1)S(1)}, u32[]{:S(2)}, u32[]{:S(2)}) collective-permute-start(bf16[2,112,1152]{2,1,0:T(8,128)(2,1)} %pad_maximum_fusion.3), channel_id=1, source_target_pairs={{0,32},{32,0},{1,33},{33,1},{2,34},{34,2},{3,35},{35,3},{4,36},{36... | collective-permute-start | bytes 1548296 | tf_op jit(solution)/shard_map/ppermute | solution.py:65
  57.4 1.8 %all-to-all-done.1 = bf16[8,2,16,112]{3,2,1,0:T(8,128)(2,1)S(1)} async-done(((bf16[8,2,16,112]{3,2,1,0:T(8,128)(2,1)}), bf16[8,2,16,112]{3,2,1,0:T(8,128)(2,1)S(1)}, u32[]{:S(2)}, u32[]{:S(2)}) %all-to-all-start.1) | async-done | bytes 57376 | tf_op jit(solution)/shard_map/all_to_all | solution.py:69
  59.6 0.8 broadcast_in_dim.124
  60.4 6.2 %all-to-all-start.2 = ((bf16[32,2,16,128]{3,2,1,0:T(8,128)(2,1)}), bf16[32,2,16,128]{3,2,1,0:T(8,128)(2,1)S(1)}, u32[]{:S(2)}, u32[]{:S(2)}) async-start(bf16[32,2,16,128]{3,2,1,0:T(8,128)(2,1)} %broadcast_in_dim.124), calls=%async_computation.2 | async-start | bytes 524288 | tf_op jit(solution)/shard_map/all_to_all | solution.py:69
  66.6 0.8 compare_reduce_fusion.3
  67.4 1.7 %fusion.72 = (bf16[1,576,112]{1,2,0:T(8,128)(2,1)S(1)}, bf16[1,576,112]{1,2,0:T(8,128)(2,1)}) fusion(bf16[2,576,112]{1,2,0:T(8,128)(2,1)} %collective-permute-done), kind=kLoop, calls=%fused_computation.173 | loop fusion | bytes 516096 | tf_op jit(solution)/shard_map/slice | solution.py:126
  69.0 2.2 %pad_maximum_fusion = bf16[4,112,1152]{2,1,0:T(8,128)(2,1)} fusion(bf16[2,112,1152]{2,1,0:T(8,128)(2,1)S(1)} %collective-permute-done.5, bf16[1,112,1152]{2,1,0:T(8,128)(2,1)} %get-tuple-element.29, bf16[1,112,1152]{2,1,0:T(8,128)(2,1)} %fusion.24), kind=kLoop, calls=%fused_computation.27 | loop fusion | flops 1032192 | bytes 2064384 | tf_op jit(solution)/shard_map/concatenate | solution.py:126
  71.2 1.9 %collective-permute-start.6 = (bf16[4,112,1152]{2,1,0:T(8,128)(2,1)}, bf16[4,112,1152]{2,1,0:T(8,128)(2,1)}, u32[]{:S(2)}, u32[]{:S(2)}) collective-permute-start(bf16[4,112,1152]{2,1,0:T(8,128)(2,1)} %pad_maximum_fusion), channel_id=1, source_target_pairs={{0,8},{8,0},{1,9},{9,1},{2,10},{10,2},{3,11},{11,3},{4,12},{12,4},... | collective-permute-start | bytes 3096584 | tf_op jit(solution)/shard_map/ppermute | solution.py:65
  73.1 4.5 %all-to-all-done.2 = bf16[32,2,16,128]{3,2,1,0:T(8,128)(2,1)S(1)} async-done(((bf16[32,2,16,128]{3,2,1,0:T(8,128)(2,1)}), bf16[32,2,16,128]{3,2,1,0:T(8,128)(2,1)S(1)}, u32[]{:S(2)}, u32[]{:S(2)}) %all-to-all-start.2) | async-done | bytes 262176 | tf_op jit(solution)/shard_map/all_to_all | solution.py:69
  77.6 0.8 slice.156
  78.4 1.1 copy.93
  81.3 1.2 fusion.22
  82.5 1.2 fusion.20
  83.7 1.2 fusion.18
  84.9 1.2 convolution_add_fusion.1
  86.8 0.8 concatenate.75
  87.7 5.2 %all-to-all-start.3 = ((bf16[8,16,1280]{2,1,0:T(8,128)(2,1)}), bf16[8,16,1280]{2,1,0:T(8,128)(2,1)S(1)}, u32[]{:S(2)}, u32[]{:S(2)}) async-start(bf16[8,16,1280]{2,1,0:T(8,128)(2,1)} %concatenate.75), calls=%async_computation.3 | async-start | bytes 655360 | tf_op jit(solution)/shard_map/all_to_all | solution.py:69
  92.9 3.2 %collective-permute-start.1 = (bf16[2,576,112]{1,2,0:T(8,128)(2,1)S(1)}, bf16[2,576,112]{1,2,0:T(8,128)(2,1)S(1)}, u32[]{:S(2)}, u32[]{:S(2)}) collective-permute-start(bf16[2,576,112]{1,2,0:T(8,128)(2,1)S(1)} %pad_maximum_fusion.5), channel_id=1, source_target_pairs={{0,32},{32,0},{1,33},{33,1},{2,34},{34,2},{3,35},{35,3},{4,36},{36... | collective-permute-start | bytes 774152 | tf_op jit(solution)/shard_map/ppermute | solution.py:65
  98.3 4.6 %collective-permute-done.1 = bf16[2,576,112]{1,2,0:T(8,128)(2,1)S(1)} collective-permute-done((bf16[2,576,112]{1,2,0:T(8,128)(2,1)S(1)}, bf16[2,576,112]{1,2,0:T(8,128)(2,1)S(1)}, u32[]{:S(2)}, u32[]{:S(2)}) %collective-permute-start.1) | collective-permute-done | bytes 258080 | tf_op jit(solution)/shard_map/ppermute | solution.py:65
  102.9 0.9 pad_maximum_fusion.1
  103.9 1.9 %collective-permute-start.7 = (bf16[4,576,112]{1,2,0:T(8,128)(2,1)}, bf16[4,576,112]{1,2,0:T(8,128)(2,1)}, u32[]{:S(2)}, u32[]{:S(2)}) collective-permute-start(bf16[4,576,112]{1,2,0:T(8,128)(2,1)} %pad_maximum_fusion.1), channel_id=1, source_target_pairs={{0,8},{8,0},{1,9},{9,1},{2,10},{10,2},{3,11},{11,3},{4,12},{12,4},... | collective-permute-start | bytes 1548296 | tf_op jit(solution)/shard_map/ppermute | solution.py:65
  106.8 7.3 %all-to-all-start.4 = ((bf16[8,16,576]{2,1,0:T(8,128)(2,1)}), bf16[8,16,576]{2,1,0:T(8,128)(2,1)S(1)}, u32[]{:S(2)}, u32[]{:S(2)}) async-start(bf16[8,16,576]{2,1,0:T(8,128)(2,1)} %broadcast_in_dim.127), calls=%async_computation.4 | async-start | bytes 327680 | tf_op jit(solution)/shard_map/all_to_all | solution.py:69
  114.1 2.4 %compare_and_fusion = pred[4]{0:T(512)(128)(4,1)S(1)} fusion(s32[1]{0:T(128)} %bitcast.7, s32[1]{0:T(128)} %bitcast.6, s32[1]{0:T(128)} %bitcast.5, s32[1]{0:T(128)} %bitcast.4), kind=kLoop, calls=%fused_computation.147 | loop fusion | flops 36 | bytes 20 | tf_op jit(solution)/shard_map/jit(_take)/and | solution.py:182
  116.7 2.4 %fusion.64 = s32[4]{0:T(128)S(1)} fusion(s32[1,1]{0,1:T(1,128)} %bitcast.73, s32[1,1]{0,1:T(1,128)} %bitcast.72, s32[1,1]{0,1:T(1,128)} %bitcast.71, s32[1,1]{0,1:T(1,128)} %bitcast.70), kind=kLoop, calls=%fused_computation.157 | loop fusion | flops 24 | bytes 32 | tf_op jit(solution)/shard_map/jit(_take)/jit(_where)/select_n | solution.py:182
  119.1 0.8 dynamic_update_slice.3
  119.9 4.6 %all-to-all-done.4 = bf16[8,16,576]{2,1,0:T(8,128)(2,1)S(1)} async-done(((bf16[8,16,576]{2,1,0:T(8,128)(2,1)}), bf16[8,16,576]{2,1,0:T(8,128)(2,1)S(1)}, u32[]{:S(2)}, u32[]{:S(2)}) %all-to-all-start.4) | async-done | bytes 147488 | tf_op jit(solution)/shard_map/all_to_all | solution.py:69
  124.6 1.4 convolution_bitcast_fusion
  126.4 1.9 %collective-permute-start.8 = (bf16[4,128,112]{1,2,0:T(8,128)(2,1)S(1)}, bf16[4,128,112]{1,2,0:T(8,128)(2,1)S(1)}, u32[]{:S(2)}, u32[]{:S(2)}) collective-permute-start(bf16[4,128,112]{1,2,0:T(8,128)(2,1)S(1)} %pad_maximum_fusion.8), channel_id=1, source_target_pairs={{0,8},{8,0},{1,9},{9,1},{2,10},{10,2},{3,11},{11,3},{4,12},{12,4},... | collective-permute-start | bytes 344072 | tf_op jit(solution)/shard_map/ppermute | solution.py:65
  128.6 1.0 collective-permute-done.8
  130.7 22.5 %all_to_all.30 = bf16[32,32,112]{2,1,0:T(8,128)(2,1)S(1)} all-to-all(bf16[32,32,112]{2,1,0:T(8,128)(2,1)S(1)} %broadcast_select_fusion), channel_id=1, replica_groups=mesh['z'=8,'xh'=2,'xl'=2,'c'=2,'y'=8] {'xh','xl','y'}, dimensions={0} | all-to-all | bytes 458752 | tf_op jit(solution)/shard_map/all_to_all | solution.py:69
  (116 shorter events, 12.7 us)
Async XLA Ops:
  0.0 9.4 %copy-start = (bf16[16,512,128]{2,1,0:T(8,128)(2,1)S(1)}, bf16[16,512,128]{2,1,0:T(8,128)(2,1)}, u32[]{:S(2)}) copy-start(bf16[16,512,128]{2,1,0:T(8,128)(2,1)} %param.17) | copy-start | bytes 6291460
  0.0 8.0 %copy-start.5 = (bf16[1,512,576]{1,2,0:T(8,128)(2,1)S(1)}, bf16[1,512,576]{1,2,0:T(8,128)(2,1)}, u32[]{:S(2)}) copy-start(bf16[1,512,576]{1,2,0:T(8,128)(2,1)} %param.14) | copy-start | bytes 1769476
  0.0 8.0 %copy-start.11 = (bf16[1,4,16,576]{3,2,1,0:T(8,128)(2,1)S(1)}, bf16[1,4,16,576]{3,2,1,0:T(8,128)(2,1)}, u32[]{:S(2)}) copy-start(bf16[1,4,16,576]{3,2,1,0:T(8,128)(2,1)} %param.12) | copy-start | bytes 221188
  0.0 8.3 %copy-start.12 = (bf16[1,4,576]{2,1,0:T(4,128)(2,1)S(1)}, bf16[1,4,576]{2,1,0:T(4,128)(2,1)}, u32[]{:S(2)}) copy-start(bf16[1,4,576]{2,1,0:T(4,128)(2,1)} %param.13) | copy-start | bytes 13828
  3.9 34.6 %collective-permute-start.4 = (bf16[2,112,1152]{2,1,0:T(8,128)(2,1)}, bf16[2,112,1152]{2,1,0:T(8,128)(2,1)S(1)}, u32[]{:S(2)}, u32[]{:S(2)}) collective-permute-start(bf16[2,112,1152]{2,1,0:T(8,128)(2,1)} %pad_maximum_fusion.2), channel_id=1, source_target_pairs={{0,16},{16,0},{1,17},{17,1},{2,18},{18,2},{3,19},{19,3},{4,20},{20... | collective-permute-start | bytes 1548296 | tf_op jit(solution)/shard_map/ppermute | solution.py:65
  9.4 16.3 %copy-start.16 = (s32[64]{0:T(128)S(1)}, s32[64]{0:T(128)}, u32[]{:S(2)}) copy-start(s32[64]{0:T(128)} %param.16) | copy-start | bytes 772
  9.4 16.9 %copy-start.9 = (bf16[256,112]{0,1:T(8,128)(2,1)S(1)}, bf16[256,112]{0,1:T(8,128)(2,1)}, u32[]{:S(2)}) copy-start(bf16[256,112]{0,1:T(8,128)(2,1)} %param.19) | copy-start | bytes 172036
  9.4 17.1 %copy-start.13 = (bf16[112]{0:T(256)(128)(2,1)S(1)}, bf16[112]{0:T(256)(128)(2,1)}, u32[]{:S(2)}) copy-start(bf16[112]{0:T(256)(128)(2,1)} %param.20) | copy-start | bytes 676
  10.9 30.4 %all-to-all-start = ((bf16[32,4,2048]{2,1,0:T(4,128)(2,1)}), bf16[32,4,2048]{2,1,0:T(4,128)(2,1)S(1)}, u32[]{:S(2)}, u32[]{:S(2)}) async-start(bf16[32,4,2048]{2,1,0:T(4,128)(2,1)} %broadcast_in_dim.122), calls=%async_computation | async-start | bytes 1048576 | tf_op jit(solution)/shard_map/all_to_all | solution.py:69
  23.8 19.1 %collective-permute-start.3 = (bf16[2048,112]{0,1:T(8,128)(2,1)}, bf16[2048,112]{0,1:T(8,128)(2,1)}, u32[]{:S(2)}, u32[]{:S(2)}) collective-permute-start(bf16[2048,112]{0,1:T(8,128)(2,1)} %param.18), channel_id=1, source_target_pairs={{0,8},{8,0},{1,9},{9,1},{2,10},{10,2},{3,11},{11,3},{4,12},{12,4},... | collective-permute-start | bytes 1376264 | tf_op jit(solution)/shard_map/ppermute | solution.py:65
  25.7 0.6 copy-start.14
  26.6 11.9 %collective-permute-start.2 = (bf16[32,112]{1,0:T(8,128)(2,1)S(1)}, bf16[32,112]{1,0:T(8,128)(2,1)S(1)}, u32[]{:S(2)}, u32[]{:S(2)}) collective-permute-start(bf16[32,112]{1,0:T(8,128)(2,1)S(1)} %pad_maximum_fusion.9), channel_id=1, source_target_pairs={{0,8},{8,0},{1,9},{9,1},{2,10},{10,2},{3,11},{11,3},{4,12},{12,4},... | collective-permute-start | bytes 21512 | tf_op jit(solution)/shard_map/ppermute | solution.py:65
  31.9 35.5 %collective-permute-start = (bf16[2,576,112]{1,2,0:T(8,128)(2,1)}, bf16[2,576,112]{1,2,0:T(8,128)(2,1)}, u32[]{:S(2)}, u32[]{:S(2)}) collective-permute-start(bf16[2,576,112]{1,2,0:T(8,128)(2,1)} %pad_maximum_fusion.4), channel_id=1, source_target_pairs={{0,16},{16,0},{1,17},{17,1},{2,18},{18,2},{3,19},{19,3},{4,20},{20... | collective-permute-start | bytes 774152 | tf_op jit(solution)/shard_map/ppermute | solution.py:65
  38.5 1.0 copy-start.1
  41.4 10.9 %copy-start.3 = (bf16[1,112,1152]{2,1,0:T(8,128)(2,1)S(1)}, bf16[1,112,1152]{2,1,0:T(8,128)(2,1)}, u32[]{:S(2)}) copy-start(bf16[1,112,1152]{2,1,0:T(8,128)(2,1)} %maximum_bitcast_fusion.2) | copy-start | bytes 774148
  41.4 10.9 %copy-start.4 = (bf16[1,112,1152]{2,1,0:T(8,128)(2,1)S(1)}, bf16[1,112,1152]{2,1,0:T(8,128)(2,1)}, u32[]{:S(2)}) copy-start(bf16[1,112,1152]{2,1,0:T(8,128)(2,1)} %get-tuple-element.30) | copy-start | bytes 774148
  44.8 14.5 %all-to-all-start.1 = ((bf16[8,2,16,112]{3,2,1,0:T(8,128)(2,1)}), bf16[8,2,16,112]{3,2,1,0:T(8,128)(2,1)S(1)}, u32[]{:S(2)}, u32[]{:S(2)}) async-start(bf16[8,2,16,112]{3,2,1,0:T(8,128)(2,1)} %copy.79), calls=%async_computation.1 | async-start | bytes 131072 | tf_op jit(solution)/shard_map/all_to_all | solution.py:69
  53.2 15.8 %collective-permute-start.5 = (bf16[2,112,1152]{2,1,0:T(8,128)(2,1)}, bf16[2,112,1152]{2,1,0:T(8,128)(2,1)S(1)}, u32[]{:S(2)}, u32[]{:S(2)}) collective-permute-start(bf16[2,112,1152]{2,1,0:T(8,128)(2,1)} %pad_maximum_fusion.3), channel_id=1, source_target_pairs={{0,32},{32,0},{1,33},{33,1},{2,34},{34,2},{3,35},{35,3},{4,36},{36... | collective-permute-start | bytes 1548296 | tf_op jit(solution)/shard_map/ppermute | solution.py:65
  60.4 17.2 %all-to-all-start.2 = ((bf16[32,2,16,128]{3,2,1,0:T(8,128)(2,1)}), bf16[32,2,16,128]{3,2,1,0:T(8,128)(2,1)S(1)}, u32[]{:S(2)}, u32[]{:S(2)}) async-start(bf16[32,2,16,128]{3,2,1,0:T(8,128)(2,1)} %broadcast_in_dim.124), calls=%async_computation.2 | async-start | bytes 524288 | tf_op jit(solution)/shard_map/all_to_all | solution.py:69
  71.2 10.1 %collective-permute-start.6 = (bf16[4,112,1152]{2,1,0:T(8,128)(2,1)}, bf16[4,112,1152]{2,1,0:T(8,128)(2,1)}, u32[]{:S(2)}, u32[]{:S(2)}) collective-permute-start(bf16[4,112,1152]{2,1,0:T(8,128)(2,1)} %pad_maximum_fusion), channel_id=1, source_target_pairs={{0,8},{8,0},{1,9},{9,1},{2,10},{10,2},{3,11},{11,3},{4,12},{12,4},... | collective-permute-start | bytes 3096584 | tf_op jit(solution)/shard_map/ppermute | solution.py:65
  81.3 4.8 %copy-start.2 = (bf16[2,112,1152]{2,1,0:T(8,128)(2,1)S(1)}, bf16[2,112,1152]{2,1,0:T(8,128)(2,1)}, u32[]{:S(2)}) copy-start(bf16[2,112,1152]{2,1,0:T(8,128)(2,1)} %copy-done.1) | copy-start | bytes 1548292
  86.1 0.8 copy-start.10
  86.1 6.8 %copy-start.7 = (bf16[1,576,112]{1,2,0:T(8,128)(2,1)S(1)}, bf16[1,576,112]{1,2,0:T(8,128)(2,1)}, u32[]{:S(2)}) copy-start(bf16[1,576,112]{1,2,0:T(8,128)(2,1)} %get-tuple-element.19) | copy-start | bytes 387076
  86.1 6.8 %copy-start.8 = (bf16[1,576,112]{1,2,0:T(8,128)(2,1)S(1)}, bf16[1,576,112]{1,2,0:T(8,128)(2,1)}, u32[]{:S(2)}) copy-start(bf16[1,576,112]{1,2,0:T(8,128)(2,1)} %get-tuple-element.32) | copy-start | bytes 387076
  86.1 16.9 %copy-start.6 = (bf16[1,576,112]{1,2,0:T(8,128)(2,1)S(1)}, bf16[1,576,112]{1,2,0:T(8,128)(2,1)}, u32[]{:S(2)}) copy-start(bf16[1,576,112]{1,2,0:T(8,128)(2,1)} %get-tuple-element.17) | copy-start | bytes 387076
  87.7 18.1 %all-to-all-start.3 = ((bf16[8,16,1280]{2,1,0:T(8,128)(2,1)}), bf16[8,16,1280]{2,1,0:T(8,128)(2,1)S(1)}, u32[]{:S(2)}, u32[]{:S(2)}) async-start(bf16[8,16,1280]{2,1,0:T(8,128)(2,1)} %concatenate.75), calls=%async_computation.3 | async-start | bytes 655360 | tf_op jit(solution)/shard_map/all_to_all | solution.py:69
  92.9 10.0 %collective-permute-start.1 = (bf16[2,576,112]{1,2,0:T(8,128)(2,1)S(1)}, bf16[2,576,112]{1,2,0:T(8,128)(2,1)S(1)}, u32[]{:S(2)}, u32[]{:S(2)}) collective-permute-start(bf16[2,576,112]{1,2,0:T(8,128)(2,1)S(1)} %pad_maximum_fusion.5), channel_id=1, source_target_pairs={{0,32},{32,0},{1,33},{33,1},{2,34},{34,2},{3,35},{35,3},{4,36},{36... | collective-permute-start | bytes 774152 | tf_op jit(solution)/shard_map/ppermute | solution.py:65
  103.9 16.1 %collective-permute-start.7 = (bf16[4,576,112]{1,2,0:T(8,128)(2,1)}, bf16[4,576,112]{1,2,0:T(8,128)(2,1)}, u32[]{:S(2)}, u32[]{:S(2)}) collective-permute-start(bf16[4,576,112]{1,2,0:T(8,128)(2,1)} %pad_maximum_fusion.1), channel_id=1, source_target_pairs={{0,8},{8,0},{1,9},{9,1},{2,10},{10,2},{3,11},{11,3},{4,12},{12,4},... | collective-permute-start | bytes 1548296 | tf_op jit(solution)/shard_map/ppermute | solution.py:65
  106.8 21.5 %copy-start.15 = (s32[128]{0:T(128)S(1)}, s32[128]{0:T(128)}, u32[]{:S(2)}) copy-start(s32[128]{0:T(128)} %copy-done.14) | copy-start | bytes 1540
  106.8 17.8 %all-to-all-start.4 = ((bf16[8,16,576]{2,1,0:T(8,128)(2,1)}), bf16[8,16,576]{2,1,0:T(8,128)(2,1)S(1)}, u32[]{:S(2)}, u32[]{:S(2)}) async-start(bf16[8,16,576]{2,1,0:T(8,128)(2,1)} %broadcast_in_dim.127), calls=%async_computation.4 | async-start | bytes 327680 | tf_op jit(solution)/shard_map/all_to_all | solution.py:69
  126.4 3.2 %collective-permute-start.8 = (bf16[4,128,112]{1,2,0:T(8,128)(2,1)S(1)}, bf16[4,128,112]{1,2,0:T(8,128)(2,1)S(1)}, u32[]{:S(2)}, u32[]{:S(2)}) collective-permute-start(bf16[4,128,112]{1,2,0:T(8,128)(2,1)S(1)} %pad_maximum_fusion.8), channel_id=1, source_target_pairs={{0,8},{8,0},{1,9},{9,1},{2,10},{10,2},{3,11},{11,3},{4,12},{12,4},... | collective-permute-start | bytes 344072 | tf_op jit(solution)/shard_map/ppermute | solution.py:65

commit v3 on v0

v3 whole, which is shorter than its diff:
```python
import jax
import jax.numpy as jnp
from jax import lax
from jax.experimental import pallas as pl
from jax.experimental.pallas import tpu as pltpu
from jax.sharding import Mesh
from jax.sharding import PartitionSpec as P

D = 7168
WIDTH = 112
SIZE = 576

PACK = 14 * 128

score_scale = 192.0 ** (-0.5)
norm_eps = 1e-06

AXES = ("z", "x", "c", "y")
DP = ("z", "x", "c")
BF = jnp.bfloat16
F32 = jnp.float32
VMEM = pl.BlockSpec(memory_space=pltpu.VMEM)
SMEM = pl.BlockSpec(memory_space=pltpu.SMEM)
HBM = pl.BlockSpec(memory_space=pltpu.HBM)


def call(kernel, in_specs, outs, scratch=(), flops=0, moved=0, limit=24):
    many = isinstance(outs, (list, tuple))
    return pl.pallas_call(
        kernel,
        in_specs=in_specs,
        out_specs=[VMEM] * len(outs) if many else VMEM,
        out_shape=list(outs) if many else outs,
        scratch_shapes=list(scratch),
        compiler_params=pltpu.CompilerParams(vmem_limit_bytes=limit * 1024 * 1024),
        cost_estimate=pl.CostEstimate(flops=flops, bytes_accessed=moved, transcendentals=0),
    )


def shape(dims, dtype=BF):
    return jax.ShapeDtypeStruct(dims, dtype)


def dot(a, b):
    return jnp.dot(a, b, preferred_element_type=F32)


def attention_kernel(len_ref, q_ref, new_ref, cache_ref, maps_ref, out_ref, q_in, cache, maps, ctx, heads, sems):
    fetches = [
        pltpu.make_async_copy(src, dst, sems.at[i])
        for i, (src, dst) in enumerate(((q_ref, q_in), (cache_ref, cache), (maps_ref, maps)))
    ]
    for fetch in fetches:
        fetch.start()
    new = new_ref[...]
    nt = (((1,), (1,)), ((), ()))
    fetches[0].wait()
    q = q_in[...]
    fresh = lax.dot_general(q, new, nt, preferred_element_type=F32) * score_scale
    fetches[1].wait()
    score = dot(q, cache[...]) * score_scale
    keep = lax.broadcasted_iota(jnp.int32, score.shape, 1) < len_ref[0]
    step = lax.broadcasted_iota(jnp.int32, fresh.shape, 0) // 16
    keep_new = lax.broadcasted_iota(jnp.int32, fresh.shape, 1) <= step
    score = jnp.where(keep, score, -1e30)
    fresh = jnp.where(keep_new, fresh, -1e30)
    top = jnp.maximum(
        jnp.max(score, axis=1, keepdims=True), jnp.max(fresh, axis=1, keepdims=True)
    )
    weight = jnp.where(keep, jnp.exp(score - top), 0.0)
    weight_new = jnp.where(keep_new, jnp.exp(fresh - top), 0.0)
    total = jnp.sum(weight, axis=1, keepdims=True) + jnp.sum(weight_new, axis=1, keepdims=True)
    prob = (weight / total).astype(BF)
    prob_new = (weight_new / total).astype(BF)
    context = lax.dot_general(prob, cache[:512, :], nt, preferred_element_type=F32)
    context = (context + dot(prob_new, new[:, :512])).astype(BF).astype(F32)
    for n in range(4):
        ctx[n] = context[:, n * 128 : (n + 1) * 128]
    fetches[2].wait()
    for h in range(16):
        rows = jnp.concatenate([ctx[n, pl.ds(h, 4, stride=16), :] for n in range(4)], axis=1).astype(BF)
        k, place = h // 4, h % 4
        heads[k * 4 : k * 4 + 4, place * 128 : place * 128 + 128] = dot(rows, maps[h])
    block = heads[...].astype(BF)
    for i in range(32):
        out_ref[i] = block


def pack_kernel(x_ref, gate_ref, up_ref, down_ref, *outs):
    pad = jnp.zeros((WIDTH, PACK - 3 * SIZE), BF)
    for r, out_ref in enumerate(outs):
        for q in range(4):

            @pl.when((x_ref[0] ^ r) == q)
            def _(out_ref=out_ref, q=q):
                cut = slice(q * SIZE, (q + 1) * SIZE)
                out_ref[...] = jnp.concatenate(
                    [gate_ref[:, cut], up_ref[:, cut], down_ref[:, cut], pad], axis=1
                )


def out_kernel(x_ref, own_ref, other_ref, out_ref, wide):
    for n in range(4):
        wide[n] = x_ref[:, :, n * 128 : (n + 1) * 128].reshape(512, 128).astype(F32)
    pad = jnp.zeros((128 - WIDTH, 512), BF)
    total = jnp.zeros((128, 256), F32)
    for k in range(4):
        rows = []
        for t in range(4):
            tiles = [wide[n, pl.ds(k * 4 + t, 32, stride=16), :] for n in range(4)]
            rows.append(jnp.concatenate(tiles, axis=1).astype(BF))
        cut = slice(k * 512, (k + 1) * 512)
        w = jnp.concatenate([own_ref[:, cut], pad, other_ref[:, cut], pad], axis=0)
        total = total + lax.dot_general(
            jnp.concatenate(rows, axis=0), w, (((1,), (1,)), ((), ())), preferred_element_type=F32
        )
    total = total.astype(BF)
    for y in range(8):
        part = total[y * 16 : y * 16 + 16]
        out_ref[y, 0:16, :] = part[:, :WIDTH]
        out_ref[y, 16:32, :] = part[:, 128 : 128 + WIDTH]


def norm_kernel(part_ref, pick_ref, own_ref, other_ref, out_ref, hidden_ref):
    attended = part_ref[0].astype(F32)
    for i in range(1, 8):
        attended = attended + part_ref[i].astype(F32)
    nt = (((1,), (1,)), ((), ()))
    pick = pick_ref[...]
    unit = (lax.broadcasted_iota(jnp.int32, (16, 128), 1) == 0).astype(F32).astype(BF)
    picked = lambda ref: lax.dot_general(pick, ref[:, :256], nt, preferred_element_type=F32)
    gains = lambda ref: lax.dot_general(unit, ref[:, 256:], nt, preferred_element_type=F32)
    hidden = attended + jnp.concatenate([picked(own_ref), picked(other_ref)], axis=0)
    gain = jnp.concatenate([gains(own_ref), gains(other_ref)], axis=0)
    squares = jnp.sum(hidden * hidden, axis=1, keepdims=True)
    squares = squares[0:16] + squares[16:32]
    high = squares.astype(BF).astype(F32)
    low = squares - high
    none = jnp.zeros((32, 128 - WIDTH), F32)
    scaled = jnp.concatenate([hidden * gain, none], axis=1)
    lane = lax.broadcasted_iota(jnp.int32, (32, 128), 1)
    first = lax.broadcasted_iota(jnp.int32, (32, 128), 0) < 16
    twice = lambda a: jnp.concatenate([a, a], axis=0)
    scaled = jnp.where(first & (lane == WIDTH), twice(high), scaled)
    scaled = jnp.where(first & (lane == WIDTH + 1), twice(low), scaled).astype(BF)
    hidden_ref[...] = jnp.concatenate([hidden, none], axis=1)
    for i in range(32):
        out_ref[i] = scaled


def gate_kernel(x_ref, full_ref, *refs):
    own_refs, other_refs, out_ref = refs[:4], refs[4:8], refs[8]
    lane = lax.broadcasted_iota(jnp.int32, (128, 128), 1)
    valid = lane < WIDTH
    none = jnp.zeros((128 - WIDTH, 384), BF)
    held, squares = [], jnp.zeros((128, 1), F32)
    for r in range(4):
        block = full_ref[pl.ds((x_ref[0] ^ r) * 8, 8)]
        own = block[:, 0:16, :].reshape(128, 128)
        other = block[:, 16:32, :].reshape(128, 128)
        sums = jnp.where((lane >= WIDTH) & (lane < WIDTH + 2), own.astype(F32), 0.0)
        squares = squares + jnp.sum(sums, axis=1, keepdims=True)
        zero = jnp.zeros((128, 128), BF)
        held.append(
            jnp.concatenate([jnp.where(valid, own, zero), jnp.where(valid, other, zero)], axis=1)
        )
    for n in range(0, 1152, 384):
        total = jnp.zeros((128, 384), F32)
        for r, w in enumerate(own_refs):
            both = [w[:, n : n + 384], none, other_refs[r][:, n : n + 384], none]
            total = total + dot(held[r], jnp.concatenate(both, axis=0))
        out_ref[:, :, n : n + 384] = total.astype(BF).reshape(8, 16, 384)
    high = squares.astype(BF).astype(F32)
    last = jnp.where(lane == 0, high, jnp.where(lane == 1, squares - high, 0.0))
    out_ref[:, :, 1152:1280] = last.astype(BF).reshape(8, 16, 128)


def units_kernel(part_ref, out_ref):
    total = part_ref[0].astype(F32)
    for i in range(1, 8):
        total = total + part_ref[i].astype(F32)
    squares = total[:, 2 * SIZE : 2 * SIZE + 1] + total[:, 2 * SIZE + 1 : 2 * SIZE + 2]
    factor = lax.rsqrt(squares / D + norm_eps)
    gate = total[:, :SIZE] * factor
    up = total[:, SIZE : 2 * SIZE] * factor
    units = (gate * jax.nn.sigmoid(gate) * up).astype(BF)
    for i in range(8):
        out_ref[i] = units


def down_kernel(
    x_ref, y_ref, own_ref, other_ref, w0, w1, w2, w3, hidden_ref, across_ref, place_ref, out_ref, total
):
    units = jnp.concatenate(
        [own_ref[...].reshape(128, SIZE), other_ref[...].reshape(128, SIZE)], axis=0
    )
    place = place_ref[...]
    none = jnp.zeros((128 - WIDTH, SIZE), BF)
    for r, w in enumerate((w0, w1, w2, w3)):
        part = lax.dot_general(
            units, jnp.concatenate([w[:, 2 * SIZE : 3 * SIZE], none], axis=0), (((1,), (1,)), ((), ())), preferred_element_type=F32
        )
        if r == 0:
            total[...] = part
            at = pl.multiple_of(y_ref[0] * 16, 16)
            total[pl.ds(at, 16), :] += hidden_ref[0:16, :]
            total[pl.ds(128 + at, 16), :] += across_ref[...]
            part = total[...]
        rows = dot(place, part.astype(BF)).astype(BF)
        out_ref[pl.ds((x_ref[0] ^ r) * 8, 8)] = rows[:, :WIDTH].reshape(8, 32, WIDTH)


def swap(value, axis="c"):
    return lax.ppermute(value, axis, [(0, 1), (1, 0)])


def exchange(blocks, axes):
    return lax.all_to_all(blocks, axes, 0, 0, tiled=True)


def local(
    queries,
    new_latents,
    latent_cache,
    lengths,
    slot_of,
    value_maps,
    out_proj,
    residual,
    norm_gain,
    w_gate,
    w_up,
    w_down,
):
    x, core, tp = lax.axis_index("x"), lax.axis_index("c"), lax.axis_index("y")
    xs, ys = x[None].astype(jnp.int32), tp[None].astype(jnp.int32)

    blocks = call(
        attention_kernel,
        [SMEM, HBM, VMEM, HBM, HBM],
        shape((32, 16, 512)),
        [
            pltpu.VMEM((64, 576), BF),
            pltpu.VMEM((576, 512), BF),
            pltpu.VMEM((16, 512, 128), BF),
            pltpu.VMEM((4, 64, 128), F32),
            pltpu.VMEM((16, 512), F32),
            pltpu.SemaphoreType.DMA((3,)),
        ],
        200_000_000,
        4_000_000,
        56,
    )(lengths, queries.reshape(64, -1), new_latents[0], latent_cache[0].T, value_maps)
    blocks, out_proj, slot_of, residual, norm_gain, w_gate, w_up, w_down = lax.optimization_barrier(
        (blocks, out_proj.T, slot_of, residual.T, norm_gain, w_gate, w_up, w_down.T)
    )
    rows = exchange(blocks, ("z", "x"))
    gains = jnp.broadcast_to(norm_gain[:, None], (WIDTH, 128))
    carry = jnp.concatenate([out_proj, residual, gains], axis=1)
    carry_other = swap(carry)
    tail, tail_other = carry[:, 2048:], carry_other[:, 2048:]

    ids = jnp.arange(128, dtype=jnp.int32)
    request_rows = jnp.repeat(slot_of, 4) * 4 + jnp.arange(256, dtype=jnp.int32) % 4
    held_rows = lambda of_core, own: (own % 32) * 8 + of_core * 4 + own // 32
    part_ids = tp * 16 + jnp.arange(16, dtype=jnp.int32)
    pick = (held_rows(core, part_ids)[:, None] == request_rows[None, :]).astype(BF)
    both_rows = jnp.concatenate([held_rows(core, ids), held_rows(1 - core, ids)])
    place = (request_rows[:, None] == both_rows[None, :]).astype(BF)

    packed = call(
        pack_kernel, [SMEM, VMEM, VMEM, VMEM], [shape((WIDTH, PACK))] * 4, (), 0, 3_200_000
    )(xs, w_gate, w_up, w_down)
    weights = [packed[0]] + [
        lax.ppermute(packed[r], "x", [(i, i ^ r) for i in range(4)]) for r in (1, 2, 3)
    ]
    part = call(
        out_kernel,
        [VMEM] * 3,
        shape((8, 32, WIDTH)),
        [pltpu.VMEM((4, 512, 128), F32)],
        300_000_000,
        1_600_000,
    )(rows, out_proj, carry_other)
    scaled, hidden = call(
        norm_kernel, [VMEM] * 4, [shape((32, 32, 128)), shape((32, 128), F32)], (), 0, 400_000
    )(exchange(part, "y"), pick, tail, tail_other)
    scaled, *weights = lax.optimization_barrier((scaled, *weights))
    others = [swap(w) for w in weights]
    part = call(
        gate_kernel, [SMEM] + [VMEM] * 9, shape((8, 16, 1280)), (), 300_000_000, 2_800_000
    )(xs, exchange(scaled, ("x", "y")), *weights, *others)
    units = call(units_kernel, [VMEM], shape((8, 16, SIZE)), (), 0, 500_000)(exchange(part, "z"))
    units, hidden = lax.optimization_barrier((units, hidden))
    across = swap(hidden[16:])
    units = exchange(units, "z")
    part = call(
        down_kernel,
        [SMEM] * 2 + [VMEM] * 9,
        shape((32, 32, WIDTH)),
        [pltpu.VMEM((256, 128), F32)],
        200_000_000,
        1_600_000,
    )(xs, ys, units, swap(units), *weights, hidden, across, place)
    return jnp.sum(exchange(part, ("x", "y")).astype(F32), axis=0).astype(BF)


def solution(mesh):
    fine = Mesh(mesh.devices.reshape(8, 4, 2, 8), AXES)
    specs = (
        P(DP, None, "y", None),
        P(DP, None, None),
        P(DP, None, None),
        P(DP),
        P(),
        P("y", None, None),
        P("y", DP),
        P(None, DP),
        P(DP),
        P(DP, "y"),
        P(DP, "y"),
        P("y", DP),
    )
    return jax.shard_map(
        local, mesh=fine, in_specs=specs, out_specs=P("y", DP), check_vma=False
    )
```

time: 700 us -> 137 us (0.20)
  the two profiles are of different devices: /device:TPU:2 before, /device:TPU:8 now
where the time goes in v3:
time: 137 us; the launch traced here: 136 us
  starting transfers between devices  56.7 us (41%)
  blocking collectives  41.9 us (31%)
  waiting for transfers between devices  19.1 us (14%)
  Pallas kernels  10.4 us (8%)
  local copies, waits for them, and re-layouts  4.46 us (3%)
  other arithmetic  2.6 us (2%)
    all_to_all x2, blocking collectives, exchange(): return lax.all_to_all(blocks, axes, 0, 0, tiled=True)  41.9 us
    all_to_all x4, starting transfers between devices, exchange(): return lax.all_to_all(blocks, axes, 0, 0, tiled=True)  31.9 us
    ppermute x7, starting transfers between devices, swap(): return lax.ppermute(value, axis, [(0, 1), (1, 0)])  14.4 us
    all_to_all x4, waiting for transfers between devices, exchange(): return lax.all_to_all(blocks, axes, 0, 0, tiled=True)  14.2 us
    ppermute x3, starting transfers between devices, local(): lax.ppermute(packed[r], 'x', [(i, i ^ r) for i in range(4)])  10.4 us
    pallas_call x1, Pallas kernels, local(): call(attention_kernel, [SMEM, HBM, VMEM, HBM, HBM], shape((32, 16, 512)),...  3.79 us
    unnamed x20, local copies, waits for them, and re-layouts  2.83 us
  transfers between devices with their start and end apart: 14, of which 7 were waited for; matrix products, arithmetic and copies ran while one was open for 3% of the time, Pallas kernels for 3%

profile of v3, /device:TPU:8, one launch (start us, length us, event | category | flops | bytes accessed | tf_op | source)
XLA Modules:
  0.0 136.3 jit_solution(9795088513248639490)
XLA Ops:
  0.7 3.8 %shard_map.118 = bf16[32,16,512]{2,1,0:T(8,128)(2,1)} custom-call(s32[1]{0:T(128)S(6)} %copy.13.len_ref, bf16[64,576]{1,0:T(8,128)(2,1)} %bitcast.16, bf16[4,576]{1,0:T(4,128)(2,1)} %bitcast.17, bf16[576,512]{1,0:T(8,128)(2,1)} %bitcast.13, bf16[16,512,128]{2,1,0:T(8,128)(2,1)} %maps_ref.1), custom_call_target="tpu_custom_call" | custom-call | flops 200000000 | bytes 4000000 | tf_op jit(solution)/shard_map/pallas_call | solution.py:238
  4.5 0.0 copy-start
  4.5 0.0 copy-start.7
  4.5 0.0 copy-start.1
  4.5 0.0 copy-start.2
  4.5 13.3 %all-to-all-start = ((bf16[32,16,512]{2,1,0:T(8,128)(2,1)}), bf16[32,16,512]{2,1,0:T(8,128)(2,1)S(1)}, u32[]{:S(2)}, u32[]{:S(2)}) async-start(bf16[32,16,512]{2,1,0:T(8,128)(2,1)} %shard_map.118), calls=%async_computation | async-start | bytes 1048576 | tf_op jit(solution)/shard_map/all_to_all | solution.py:218
  17.8 0.1 broadcast_in_dim.10
  18.0 0.0 copy-start.9
  18.0 0.9 pad_maximum_fusion
  18.8 1.9 %collective-permute-start = (bf16[112,2432]{1,0:T(8,128)(2,1)}, bf16[112,2432]{1,0:T(8,128)(2,1)S(1)}, u32[]{:S(2)}, u32[]{:S(2)}) collective-permute-start(bf16[112,2432]{1,0:T(8,128)(2,1)} %pad_maximum_fusion), channel_id=1, source_target_pairs={{0,8},{8,0},{1,9},{9,1},{2,10},{10,2},{3,11},{11,3},{4,12},{12,4},... | collective-permute-start | bytes 1634312 | tf_op jit(solution)/shard_map/ppermute | solution.py:214
  20.8 0.0 copy-start.3
  20.8 1.0 copy-done.3
  21.8 1.5 %shard_map.121 = (bf16[112,1792]{1,0:T(8,128)(2,1)S(1)}, bf16[112,1792]{1,0:T(8,128)(2,1)}, bf16[112,1792]{1,0:T(8,128)(2,1)}, bf16[112,1792]{1,0:T(8,128)(2,1)S(1)}) custom-call(s32[1]{0:T(128)} %bitcast.x_ref, bf16[112,2304]{1,0:T(8,128)(2,1)S(1)} %copy-done.1, bf16[112,2304]{1,0:T(8,128)(2,1)S(1)} %copy-done.2, bf16[112,2304]{1,0:T(8,128)(2,1)S(1)} %bitcast.12), custom_call_target="tpu_custom_call" | custom-call | bytes 3200000 | tf_op jit(solution)/shard_map/pallas_call | solution.py:271
  23.3 3.7 %collective-permute-start.1 = (bf16[112,1792]{1,0:T(8,128)(2,1)}, bf16[112,1792]{1,0:T(8,128)(2,1)S(1)}, u32[]{:S(2)}, u32[]{:S(2)}) collective-permute-start(bf16[112,1792]{1,0:T(8,128)(2,1)} %get-tuple-element.36), channel_id=1, source_target_pairs={{0,16},{16,0},{32,48},{48,32},{1,17},{17,1},{33,49},{49,33},{2,18}... | collective-permute-start | bytes 1204232 | tf_op jit(solution)/shard_map/ppermute | solution.py:275
  27.0 4.6 %collective-permute-start.2 = (bf16[112,1792]{1,0:T(8,128)(2,1)}, bf16[112,1792]{1,0:T(8,128)(2,1)S(1)}, u32[]{:S(2)}, u32[]{:S(2)}) collective-permute-start(bf16[112,1792]{1,0:T(8,128)(2,1)} %get-tuple-element.37), channel_id=1, source_target_pairs={{0,32},{16,48},{32,0},{48,16},{1,33},{17,49},{33,1},{49,17},{2,34}... | collective-permute-start | bytes 1204232 | tf_op jit(solution)/shard_map/ppermute | solution.py:275
  31.6 2.2 %collective-permute-start.3 = (bf16[112,1792]{1,0:T(8,128)(2,1)S(1)}, bf16[112,1792]{1,0:T(8,128)(2,1)S(1)}, u32[]{:S(2)}, u32[]{:S(2)}) collective-permute-start(bf16[112,1792]{1,0:T(8,128)(2,1)S(1)} %get-tuple-element.38), channel_id=1, source_target_pairs={{0,48},{16,32},{32,16},{48,0},{1,49},{17,33},{33,17},{49,1},{2,50}... | collective-permute-start | bytes 1204232 | tf_op jit(solution)/shard_map/ppermute | solution.py:275
  33.8 0.7 broadcast_in_dim.22
  34.5 0.9 mul.48
  35.4 0.1 compare_convert_fusion.1.pick_ref
  35.5 0.1 all-to-all-done.x_ref
  35.5 1.1 shard_map.119
  36.7 7.6 %all-to-all-start.1 = ((bf16[8,32,112]{2,1,0:T(8,128)(2,1)}), bf16[8,32,112]{2,1,0:T(8,128)(2,1)S(1)}, u32[]{:S(2)}, u32[]{:S(2)}) async-start(bf16[8,32,112]{2,1,0:T(8,128)(2,1)} %shard_map.119), calls=%async_computation.1 | async-start | bytes 131072 | tf_op jit(solution)/shard_map/all_to_all | solution.py:218
  44.2 0.8 pad_maximum_fusion.1.own_ref
  45.1 6.1 %all-to-all-done.1.part_ref = bf16[8,32,112]{2,1,0:T(8,128)(2,1)S(1)} async-done(((bf16[8,32,112]{2,1,0:T(8,128)(2,1)}), bf16[8,32,112]{2,1,0:T(8,128)(2,1)S(1)}, u32[]{:S(2)}, u32[]{:S(2)}) %all-to-all-start.1) | async-done | bytes 57376 | tf_op jit(solution)/shard_map/all_to_all | solution.py:218
  51.1 1.0 shard_map.120
  52.2 2.3 %collective-permute-done.3.refs_3_.w3 = bf16[112,1792]{1,0:T(8,128)(2,1)S(1)} collective-permute-done((bf16[112,1792]{1,0:T(8,128)(2,1)S(1)}, bf16[112,1792]{1,0:T(8,128)(2,1)S(1)}, u32[]{:S(2)}, u32[]{:S(2)}) %collective-permute-start.3) | collective-permute-done | bytes 401440 | tf_op jit(solution)/shard_map/ppermute | solution.py:275
  54.4 7.7 %all-to-all-start.2 = ((bf16[32,32,128]{2,1,0:T(8,128)(2,1)}), bf16[32,32,128]{2,1,0:T(8,128)(2,1)S(1)}, u32[]{:S(2)}, u32[]{:S(2)}) async-start(bf16[32,32,128]{2,1,0:T(8,128)(2,1)} %get-tuple-element.39), calls=%async_computation.2 | async-start | bytes 524288 | tf_op jit(solution)/shard_map/all_to_all | solution.py:218
  62.1 1.9 %collective-permute-start.4 = (bf16[112,1792]{1,0:T(8,128)(2,1)S(1)}, bf16[112,1792]{1,0:T(8,128)(2,1)S(1)}, u32[]{:S(2)}, u32[]{:S(2)}) collective-permute-start(bf16[112,1792]{1,0:T(8,128)(2,1)S(1)} %get-tuple-element.40.refs_0_.w0), channel_id=1, source_target_pairs={{0,8},{8,0},{1,9},{9,1},{2,10},{10,2},{3,11},{11,3},{4,12},{12,4},... | collective-permute-start | bytes 1204232 | tf_op jit(solution)/shard_map/ppermute | solution.py:214
  64.1 2.4 %collective-permute-start.5 = (bf16[112,1792]{1,0:T(8,128)(2,1)S(1)}, bf16[112,1792]{1,0:T(8,128)(2,1)S(1)}, u32[]{:S(2)}, u32[]{:S(2)}) collective-permute-start(bf16[112,1792]{1,0:T(8,128)(2,1)S(1)} %collective-permute-done.1.refs_1_.w1), channel_id=1, source_target_pairs={{0,8},{8,0},{1,9},{9,1},{2,10},{10,2},{3,11},{11,3},{4,12},{12,4},... | collective-permute-start | bytes 1204232 | tf_op jit(solution)/shard_map/ppermute | solution.py:214
  66.5 1.9 %collective-permute-start.6 = (bf16[112,1792]{1,0:T(8,128)(2,1)S(1)}, bf16[112,1792]{1,0:T(8,128)(2,1)S(1)}, u32[]{:S(2)}, u32[]{:S(2)}) collective-permute-start(bf16[112,1792]{1,0:T(8,128)(2,1)S(1)} %collective-permute-done.2.refs_2_.w2), channel_id=1, source_target_pairs={{0,8},{8,0},{1,9},{9,1},{2,10},{10,2},{3,11},{11,3},{4,12},{12,4},... | collective-permute-start | bytes 1204232 | tf_op jit(solution)/shard_map/ppermute | solution.py:214
  68.4 2.4 %collective-permute-start.7 = (bf16[112,1792]{1,0:T(8,128)(2,1)S(1)}, bf16[112,1792]{1,0:T(8,128)(2,1)S(1)}, u32[]{:S(2)}, u32[]{:S(2)}) collective-permute-start(bf16[112,1792]{1,0:T(8,128)(2,1)S(1)} %collective-permute-done.3.refs_3_.w3), channel_id=1, source_target_pairs={{0,8},{8,0},{1,9},{9,1},{2,10},{10,2},{3,11},{11,3},{4,12},{12,4},... | collective-permute-start | bytes 1204232 | tf_op jit(solution)/shard_map/ppermute | solution.py:214
  70.8 0.0 collective-permute-done.4.refs_4_
  70.9 1.3 collective-permute-done.7.refs_7_
  72.2 0.8 copy-done.4
  72.9 0.7 all-to-all-done.2.full_ref
  73.7 1.0 copy-done.5
  74.7 0.6 shard_map.122
  75.3 19.6 %all_to_all.30.part_ref = bf16[8,16,1280]{2,1,0:T(8,128)(2,1)S(1)} all-to-all(bf16[8,16,1280]{2,1,0:T(8,128)(2,1)S(1)} %shard_map.122), channel_id=1, replica_groups=mesh['z'=8,'x'=4,'c'=2,'y'=8] {'z'}, dimensions={0} | all-to-all | bytes 655360 | tf_op jit(solution)/shard_map/all_to_all | solution.py:218
  94.8 0.9 shard_map.123
  95.7 3.4 %all-to-all-start.4 = ((bf16[8,16,576]{2,1,0:T(8,128)(2,1)}), bf16[8,16,576]{2,1,0:T(8,128)(2,1)S(1)}, u32[]{:S(2)}, u32[]{:S(2)}) async-start(bf16[8,16,576]{2,1,0:T(8,128)(2,1)} %shard_map.123), calls=%async_computation.4 | async-start | bytes 327680 | tf_op jit(solution)/shard_map/all_to_all | solution.py:218
  99.2 1.9 %collective-permute-start.9 = (f32[16,128]{1,0:T(8,128)S(1)}, f32[16,128]{1,0:T(8,128)S(1)}, u32[]{:S(2)}, u32[]{:S(2)}) collective-permute-start(f32[16,128]{1,0:T(8,128)S(1)} %slice.9), channel_id=1, source_target_pairs={{0,8},{8,0},{1,9},{9,1},{2,10},{10,2},{3,11},{11,3},{4,12},{12,4},... | collective-permute-start | bytes 24584 | tf_op jit(solution)/shard_map/ppermute | solution.py:214
  101.1 7.4 %all-to-all-done.4.own_ref = bf16[8,16,576]{2,1,0:T(8,128)(2,1)S(1)} async-done(((bf16[8,16,576]{2,1,0:T(8,128)(2,1)}), bf16[8,16,576]{2,1,0:T(8,128)(2,1)S(1)}, u32[]{:S(2)}, u32[]{:S(2)}) %all-to-all-start.4) | async-done | bytes 147488 | tf_op jit(solution)/shard_map/all_to_all | solution.py:218
  108.5 1.9 %collective-permute-start.8 = (bf16[8,16,576]{2,1,0:T(8,128)(2,1)S(1)}, bf16[8,16,576]{2,1,0:T(8,128)(2,1)S(1)}, u32[]{:S(2)}, u32[]{:S(2)}) collective-permute-start(bf16[8,16,576]{2,1,0:T(8,128)(2,1)S(1)} %all-to-all-done.4.own_ref), channel_id=1, source_target_pairs={{0,8},{8,0},{1,9},{9,1},{2,10},{10,2},{3,11},{11,3},{4,12},{12,4},... | collective-permute-start | bytes 442376 | tf_op jit(solution)/shard_map/ppermute | solution.py:214
  110.4 0.1 compare_convert_fusion.place_ref
  110.5 1.2 collective-permute-done.8.other_ref
  111.7 1.5 %shard_map.124 = bf16[32,32,112]{2,1,0:T(8,128)(2,1)S(1)} custom-call(s32[1]{0:T(128)} %bitcast.x_ref, s32[1]{0:T(128)} %bitcast.1.y_ref, bf16[8,16,576]{2,1,0:T(8,128)(2,1)S(1)} %all-to-all-done.4.own_ref, bf16[8,16,576]{2,1,0:T(8,128)(2,1)S(1)} %collective-permute-done.8.other_ref, bf16[112,1792]{1,0:T(8,128)(2,1)S(1)} %get-tuple-element.40.refs_0_.w0, ...), custom_call_target="tpu_custom_call" | custom-call | flops 200000000 | bytes 1600000 | tf_op jit(solution)/shard_map/pallas_call | solution.py:297
  113.2 22.4 %all_to_all.31 = bf16[32,32,112]{2,1,0:T(8,128)(2,1)S(1)} all-to-all(bf16[32,32,112]{2,1,0:T(8,128)(2,1)S(1)} %shard_map.124), channel_id=1, replica_groups=mesh['z'=8,'x'=4,'c'=2,'y'=8] {'x','y'}, dimensions={0} | all-to-all | bytes 458752 | tf_op jit(solution)/shard_map/all_to_all | solution.py:218
  135.6 0.7 reduce_sum.12
  (24 shorter events, 0.1 us)
Async XLA Ops:
  0.7 17.2 %copy-start.8 = (bf16[112]{0:T(256)(128)(2,1)S(1)}, bf16[112]{0:T(256)(128)(2,1)}, u32[]{:S(2)}) copy-start(bf16[112]{0:T(256)(128)(2,1)} %param.20) | copy-start | bytes 676
  4.5 13.5 %copy-start = (bf16[2048,112]{0,1:T(8,128)(2,1)S(1)}, bf16[2048,112]{0,1:T(8,128)(2,1)}, u32[]{:S(2)}) copy-start(bf16[2048,112]{0,1:T(8,128)(2,1)} %param.18) | copy-start | bytes 1376260
  4.5 13.5 %copy-start.7 = (bf16[256,112]{0,1:T(8,128)(2,1)S(1)}, bf16[256,112]{0,1:T(8,128)(2,1)}, u32[]{:S(2)}) copy-start(bf16[256,112]{0,1:T(8,128)(2,1)} %param.19) | copy-start | bytes 172036
  4.5 16.3 %copy-start.1 = (bf16[112,2304]{1,0:T(8,128)(2,1)S(1)}, bf16[112,2304]{1,0:T(8,128)(2,1)}, u32[]{:S(2)}) copy-start(bf16[112,2304]{1,0:T(8,128)(2,1)} %gate_ref) | copy-start | bytes 1548292
  4.5 16.3 %copy-start.2 = (bf16[112,2304]{1,0:T(8,128)(2,1)S(1)}, bf16[112,2304]{1,0:T(8,128)(2,1)}, u32[]{:S(2)}) copy-start(bf16[112,2304]{1,0:T(8,128)(2,1)} %up_ref) | copy-start | bytes 1548292
  4.5 31.0 %all-to-all-start = ((bf16[32,16,512]{2,1,0:T(8,128)(2,1)}), bf16[32,16,512]{2,1,0:T(8,128)(2,1)S(1)}, u32[]{:S(2)}, u32[]{:S(2)}) async-start(bf16[32,16,512]{2,1,0:T(8,128)(2,1)} %shard_map.118), calls=%async_computation | async-start | bytes 1048576 | tf_op jit(solution)/shard_map/all_to_all | solution.py:218
  17.9 2.8 %copy-start.6 = (bf16[112,128]{1,0:T(8,128)(2,1)}, bf16[112,128]{1,0:T(8,128)(2,1)S(1)}, u32[]{:S(2)}) copy-start(bf16[112,128]{1,0:T(8,128)(2,1)S(1)} %broadcast_in_dim.10) | copy-start | bytes 86020
  18.0 15.8 %copy-start.9 = (s32[64]{0:T(128)S(1)}, s32[64]{0:T(128)}, u32[]{:S(2)}) copy-start(s32[64]{0:T(128)} %param.16) | copy-start | bytes 772
  18.8 16.6 %collective-permute-start = (bf16[112,2432]{1,0:T(8,128)(2,1)}, bf16[112,2432]{1,0:T(8,128)(2,1)S(1)}, u32[]{:S(2)}, u32[]{:S(2)}) collective-permute-start(bf16[112,2432]{1,0:T(8,128)(2,1)} %pad_maximum_fusion), channel_id=1, source_target_pairs={{0,8},{8,0},{1,9},{9,1},{2,10},{10,2},{3,11},{11,3},{4,12},{12,4},... | collective-permute-start | bytes 1634312 | tf_op jit(solution)/shard_map/ppermute | solution.py:214
  20.8 1.0 copy-start.3
  23.3 28.8 %collective-permute-start.1 = (bf16[112,1792]{1,0:T(8,128)(2,1)}, bf16[112,1792]{1,0:T(8,128)(2,1)S(1)}, u32[]{:S(2)}, u32[]{:S(2)}) collective-permute-start(bf16[112,1792]{1,0:T(8,128)(2,1)} %get-tuple-element.36), channel_id=1, source_target_pairs={{0,16},{16,0},{32,48},{48,32},{1,17},{17,1},{33,49},{49,33},{2,18}... | collective-permute-start | bytes 1204232 | tf_op jit(solution)/shard_map/ppermute | solution.py:275
  27.0 25.1 %collective-permute-start.2 = (bf16[112,1792]{1,0:T(8,128)(2,1)}, bf16[112,1792]{1,0:T(8,128)(2,1)S(1)}, u32[]{:S(2)}, u32[]{:S(2)}) collective-permute-start(bf16[112,1792]{1,0:T(8,128)(2,1)} %get-tuple-element.37), channel_id=1, source_target_pairs={{0,32},{16,48},{32,0},{48,16},{1,33},{17,49},{33,1},{49,17},{2,34}... | collective-permute-start | bytes 1204232 | tf_op jit(solution)/shard_map/ppermute | solution.py:275
  31.6 22.8 %collective-permute-start.3 = (bf16[112,1792]{1,0:T(8,128)(2,1)S(1)}, bf16[112,1792]{1,0:T(8,128)(2,1)S(1)}, u32[]{:S(2)}, u32[]{:S(2)}) collective-permute-start(bf16[112,1792]{1,0:T(8,128)(2,1)S(1)} %get-tuple-element.38), channel_id=1, source_target_pairs={{0,48},{16,32},{32,16},{48,0},{1,49},{17,33},{33,17},{49,1},{2,50}... | collective-permute-start | bytes 1204232 | tf_op jit(solution)/shard_map/ppermute | solution.py:275
  36.7 14.5 %all-to-all-start.1 = ((bf16[8,32,112]{2,1,0:T(8,128)(2,1)}), bf16[8,32,112]{2,1,0:T(8,128)(2,1)S(1)}, u32[]{:S(2)}, u32[]{:S(2)}) async-start(bf16[8,32,112]{2,1,0:T(8,128)(2,1)} %shard_map.119), calls=%async_computation.1 | async-start | bytes 131072 | tf_op jit(solution)/shard_map/all_to_all | solution.py:218
  54.4 19.2 %all-to-all-start.2 = ((bf16[32,32,128]{2,1,0:T(8,128)(2,1)}), bf16[32,32,128]{2,1,0:T(8,128)(2,1)S(1)}, u32[]{:S(2)}, u32[]{:S(2)}) async-start(bf16[32,32,128]{2,1,0:T(8,128)(2,1)} %get-tuple-element.39), calls=%async_computation.2 | async-start | bytes 524288 | tf_op jit(solution)/shard_map/all_to_all | solution.py:218
  62.1 8.7 %collective-permute-start.4 = (bf16[112,1792]{1,0:T(8,128)(2,1)S(1)}, bf16[112,1792]{1,0:T(8,128)(2,1)S(1)}, u32[]{:S(2)}, u32[]{:S(2)}) collective-permute-start(bf16[112,1792]{1,0:T(8,128)(2,1)S(1)} %get-tuple-element.40.refs_0_.w0), channel_id=1, source_target_pairs={{0,8},{8,0},{1,9},{9,1},{2,10},{10,2},{3,11},{11,3},{4,12},{12,4},... | collective-permute-start | bytes 1204232 | tf_op jit(solution)/shard_map/ppermute | solution.py:214
  64.1 6.8 %collective-permute-start.5 = (bf16[112,1792]{1,0:T(8,128)(2,1)S(1)}, bf16[112,1792]{1,0:T(8,128)(2,1)S(1)}, u32[]{:S(2)}, u32[]{:S(2)}) collective-permute-start(bf16[112,1792]{1,0:T(8,128)(2,1)S(1)} %collective-permute-done.1.refs_1_.w1), channel_id=1, source_target_pairs={{0,8},{8,0},{1,9},{9,1},{2,10},{10,2},{3,11},{11,3},{4,12},{12,4},... | collective-permute-start | bytes 1204232 | tf_op jit(solution)/shard_map/ppermute | solution.py:214
  66.5 4.4 %collective-permute-start.6 = (bf16[112,1792]{1,0:T(8,128)(2,1)S(1)}, bf16[112,1792]{1,0:T(8,128)(2,1)S(1)}, u32[]{:S(2)}, u32[]{:S(2)}) collective-permute-start(bf16[112,1792]{1,0:T(8,128)(2,1)S(1)} %collective-permute-done.2.refs_2_.w2), channel_id=1, source_target_pairs={{0,8},{8,0},{1,9},{9,1},{2,10},{10,2},{3,11},{11,3},{4,12},{12,4},... | collective-permute-start | bytes 1204232 | tf_op jit(solution)/shard_map/ppermute | solution.py:214
  68.4 3.8 %collective-permute-start.7 = (bf16[112,1792]{1,0:T(8,128)(2,1)S(1)}, bf16[112,1792]{1,0:T(8,128)(2,1)S(1)}, u32[]{:S(2)}, u32[]{:S(2)}) collective-permute-start(bf16[112,1792]{1,0:T(8,128)(2,1)S(1)} %collective-permute-done.3.refs_3_.w3), channel_id=1, source_target_pairs={{0,8},{8,0},{1,9},{9,1},{2,10},{10,2},{3,11},{11,3},{4,12},{12,4},... | collective-permute-start | bytes 1204232 | tf_op jit(solution)/shard_map/ppermute | solution.py:214
  72.2 0.8 copy-start.4
  73.7 1.0 copy-start.5
  95.7 12.7 %all-to-all-start.4 = ((bf16[8,16,576]{2,1,0:T(8,128)(2,1)}), bf16[8,16,576]{2,1,0:T(8,128)(2,1)S(1)}, u32[]{:S(2)}, u32[]{:S(2)}) async-start(bf16[8,16,576]{2,1,0:T(8,128)(2,1)} %shard_map.123), calls=%async_computation.4 | async-start | bytes 327680 | tf_op jit(solution)/shard_map/all_to_all | solution.py:218
  99.2 11.3 %collective-permute-start.9 = (f32[16,128]{1,0:T(8,128)S(1)}, f32[16,128]{1,0:T(8,128)S(1)}, u32[]{:S(2)}, u32[]{:S(2)}) collective-permute-start(f32[16,128]{1,0:T(8,128)S(1)} %slice.9), channel_id=1, source_target_pairs={{0,8},{8,0},{1,9},{9,1},{2,10},{10,2},{3,11},{11,3},{4,12},{12,4},... | collective-permute-start | bytes 24584 | tf_op jit(solution)/shard_map/ppermute | solution.py:214
  108.5 3.3 %collective-permute-start.8 = (bf16[8,16,576]{2,1,0:T(8,128)(2,1)S(1)}, bf16[8,16,576]{2,1,0:T(8,128)(2,1)S(1)}, u32[]{:S(2)}, u32[]{:S(2)}) collective-permute-start(bf16[8,16,576]{2,1,0:T(8,128)(2,1)S(1)} %all-to-all-done.4.own_ref), channel_id=1, source_target_pairs={{0,8},{8,0},{1,9},{9,1},{2,10},{10,2},{3,11},{11,3},{4,12},{12,4},... | collective-permute-start | bytes 442376 | tf_op jit(solution)/shard_map/ppermute | solution.py:214

commit v4 on v3

--- a/solution.py
+++ b/solution.py
@@ -9,14 +9,13 @@
 D = 7168
 WIDTH = 112
 SIZE = 576
-
-PACK = 14 * 128
+DOWN = 5 * 128
 
 score_scale = 192.0 ** (-0.5)
 norm_eps = 1e-06
 
-AXES = ("z", "x", "c", "y")
-DP = ("z", "x", "c")
+AXES = ("z", "xh", "xl", "c", "y")
+DP = ("z", "xh", "xl", "c")
 BF = jnp.bfloat16
 F32 = jnp.float32
 VMEM = pl.BlockSpec(memory_space=pltpu.VMEM)
@@ -86,17 +85,46 @@
         out_ref[i] = block
 
 
-def pack_kernel(x_ref, gate_ref, up_ref, down_ref, *outs):
-    pad = jnp.zeros((WIDTH, PACK - 3 * SIZE), BF)
-    for r, out_ref in enumerate(outs):
-        for q in range(4):
-
-            @pl.when((x_ref[0] ^ r) == q)
-            def _(out_ref=out_ref, q=q):
-                cut = slice(q * SIZE, (q + 1) * SIZE)
-                out_ref[...] = jnp.concatenate(
-                    [gate_ref[:, cut], up_ref[:, cut], down_ref[:, cut], pad], axis=1
-                )
+def pack_kernel(xh_ref, xl_ref, gate_ref, up_ref, down_ref, ff0, ff1, ff2, ff3, fd_ref, send_fd_ref):
+    cuts = [slice(i * SIZE, (i + 1) * SIZE) for i in range(4)]
+    pad = jnp.zeros((WIDTH, DOWN - SIZE), BF)
+    for i, cut in enumerate(cuts):
+        block = jnp.concatenate([gate_ref[:, cut], up_ref[:, cut]], axis=1)
+        for r, out_ref in enumerate((ff0, ff1, ff2, ff3)):
+            target = 2 * (xl_ref[0] ^ (r & 1)) + (xh_ref[0] ^ (r >> 1))
+
+            @pl.when(target == i)
+            def _(out_ref=out_ref, block=block):
+                out_ref[...] = block
+
+    for half in range(2):
+        both = [down_ref[:, cuts[2 * half]], pad, down_ref[:, cuts[2 * half + 1]], pad]
+        both = jnp.concatenate(both, axis=1)
+
+        @pl.when(xl_ref[0] == half)
+        def _(both=both):
+            fd_ref[...] = both
+
+        @pl.when(xl_ref[0] != half)
+        def _(both=both):
+            send_fd_ref[...] = both
+
+
+def rows_kernel(core_ref, y_ref, slot_ref, pick_ref, place_ref):
+    iota = lambda dims, axis: lax.broadcasted_iota(jnp.int32, dims, axis)
+    slot = slot_ref[...].astype(F32)
+    col = iota((256, 256), 1)
+    core = jnp.where(col < 128, core_ref[0], 1 - core_ref[0])
+    held = (col & 31) * 8 + core * 4 + ((col >> 5) & 3)
+    spread = (iota((256, 64), 0) >> 2) == iota((256, 64), 1)
+    of_row = jnp.sum(jnp.where(spread, slot, 0.0), axis=1, keepdims=True).astype(jnp.int32)
+    place = (of_row * 4 + (iota((256, 256), 0) & 3)) == held
+    place_ref[...] = jnp.where(place, 1.0, 0.0).astype(BF)
+    across = jnp.where((iota((64, 256), 1) >> 2) == iota((64, 256), 0), 1.0, 0.0).astype(BF)
+    of_col = dot(jnp.broadcast_to(slot, (16, 64)).astype(BF), across).astype(jnp.int32)
+    own = iota((16, 256), 0) + y_ref[0] * 16
+    held = (own & 31) * 8 + core_ref[0] * 4 + (own >> 5)
+    pick_ref[...] = jnp.where(of_col * 4 + (iota((16, 256), 1) & 3) == held, 1.0, 0.0).astype(BF)
 
 
 def out_kernel(x_ref, own_ref, other_ref, out_ref, wide):
@@ -117,14 +145,15 @@
     total = total.astype(BF)
     for y in range(8):
         part = total[y * 16 : y * 16 + 16]
-        out_ref[y, 0:16, :] = part[:, :WIDTH]
-        out_ref[y, 16:32, :] = part[:, 128 : 128 + WIDTH]
+        out_ref[y, 0:16, :] = part[:, :128]
+        out_ref[y, 16:32, :] = part[:, 128:]
 
 
 def norm_kernel(part_ref, pick_ref, own_ref, other_ref, out_ref, hidden_ref):
     attended = part_ref[0].astype(F32)
     for i in range(1, 8):
         attended = attended + part_ref[i].astype(F32)
+    attended = attended[:, :WIDTH]
     nt = (((1,), (1,)), ((), ()))
     pick = pick_ref[...]
     unit = (lax.broadcasted_iota(jnp.int32, (16, 128), 1) == 0).astype(F32).astype(BF)
@@ -134,40 +163,39 @@
     gain = jnp.concatenate([gains(own_ref), gains(other_ref)], axis=0)
     squares = jnp.sum(hidden * hidden, axis=1, keepdims=True)
     squares = squares[0:16] + squares[16:32]
-    high = squares.astype(BF).astype(F32)
-    low = squares - high
     none = jnp.zeros((32, 128 - WIDTH), F32)
     scaled = jnp.concatenate([hidden * gain, none], axis=1)
     lane = lax.broadcasted_iota(jnp.int32, (32, 128), 1)
     first = lax.broadcasted_iota(jnp.int32, (32, 128), 0) < 16
+    high = squares.astype(BF).astype(F32)
     twice = lambda a: jnp.concatenate([a, a], axis=0)
     scaled = jnp.where(first & (lane == WIDTH), twice(high), scaled)
-    scaled = jnp.where(first & (lane == WIDTH + 1), twice(low), scaled).astype(BF)
+    scaled = jnp.where(first & (lane == WIDTH + 1), twice(squares - high), scaled).astype(BF)
     hidden_ref[...] = jnp.concatenate([hidden, none], axis=1)
     for i in range(32):
         out_ref[i] = scaled
 
 
-def gate_kernel(x_ref, full_ref, *refs):
+def gate_kernel(xh_ref, xl_ref, full_ref, *refs):
     own_refs, other_refs, out_ref = refs[:4], refs[4:8], refs[8]
     lane = lax.broadcasted_iota(jnp.int32, (128, 128), 1)
     valid = lane < WIDTH
     none = jnp.zeros((128 - WIDTH, 384), BF)
+    zero = jnp.zeros((128, 128), BF)
     held, squares = [], jnp.zeros((128, 1), F32)
     for r in range(4):
-        block = full_ref[pl.ds((x_ref[0] ^ r) * 8, 8)]
+        x = 2 * (xh_ref[0] ^ (r >> 1)) + (xl_ref[0] ^ (r & 1))
+        block = full_ref[pl.ds(x * 8, 8)]
         own = block[:, 0:16, :].reshape(128, 128)
         other = block[:, 16:32, :].reshape(128, 128)
-        sums = jnp.where((lane >= WIDTH) & (lane < WIDTH + 2), own.astype(F32), 0.0)
+        sums = jnp.where((lane == WIDTH) | (lane == WIDTH + 1), own.astype(F32), 0.0)
         squares = squares + jnp.sum(sums, axis=1, keepdims=True)
-        zero = jnp.zeros((128, 128), BF)
-        held.append(
-            jnp.concatenate([jnp.where(valid, own, zero), jnp.where(valid, other, zero)], axis=1)
-        )
-    for n in range(0, 1152, 384):
+        both = [jnp.where(valid, own, zero), jnp.where(valid, other, zero)]
+        held.append(jnp.concatenate(both, axis=1))
+    for n in range(0, 2 * SIZE, 384):
         total = jnp.zeros((128, 384), F32)
-        for r, w in enumerate(own_refs):
-            both = [w[:, n : n + 384], none, other_refs[r][:, n : n + 384], none]
+        for r in range(4):
+            both = [own_refs[r][:, n : n + 384], none, other_refs[r][:, n : n + 384], none]
             total = total + dot(held[r], jnp.concatenate(both, axis=0))
         out_ref[:, :, n : n + 384] = total.astype(BF).reshape(8, 16, 384)
     high = squares.astype(BF).astype(F32)
@@ -184,22 +212,28 @@
     gate = total[:, :SIZE] * factor
     up = total[:, SIZE : 2 * SIZE] * factor
     units = (gate * jax.nn.sigmoid(gate) * up).astype(BF)
-    for i in range(8):
+    for i in range(16):
         out_ref[i] = units
 
 
 def down_kernel(
-    x_ref, y_ref, own_ref, other_ref, w0, w1, w2, w3, hidden_ref, across_ref, place_ref, out_ref, total
+    xl_ref, y_ref, own_ref, other_ref, w0, w1, hidden_ref, across_ref, place_ref, out_ref, total
 ):
-    units = jnp.concatenate(
-        [own_ref[...].reshape(128, SIZE), other_ref[...].reshape(128, SIZE)], axis=0
-    )
+    units = [
+        jnp.concatenate(
+            [own_ref[:, i].reshape(128, SIZE), other_ref[:, i].reshape(128, SIZE)], axis=0
+        )
+        for i in range(2)
+    ]
     place = place_ref[...]
     none = jnp.zeros((128 - WIDTH, SIZE), BF)
-    for r, w in enumerate((w0, w1, w2, w3)):
-        part = lax.dot_general(
-            units, jnp.concatenate([w[:, 2 * SIZE : 3 * SIZE], none], axis=0), (((1,), (1,)), ((), ())), preferred_element_type=F32
-        )
+    nt = (((1,), (1,)), ((), ()))
+    for r, w in enumerate((w0, w1)):
+        part = jnp.zeros((256, 128), F32)
+        for i in range(2):
+            at = i * DOWN
+            wide = jnp.concatenate([w[:, at : at + SIZE], none], axis=0)
+            part = part + lax.dot_general(units[i], wide, nt, preferred_element_type=F32)
         if r == 0:
             total[...] = part
             at = pl.multiple_of(y_ref[0] * 16, 16)
@@ -207,7 +241,7 @@
             total[pl.ds(128 + at, 16), :] += across_ref[...]
             part = total[...]
         rows = dot(place, part.astype(BF)).astype(BF)
-        out_ref[pl.ds((x_ref[0] ^ r) * 8, 8)] = rows[:, :WIDTH].reshape(8, 32, WIDTH)
+        out_ref[pl.ds((xl_ref[0] ^ r) * 8, 8)] = rows.reshape(8, 32, 128)
 
 
 def swap(value, axis="c"):
@@ -232,8 +266,7 @@
     w_up,
     w_down,
 ):
-    x, core, tp = lax.axis_index("x"), lax.axis_index("c"), lax.axis_index("y")
-    xs, ys = x[None].astype(jnp.int32), tp[None].astype(jnp.int32)
+    xh, xl, core, tp = (lax.axis_index(a)[None].astype(jnp.int32) for a in ("xh", "xl", "c", "y"))
 
     blocks = call(
         attention_kernel,
@@ -254,59 +287,76 @@
     blocks, out_proj, slot_of, residual, norm_gain, w_gate, w_up, w_down = lax.optimization_barrier(
         (blocks, out_proj.T, slot_of, residual.T, norm_gain, w_gate, w_up, w_down.T)
     )
-    rows = exchange(blocks, ("z", "x"))
+    rows = exchange(blocks, ("z", "xh", "xl"))
     gains = jnp.broadcast_to(norm_gain[:, None], (WIDTH, 128))
     carry = jnp.concatenate([out_proj, residual, gains], axis=1)
     carry_other = swap(carry)
     tail, tail_other = carry[:, 2048:], carry_other[:, 2048:]
 
-    ids = jnp.arange(128, dtype=jnp.int32)
-    request_rows = jnp.repeat(slot_of, 4) * 4 + jnp.arange(256, dtype=jnp.int32) % 4
-    held_rows = lambda of_core, own: (own % 32) * 8 + of_core * 4 + own // 32
-    part_ids = tp * 16 + jnp.arange(16, dtype=jnp.int32)
-    pick = (held_rows(core, part_ids)[:, None] == request_rows[None, :]).astype(BF)
-    both_rows = jnp.concatenate([held_rows(core, ids), held_rows(1 - core, ids)])
-    place = (request_rows[:, None] == both_rows[None, :]).astype(BF)
-
-    packed = call(
-        pack_kernel, [SMEM, VMEM, VMEM, VMEM], [shape((WIDTH, PACK))] * 4, (), 0, 3_200_000
-    )(xs, w_gate, w_up, w_down)
-    weights = [packed[0]] + [
-        lax.ppermute(packed[r], "x", [(i, i ^ r) for i in range(4)]) for r in (1, 2, 3)
+    *ff, down_own, down_sent = call(
+        pack_kernel,
+        [SMEM, SMEM, VMEM, VMEM, VMEM],
+        [shape((WIDTH, 2 * SIZE))] * 4 + [shape((WIDTH, 2 * DOWN))] * 2,
+        (),
+        0,
+        3_200_000,
+    )(xh, xl, w_gate, w_up, w_down)
+    ff = [
+        ff[0],
+        swap(ff[1], "xl"),
+        swap(ff[2], "xh"),
+        lax.ppermute(ff[3], ("xh", "xl"), [(i, 3 - i) for i in range(4)]),
     ]
+    rows, ff[0] = lax.optimization_barrier((rows, ff[0]))
     part = call(
         out_kernel,
         [VMEM] * 3,
-        shape((8, 32, WIDTH)),
+        shape((8, 32, 128)),
         [pltpu.VMEM((4, 512, 128), F32)],
-        300_000_000,
-        1_600_000,
+        1_000_000,
+        100_000,
     )(rows, out_proj, carry_other)
+    pick, place = call(
+        rows_kernel, [SMEM, SMEM, VMEM], [shape((16, 256)), shape((256, 256))], (), 0, 200_000
+    )(core, tp, slot_of[None])
+    part, *ff = lax.optimization_barrier((exchange(part, "y"), *ff))
     scaled, hidden = call(
         norm_kernel, [VMEM] * 4, [shape((32, 32, 128)), shape((32, 128), F32)], (), 0, 400_000
-    )(exchange(part, "y"), pick, tail, tail_other)
-    scaled, *weights = lax.optimization_barrier((scaled, *weights))
-    others = [swap(w) for w in weights]
+    )(part, pick, tail, tail_other)
+    hidden, *ff = lax.optimization_barrier((hidden, *ff))
+    ff_other = [swap(w) for w in ff]
     part = call(
-        gate_kernel, [SMEM] + [VMEM] * 9, shape((8, 16, 1280)), (), 300_000_000, 2_800_000
-    )(xs, exchange(scaled, ("x", "y")), *weights, *others)
-    units = call(units_kernel, [VMEM], shape((8, 16, SIZE)), (), 0, 500_000)(exchange(part, "z"))
-    units, hidden = lax.optimization_barrier((units, hidden))
-    across = swap(hidden[16:])
-    units = exchange(units, "z")
+        gate_kernel, [SMEM] * 2 + [VMEM] * 9, shape((8, 16, 1280)), (), 300_000_000, 2_800_000
+    )(xh, xl, exchange(scaled, ("xh", "xl", "y")), *ff, *ff_other)
+    _, hidden, down_sent = lax.optimization_barrier((part, hidden, down_sent))
+    part, across, down_near = lax.optimization_barrier(
+        (exchange(part, "z"), swap(hidden[16:]), swap(down_sent, "xl"))
+    )
+    units = call(units_kernel, [VMEM], shape((16, 16, SIZE)), (), 0, 500_000)(part)
+    units = exchange(units, ("z", "xh"))
     part = call(
         down_kernel,
-        [SMEM] * 2 + [VMEM] * 9,
-        shape((32, 32, WIDTH)),
+        [SMEM] * 2 + [VMEM] * 7,
+        shape((16, 32, 128)),
         [pltpu.VMEM((256, 128), F32)],
         200_000_000,
         1_600_000,
-    )(xs, ys, units, swap(units), *weights, hidden, across, place)
-    return jnp.sum(exchange(part, ("x", "y")).astype(F32), axis=0).astype(BF)
+    )(
+        xl,
+        tp,
+        units.reshape(8, 2, 16, SIZE),
+        swap(units).reshape(8, 2, 16, SIZE),
+        down_own,
+        down_near,
+        hidden,
+        across,
+        place,
+    )
+    return jnp.sum(exchange(part, ("xl", "y"))[:, :, :WIDTH].astype(F32), axis=0).astype(BF)
 
 
 def solution(mesh):
-    fine = Mesh(mesh.devices.reshape(8, 4, 2, 8), AXES)
+    fine = Mesh(mesh.devices.reshape(8, 2, 2, 2, 8), AXES)
     specs = (
         P(DP, None, "y", None),
         P(DP, None, None),

time: 137 us -> 131 us (0.956)
  blocking collectives: 41.9 us -> 34.8 us
  starting transfers between devices: 56.7 us -> 60.3 us
  local copies, waits for them, and re-layouts: 4.46 us -> 1.53 us
    ppermute x7 -> x10, starting transfers between devices: 14.4 us -> 25.4 us  [swap(): return lax.ppermute(value, axis, [(0, 1), (1, 0)])]
    ppermute x3 -> x1, starting transfers between devices: 10.4 us -> 2.13 us  [local(): lax.ppermute(ff[3], ('xh', 'xl'), [(i, 3 - i) for i in range(4)])]
    all_to_all x2, blocking collectives: 41.9 us -> 34.8 us  [exchange(): return lax.all_to_all(blocks, axes, 0, 0, tiled=True)]
    all_to_all x4, waiting for transfers between devices: 14.2 us -> 8.41 us  [exchange(): return lax.all_to_all(blocks, axes, 0, 0, tiled=True)]
    ppermute x7 -> x10, waiting for transfers between devices: 2.56 us -> 7.25 us  [swap(): return lax.ppermute(value, axis, [(0, 1), (1, 0)])]
    ppermute x3 -> x1, waiting for transfers between devices: 2.28 us -> 4.77 us  [local(): lax.ppermute(ff[3], ('xh', 'xl'), [(i, 3 - i) for i in range(4)])]
    unnamed x20 -> x22, local copies, waits for them, and re-layouts: 2.83 us -> 1.44 us
    pallas_call x5 -> x6, Pallas kernels: 5.63 us -> 5.45 us  [the longest x1 1.71 us: local(): call(pack_kernel, [SMEM, SMEM, VMEM, VMEM, VMEM], [shape((WIDTH, 2 * SIZE...]
  transfers between devices with their start and end apart: 14 -> 15, of which waited for: 7 -> 9; matrix products, arithmetic and copies ran while one was open for 3% -> 1% of each run, Pallas kernels for 3% -> 2%
where the time goes in v4:
time: 131 us; the launch traced here: 130 us
  starting transfers between devices  60.3 us (46%)
  blocking collectives  34.8 us (27%)
  waiting for transfers between devices  20.4 us (16%)
  Pallas kernels  10.3 us (8%)
  local copies, waits for them, and re-layouts  1.53 us (1%)
  other arithmetic  1.51 us (1%)
    all_to_all x2, blocking collectives, exchange(): return lax.all_to_all(blocks, axes, 0, 0, tiled=True)  34.8 us
    all_to_all x4, starting transfers between devices, exchange(): return lax.all_to_all(blocks, axes, 0, 0, tiled=True)  32.7 us
    ppermute x10, starting transfers between devices, swap(): return lax.ppermute(value, axis, [(0, 1), (1, 0)])  25.4 us
    all_to_all x4, waiting for transfers between devices, exchange(): return lax.all_to_all(blocks, axes, 0, 0, tiled=True)  8.41 us
    ppermute x10, waiting for transfers between devices, swap(): return lax.ppermute(value, axis, [(0, 1), (1, 0)])  7.25 us
    ppermute x1, waiting for transfers between devices, local(): lax.ppermute(ff[3], ('xh', 'xl'), [(i, 3 - i) for i in range(4)])  4.77 us
    pallas_call x1, Pallas kernels, local(): call(attention_kernel, [SMEM, HBM, VMEM, HBM, HBM], shape((32, 16, 512)),...  3.8 us
  transfers between devices with their start and end apart: 15, of which 9 were waited for; matrix products, arithmetic and copies ran while one was open for 1% of the time, Pallas kernels for 2%

profile of v4, /device:TPU:8, one launch (start us, length us, event | category | flops | bytes accessed | tf_op | source)
XLA Modules:
  0.0 129.8 jit_solution(1070815021674587865)
XLA Ops:
  0.7 3.8 %shard_map.118 = bf16[32,16,512]{2,1,0:T(8,128)(2,1)} custom-call(s32[1]{0:T(128)S(6)} %copy.13.len_ref, bf16[64,576]{1,0:T(8,128)(2,1)} %bitcast.24, bf16[4,576]{1,0:T(4,128)(2,1)} %bitcast.25, bf16[576,512]{1,0:T(8,128)(2,1)} %bitcast.21, bf16[16,512,128]{2,1,0:T(8,128)(2,1)} %maps_ref.1), custom_call_target="tpu_custom_call" | custom-call | flops 200000000 | bytes 4000000 | tf_op jit(solution)/shard_map/pallas_call | solution.py:271
  4.5 0.0 copy-start
  4.5 0.0 copy-start.9
  4.5 0.0 copy-start.1
  4.5 0.0 copy-start.2
  4.5 0.0 copy-start.3
  4.5 13.3 %all-to-all-start = ((bf16[32,16,512]{2,1,0:T(8,128)(2,1)}), bf16[32,16,512]{2,1,0:T(8,128)(2,1)S(1)}, u32[]{:S(2)}, u32[]{:S(2)}) async-start(bf16[32,16,512]{2,1,0:T(8,128)(2,1)} %shard_map.118), calls=%async_computation | async-start | bytes 1048576 | tf_op jit(solution)/shard_map/all_to_all | solution.py:252
  17.9 0.1 broadcast_in_dim.24
  18.0 0.9 pad_maximum_fusion
  18.8 1.9 %collective-permute-start = (bf16[112,2432]{1,0:T(8,128)(2,1)}, bf16[112,2432]{1,0:T(8,128)(2,1)S(1)}, u32[]{:S(2)}, u32[]{:S(2)}) collective-permute-start(bf16[112,2432]{1,0:T(8,128)(2,1)} %pad_maximum_fusion), channel_id=1, source_target_pairs={{0,8},{8,0},{1,9},{9,1},{2,10},{10,2},{3,11},{11,3},{4,12},{12,4},... | collective-permute-start | bytes 1634312 | tf_op jit(solution)/shard_map/ppermute | solution.py:248
  20.8 1.7 %shard_map.119 = (bf16[112,1152]{1,0:T(8,128)(2,1)S(1)}, bf16[112,1152]{1,0:T(8,128)(2,1)}, bf16[112,1152]{1,0:T(8,128)(2,1)}, bf16[112,1152]{1,0:T(8,128)(2,1)}...) custom-call(s32[1]{0:T(128)} %bitcast.2.xh_ref, s32[1]{0:T(128)} %bitcast.xl_ref, ...), custom_call_target="tpu_custom_call" | custom-call | bytes 3200000 | tf_op jit(solution)/shard_map/pallas_call | solution.py:296
  22.5 0.7 copy-done.4
  23.2 0.7 copy-done.6
  23.9 3.8 %collective-permute-start.1 = (bf16[112,1152]{1,0:T(8,128)(2,1)}, bf16[112,1152]{1,0:T(8,128)(2,1)S(1)}, u32[]{:S(2)}, u32[]{:S(2)}) collective-permute-start(bf16[112,1152]{1,0:T(8,128)(2,1)} %get-tuple-element.50), channel_id=1, source_target_pairs={{0,16},{16,0},{1,17},{17,1},{2,18},{18,2},{3,19},{19,3},{4,20},{20... | collective-permute-start | bytes 774152 | tf_op jit(solution)/shard_map/ppermute | solution.py:248
  27.7 4.6 %collective-permute-start.2 = (bf16[112,1152]{1,0:T(8,128)(2,1)}, bf16[112,1152]{1,0:T(8,128)(2,1)S(1)}, u32[]{:S(2)}, u32[]{:S(2)}) collective-permute-start(bf16[112,1152]{1,0:T(8,128)(2,1)} %get-tuple-element.51), channel_id=1, source_target_pairs={{0,32},{32,0},{1,33},{33,1},{2,34},{34,2},{3,35},{35,3},{4,36},{36... | collective-permute-start | bytes 774152 | tf_op jit(solution)/shard_map/ppermute | solution.py:248
  32.3 2.1 %collective-permute-start.3 = (bf16[112,1152]{1,0:T(8,128)(2,1)}, bf16[112,1152]{1,0:T(8,128)(2,1)S(1)}, u32[]{:S(2)}, u32[]{:S(2)}) collective-permute-start(bf16[112,1152]{1,0:T(8,128)(2,1)} %get-tuple-element.52), channel_id=1, source_target_pairs={{0,48},{16,32},{32,16},{48,0},{1,49},{17,33},{33,17},{49,1},{2,50}... | collective-permute-start | bytes 774152 | tf_op jit(solution)/shard_map/ppermute | solution.py:308
  34.5 1.1 all-to-all-done.x_ref
  35.6 0.0 collective-permute-done.other_ref
  35.6 1.1 shard_map.120
  36.7 7.6 %all-to-all-start.1 = ((bf16[8,32,128]{2,1,0:T(8,128)(2,1)}), bf16[8,32,128]{2,1,0:T(8,128)(2,1)S(1)}, u32[]{:S(2)}, u32[]{:S(2)}) async-start(bf16[8,32,128]{2,1,0:T(8,128)(2,1)} %shard_map.120), calls=%async_computation.1 | async-start | bytes 131072 | tf_op jit(solution)/shard_map/all_to_all | solution.py:252
  44.3 0.1 shard_map.121
  44.4 0.0 collective-permute-done.1.refs_1_
  44.4 0.0 collective-permute-done.2.refs_2_
  44.5 4.8 %collective-permute-done.3.refs_3_ = bf16[112,1152]{1,0:T(8,128)(2,1)S(1)} collective-permute-done((bf16[112,1152]{1,0:T(8,128)(2,1)}, bf16[112,1152]{1,0:T(8,128)(2,1)S(1)}, u32[]{:S(2)}, u32[]{:S(2)}) %collective-permute-start.3) | collective-permute-done | bytes 258080 | tf_op jit(solution)/shard_map/ppermute | solution.py:308
  49.2 1.9 %all-to-all-done.1.part_ref = bf16[8,32,128]{2,1,0:T(8,128)(2,1)S(1)} async-done(((bf16[8,32,128]{2,1,0:T(8,128)(2,1)}), bf16[8,32,128]{2,1,0:T(8,128)(2,1)S(1)}, u32[]{:S(2)}, u32[]{:S(2)}) %all-to-all-start.1) | async-done | bytes 65568 | tf_op jit(solution)/shard_map/all_to_all | solution.py:252
  51.2 1.0 shard_map.122
  52.2 5.8 %all-to-all-start.2 = ((bf16[32,32,128]{2,1,0:T(8,128)(2,1)}), bf16[32,32,128]{2,1,0:T(8,128)(2,1)S(1)}, u32[]{:S(2)}, u32[]{:S(2)}) async-start(bf16[32,32,128]{2,1,0:T(8,128)(2,1)} %get-tuple-element.56), calls=%async_computation.2 | async-start | bytes 524288 | tf_op jit(solution)/shard_map/all_to_all | solution.py:252
  58.0 2.1 %collective-permute-start.4 = (bf16[112,1152]{1,0:T(8,128)(2,1)S(1)}, bf16[112,1152]{1,0:T(8,128)(2,1)S(1)}, u32[]{:S(2)}, u32[]{:S(2)}) collective-permute-start(bf16[112,1152]{1,0:T(8,128)(2,1)S(1)} %copy-done.5), channel_id=1, source_target_pairs={{0,8},{8,0},{1,9},{9,1},{2,10},{10,2},{3,11},{11,3},{4,12},{12,4},... | collective-permute-start | bytes 774152 | tf_op jit(solution)/shard_map/ppermute | solution.py:248
  60.0 2.4 %collective-permute-start.5 = (bf16[112,1152]{1,0:T(8,128)(2,1)S(1)}, bf16[112,1152]{1,0:T(8,128)(2,1)S(1)}, u32[]{:S(2)}, u32[]{:S(2)}) collective-permute-start(bf16[112,1152]{1,0:T(8,128)(2,1)S(1)} %collective-permute-done.1.refs_1_), channel_id=1, source_target_pairs={{0,8},{8,0},{1,9},{9,1},{2,10},{10,2},{3,11},{11,3},{4,12},{12,4},... | collective-permute-start | bytes 774152 | tf_op jit(solution)/shard_map/ppermute | solution.py:248
  62.4 1.9 %collective-permute-start.6 = (bf16[112,1152]{1,0:T(8,128)(2,1)S(1)}, bf16[112,1152]{1,0:T(8,128)(2,1)S(1)}, u32[]{:S(2)}, u32[]{:S(2)}) collective-permute-start(bf16[112,1152]{1,0:T(8,128)(2,1)S(1)} %collective-permute-done.2.refs_2_), channel_id=1, source_target_pairs={{0,8},{8,0},{1,9},{9,1},{2,10},{10,2},{3,11},{11,3},{4,12},{12,4},... | collective-permute-start | bytes 774152 | tf_op jit(solution)/shard_map/ppermute | solution.py:248
  64.4 2.4 %collective-permute-start.7 = (bf16[112,1152]{1,0:T(8,128)(2,1)S(1)}, bf16[112,1152]{1,0:T(8,128)(2,1)S(1)}, u32[]{:S(2)}, u32[]{:S(2)}) collective-permute-start(bf16[112,1152]{1,0:T(8,128)(2,1)S(1)} %collective-permute-done.3.refs_3_), channel_id=1, source_target_pairs={{0,8},{8,0},{1,9},{9,1},{2,10},{10,2},{3,11},{11,3},{4,12},{12,4},... | collective-permute-start | bytes 774152 | tf_op jit(solution)/shard_map/ppermute | solution.py:248
  66.8 0.0 collective-permute-done.5.refs_5_
  66.8 1.1 collective-permute-done.7.refs_7_
  67.9 2.3 %all-to-all-done.2.full_ref = bf16[32,32,128]{2,1,0:T(8,128)(2,1)S(1)} async-done(((bf16[32,32,128]{2,1,0:T(8,128)(2,1)}), bf16[32,32,128]{2,1,0:T(8,128)(2,1)S(1)}, u32[]{:S(2)}, u32[]{:S(2)}) %all-to-all-start.2) | async-done | bytes 262176 | tf_op jit(solution)/shard_map/all_to_all | solution.py:252
  70.2 1.3 %shard_map.123 = bf16[8,16,1280]{2,1,0:T(8,128)(2,1)} custom-call(s32[1]{0:T(128)} %bitcast.2.xh_ref, s32[1]{0:T(128)} %bitcast.xl_ref, bf16[32,32,128]{2,1,0:T(8,128)(2,1)S(1)} %all-to-all-done.2.full_ref, bf16[112,1152]{1,0:T(8,128)(2,1)S(1)} %copy-done.5, bf16[112,1152]{1,0:T(8,128)(2,1)S(1)} %collective-permute-done.1.refs_1_, ...), custom_call_target="tpu_custom_call" | custom-call | flops 300000000 | bytes 2800000 | tf_op jit(solution)/shard_map/pallas_call | solution.py:328
  71.5 6.1 %all-to-all-start.3 = ((bf16[8,16,1280]{2,1,0:T(8,128)(2,1)}), bf16[8,16,1280]{2,1,0:T(8,128)(2,1)S(1)}, u32[]{:S(2)}, u32[]{:S(2)}) async-start(bf16[8,16,1280]{2,1,0:T(8,128)(2,1)} %shard_map.123), calls=%async_computation.3 | async-start | bytes 655360 | tf_op jit(solution)/shard_map/all_to_all | solution.py:252
  77.6 2.5 %collective-permute-start.9 = (bf16[112,1280]{1,0:T(8,128)(2,1)S(1)}, bf16[112,1280]{1,0:T(8,128)(2,1)S(1)}, u32[]{:S(2)}, u32[]{:S(2)}) collective-permute-start(bf16[112,1280]{1,0:T(8,128)(2,1)S(1)} %copy-done.7), channel_id=1, source_target_pairs={{0,16},{16,0},{1,17},{17,1},{2,18},{18,2},{3,19},{19,3},{4,20},{20... | collective-permute-start | bytes 860168 | tf_op jit(solution)/shard_map/ppermute | solution.py:248
  80.2 1.9 %collective-permute-start.8 = (f32[16,128]{1,0:T(8,128)S(1)}, f32[16,128]{1,0:T(8,128)S(1)}, u32[]{:S(2)}, u32[]{:S(2)}) collective-permute-start(f32[16,128]{1,0:T(8,128)S(1)} %slice.12), channel_id=1, source_target_pairs={{0,8},{8,0},{1,9},{9,1},{2,10},{10,2},{3,11},{11,3},{4,12},{12,4},... | collective-permute-start | bytes 24584 | tf_op jit(solution)/shard_map/ppermute | solution.py:248
  82.1 1.1 collective-permute-done.8.across_ref
  83.2 3.4 %collective-permute-done.9.w1 = bf16[112,1280]{1,0:T(8,128)(2,1)S(1)} collective-permute-done((bf16[112,1280]{1,0:T(8,128)(2,1)S(1)}, bf16[112,1280]{1,0:T(8,128)(2,1)S(1)}, u32[]{:S(2)}, u32[]{:S(2)}) %collective-permute-start.9) | collective-permute-done | bytes 286752 | tf_op jit(solution)/shard_map/ppermute | solution.py:248
  86.6 3.1 %all-to-all-done.3.part_ref = bf16[8,16,1280]{2,1,0:T(8,128)(2,1)S(1)} async-done(((bf16[8,16,1280]{2,1,0:T(8,128)(2,1)}), bf16[8,16,1280]{2,1,0:T(8,128)(2,1)S(1)}, u32[]{:S(2)}, u32[]{:S(2)}) %all-to-all-start.3) | async-done | bytes 327712 | tf_op jit(solution)/shard_map/all_to_all | solution.py:252
  89.7 0.3 shard_map.124
  90.0 18.5 %all_to_all.30 = bf16[16,16,576]{2,1,0:T(8,128)(2,1)S(1)} all-to-all(bf16[16,16,576]{2,1,0:T(8,128)(2,1)S(1)} %shard_map.124), channel_id=1, replica_groups=mesh['z'=8,'xh'=2,'xl'=2,'c'=2,'y'=8] {'z','xh'}, dimensions={0} | all-to-all | bytes 589824 | tf_op jit(solution)/shard_map/all_to_all | solution.py:252
  108.5 1.9 %collective-permute-start.10 = (bf16[16,16,576]{2,1,0:T(8,128)(2,1)S(1)}, bf16[16,16,576]{2,1,0:T(8,128)(2,1)S(1)}, u32[]{:S(2)}, u32[]{:S(2)}) collective-permute-start(bf16[16,16,576]{2,1,0:T(8,128)(2,1)S(1)} %all_to_all.30), channel_id=1, source_target_pairs={{0,8},{8,0},{1,9},{9,1},{2,10},{10,2},{3,11},{11,3},{4,12},{12,4},... | collective-permute-start | bytes 884744 | tf_op jit(solution)/shard_map/ppermute | solution.py:248
  110.4 1.6 %collective-permute-done.10 = bf16[16,16,576]{2,1,0:T(8,128)(2,1)S(1)} collective-permute-done((bf16[16,16,576]{2,1,0:T(8,128)(2,1)S(1)}, bf16[16,16,576]{2,1,0:T(8,128)(2,1)S(1)}, u32[]{:S(2)}, u32[]{:S(2)}) %collective-permute-start.10) | collective-permute-done | bytes 294944 | tf_op jit(solution)/shard_map/ppermute | solution.py:248
  112.0 0.9 shard_map.125
  112.9 16.2 %all_to_all.31 = bf16[16,32,128]{2,1,0:T(8,128)(2,1)S(1)} all-to-all(bf16[16,32,128]{2,1,0:T(8,128)(2,1)S(1)} %shard_map.125), channel_id=1, replica_groups=mesh['z'=8,'xh'=2,'xl'=2,'c'=2,'y'=8] {'xl','y'}, dimensions={0} | all-to-all | bytes 262144 | tf_op jit(solution)/shard_map/all_to_all | solution.py:252
  129.2 0.6 slice_reduce_fusion
  (20 shorter events, 0.1 us)
Async XLA Ops:
  0.7 17.2 %copy-start.10 = (bf16[112]{0:T(256)(128)(2,1)S(1)}, bf16[112]{0:T(256)(128)(2,1)}, u32[]{:S(2)}) copy-start(bf16[112]{0:T(256)(128)(2,1)} %param.20) | copy-start | bytes 676
  4.5 13.5 %copy-start = (bf16[2048,112]{0,1:T(8,128)(2,1)S(1)}, bf16[2048,112]{0,1:T(8,128)(2,1)}, u32[]{:S(2)}) copy-start(bf16[2048,112]{0,1:T(8,128)(2,1)} %param.18) | copy-start | bytes 1376260
  4.5 13.5 %copy-start.9 = (bf16[256,112]{0,1:T(8,128)(2,1)S(1)}, bf16[256,112]{0,1:T(8,128)(2,1)}, u32[]{:S(2)}) copy-start(bf16[256,112]{0,1:T(8,128)(2,1)} %param.19) | copy-start | bytes 172036
  4.5 16.3 %copy-start.1 = (bf16[112,2304]{1,0:T(8,128)(2,1)S(1)}, bf16[112,2304]{1,0:T(8,128)(2,1)}, u32[]{:S(2)}) copy-start(bf16[112,2304]{1,0:T(8,128)(2,1)} %gate_ref) | copy-start | bytes 1548292
  4.5 16.3 %copy-start.2 = (bf16[112,2304]{1,0:T(8,128)(2,1)S(1)}, bf16[112,2304]{1,0:T(8,128)(2,1)}, u32[]{:S(2)}) copy-start(bf16[112,2304]{1,0:T(8,128)(2,1)} %up_ref) | copy-start | bytes 1548292
  4.5 16.3 %copy-start.3 = (bf16[2304,112]{0,1:T(8,128)(2,1)S(1)}, bf16[2304,112]{0,1:T(8,128)(2,1)}, u32[]{:S(2)}) copy-start(bf16[2304,112]{0,1:T(8,128)(2,1)} %param.23) | copy-start | bytes 1548292
  4.5 31.0 %all-to-all-start = ((bf16[32,16,512]{2,1,0:T(8,128)(2,1)}), bf16[32,16,512]{2,1,0:T(8,128)(2,1)S(1)}, u32[]{:S(2)}, u32[]{:S(2)}) async-start(bf16[32,16,512]{2,1,0:T(8,128)(2,1)} %shard_map.118), calls=%async_computation | async-start | bytes 1048576 | tf_op jit(solution)/shard_map/all_to_all | solution.py:252
  18.8 16.7 %collective-permute-start = (bf16[112,2432]{1,0:T(8,128)(2,1)}, bf16[112,2432]{1,0:T(8,128)(2,1)S(1)}, u32[]{:S(2)}, u32[]{:S(2)}) collective-permute-start(bf16[112,2432]{1,0:T(8,128)(2,1)} %pad_maximum_fusion), channel_id=1, source_target_pairs={{0,8},{8,0},{1,9},{9,1},{2,10},{10,2},{3,11},{11,3},{4,12},{12,4},... | collective-permute-start | bytes 1634312 | tf_op jit(solution)/shard_map/ppermute | solution.py:248
  22.5 0.7 copy-start.4
  23.2 0.7 copy-start.6
  23.9 20.4 %copy-start.8 = (s32[64]{0:T(128)S(1)}, s32[64]{0:T(128)}, u32[]{:S(2)}) copy-start(s32[64]{0:T(128)} %param.16) | copy-start | bytes 772
  23.9 20.5 %collective-permute-start.1 = (bf16[112,1152]{1,0:T(8,128)(2,1)}, bf16[112,1152]{1,0:T(8,128)(2,1)S(1)}, u32[]{:S(2)}, u32[]{:S(2)}) collective-permute-start(bf16[112,1152]{1,0:T(8,128)(2,1)} %get-tuple-element.50), channel_id=1, source_target_pairs={{0,16},{16,0},{1,17},{17,1},{2,18},{18,2},{3,19},{19,3},{4,20},{20... | collective-permute-start | bytes 774152 | tf_op jit(solution)/shard_map/ppermute | solution.py:248
  27.7 16.7 %collective-permute-start.2 = (bf16[112,1152]{1,0:T(8,128)(2,1)}, bf16[112,1152]{1,0:T(8,128)(2,1)S(1)}, u32[]{:S(2)}, u32[]{:S(2)}) collective-permute-start(bf16[112,1152]{1,0:T(8,128)(2,1)} %get-tuple-element.51), channel_id=1, source_target_pairs={{0,32},{32,0},{1,33},{33,1},{2,34},{34,2},{3,35},{35,3},{4,36},{36... | collective-permute-start | bytes 774152 | tf_op jit(solution)/shard_map/ppermute | solution.py:248
  32.3 16.9 %collective-permute-start.3 = (bf16[112,1152]{1,0:T(8,128)(2,1)}, bf16[112,1152]{1,0:T(8,128)(2,1)S(1)}, u32[]{:S(2)}, u32[]{:S(2)}) collective-permute-start(bf16[112,1152]{1,0:T(8,128)(2,1)} %get-tuple-element.52), channel_id=1, source_target_pairs={{0,48},{16,32},{32,16},{48,0},{1,49},{17,33},{33,17},{49,1},{2,50}... | collective-permute-start | bytes 774152 | tf_op jit(solution)/shard_map/ppermute | solution.py:308
  35.6 22.4 %copy-start.5 = (bf16[112,1152]{1,0:T(8,128)(2,1)S(1)}, bf16[112,1152]{1,0:T(8,128)(2,1)}, u32[]{:S(2)}) copy-start(bf16[112,1152]{1,0:T(8,128)(2,1)} %copy-done.4) | copy-start | bytes 774148
  36.7 14.5 %all-to-all-start.1 = ((bf16[8,32,128]{2,1,0:T(8,128)(2,1)}), bf16[8,32,128]{2,1,0:T(8,128)(2,1)S(1)}, u32[]{:S(2)}, u32[]{:S(2)}) async-start(bf16[8,32,128]{2,1,0:T(8,128)(2,1)} %shard_map.120), calls=%async_computation.1 | async-start | bytes 131072 | tf_op jit(solution)/shard_map/all_to_all | solution.py:252
  52.2 18.0 %all-to-all-start.2 = ((bf16[32,32,128]{2,1,0:T(8,128)(2,1)}), bf16[32,32,128]{2,1,0:T(8,128)(2,1)S(1)}, u32[]{:S(2)}, u32[]{:S(2)}) async-start(bf16[32,32,128]{2,1,0:T(8,128)(2,1)} %get-tuple-element.56), calls=%async_computation.2 | async-start | bytes 524288 | tf_op jit(solution)/shard_map/all_to_all | solution.py:252
  58.0 19.7 %copy-start.7 = (bf16[112,1280]{1,0:T(8,128)(2,1)S(1)}, bf16[112,1280]{1,0:T(8,128)(2,1)}, u32[]{:S(2)}) copy-start(bf16[112,1280]{1,0:T(8,128)(2,1)} %copy-done.6) | copy-start | bytes 860164
  58.0 8.8 %collective-permute-start.4 = (bf16[112,1152]{1,0:T(8,128)(2,1)S(1)}, bf16[112,1152]{1,0:T(8,128)(2,1)S(1)}, u32[]{:S(2)}, u32[]{:S(2)}) collective-permute-start(bf16[112,1152]{1,0:T(8,128)(2,1)S(1)} %copy-done.5), channel_id=1, source_target_pairs={{0,8},{8,0},{1,9},{9,1},{2,10},{10,2},{3,11},{11,3},{4,12},{12,4},... | collective-permute-start | bytes 774152 | tf_op jit(solution)/shard_map/ppermute | solution.py:248
  60.0 6.8 %collective-permute-start.5 = (bf16[112,1152]{1,0:T(8,128)(2,1)S(1)}, bf16[112,1152]{1,0:T(8,128)(2,1)S(1)}, u32[]{:S(2)}, u32[]{:S(2)}) collective-permute-start(bf16[112,1152]{1,0:T(8,128)(2,1)S(1)} %collective-permute-done.1.refs_1_), channel_id=1, source_target_pairs={{0,8},{8,0},{1,9},{9,1},{2,10},{10,2},{3,11},{11,3},{4,12},{12,4},... | collective-permute-start | bytes 774152 | tf_op jit(solution)/shard_map/ppermute | solution.py:248
  62.4 4.4 %collective-permute-start.6 = (bf16[112,1152]{1,0:T(8,128)(2,1)S(1)}, bf16[112,1152]{1,0:T(8,128)(2,1)S(1)}, u32[]{:S(2)}, u32[]{:S(2)}) collective-permute-start(bf16[112,1152]{1,0:T(8,128)(2,1)S(1)} %collective-permute-done.2.refs_2_), channel_id=1, source_target_pairs={{0,8},{8,0},{1,9},{9,1},{2,10},{10,2},{3,11},{11,3},{4,12},{12,4},... | collective-permute-start | bytes 774152 | tf_op jit(solution)/shard_map/ppermute | solution.py:248
  64.4 3.5 %collective-permute-start.7 = (bf16[112,1152]{1,0:T(8,128)(2,1)S(1)}, bf16[112,1152]{1,0:T(8,128)(2,1)S(1)}, u32[]{:S(2)}, u32[]{:S(2)}) collective-permute-start(bf16[112,1152]{1,0:T(8,128)(2,1)S(1)} %collective-permute-done.3.refs_3_), channel_id=1, source_target_pairs={{0,8},{8,0},{1,9},{9,1},{2,10},{10,2},{3,11},{11,3},{4,12},{12,4},... | collective-permute-start | bytes 774152 | tf_op jit(solution)/shard_map/ppermute | solution.py:248
  71.5 18.2 %all-to-all-start.3 = ((bf16[8,16,1280]{2,1,0:T(8,128)(2,1)}), bf16[8,16,1280]{2,1,0:T(8,128)(2,1)S(1)}, u32[]{:S(2)}, u32[]{:S(2)}) async-start(bf16[8,16,1280]{2,1,0:T(8,128)(2,1)} %shard_map.123), calls=%async_computation.3 | async-start | bytes 655360 | tf_op jit(solution)/shard_map/all_to_all | solution.py:252
  77.6 9.0 %collective-permute-start.9 = (bf16[112,1280]{1,0:T(8,128)(2,1)S(1)}, bf16[112,1280]{1,0:T(8,128)(2,1)S(1)}, u32[]{:S(2)}, u32[]{:S(2)}) collective-permute-start(bf16[112,1280]{1,0:T(8,128)(2,1)S(1)} %copy-done.7), channel_id=1, source_target_pairs={{0,16},{16,0},{1,17},{17,1},{2,18},{18,2},{3,19},{19,3},{4,20},{20... | collective-permute-start | bytes 860168 | tf_op jit(solution)/shard_map/ppermute | solution.py:248
  80.2 3.1 %collective-permute-start.8 = (f32[16,128]{1,0:T(8,128)S(1)}, f32[16,128]{1,0:T(8,128)S(1)}, u32[]{:S(2)}, u32[]{:S(2)}) collective-permute-start(f32[16,128]{1,0:T(8,128)S(1)} %slice.12), channel_id=1, source_target_pairs={{0,8},{8,0},{1,9},{9,1},{2,10},{10,2},{3,11},{11,3},{4,12},{12,4},... | collective-permute-start | bytes 24584 | tf_op jit(solution)/shard_map/ppermute | solution.py:248
  108.5 3.5 %collective-permute-start.10 = (bf16[16,16,576]{2,1,0:T(8,128)(2,1)S(1)}, bf16[16,16,576]{2,1,0:T(8,128)(2,1)S(1)}, u32[]{:S(2)}, u32[]{:S(2)}) collective-permute-start(bf16[16,16,576]{2,1,0:T(8,128)(2,1)S(1)} %all_to_all.30), channel_id=1, source_target_pairs={{0,8},{8,0},{1,9},{9,1},{2,10},{10,2},{3,11},{11,3},{4,12},{12,4},... | collective-permute-start | bytes 884744 | tf_op jit(solution)/shard_map/ppermute | solution.py:248

commit v5 on v4

--- a/solution.py
+++ b/solution.py
@@ -9,7 +9,6 @@
 D = 7168
 WIDTH = 112
 SIZE = 576
-DOWN = 5 * 128
 
 score_scale = 192.0 ** (-0.5)
 norm_eps = 1e-06
@@ -44,7 +43,7 @@
     return jnp.dot(a, b, preferred_element_type=F32)
 
 
-def attention_kernel(len_ref, q_ref, new_ref, cache_ref, maps_ref, out_ref, q_in, cache, maps, ctx, heads, sems):
+def attention_kernel(len_ref, q_ref, new_ref, cache_ref, maps_ref, out_ref, q_in, cache, maps, ctx, pairs, heads, sems):
     fetches = [
         pltpu.make_async_copy(src, dst, sems.at[i])
         for i, (src, dst) in enumerate(((q_ref, q_in), (cache_ref, cache), (maps_ref, maps)))
@@ -76,38 +75,44 @@
     for n in range(4):
         ctx[n] = context[:, n * 128 : (n + 1) * 128]
     fetches[2].wait()
-    for h in range(16):
-        rows = jnp.concatenate([ctx[n, pl.ds(h, 4, stride=16), :] for n in range(4)], axis=1).astype(BF)
-        k, place = h // 4, h % 4
-        heads[k * 4 : k * 4 + 4, place * 128 : place * 128 + 128] = dot(rows, maps[h])
+    for h in range(8):
+        rows = jnp.concatenate([ctx[n, pl.ds(h, 8, stride=8), :] for n in range(4)], axis=1).astype(BF)
+        pair = dot(rows, jnp.concatenate([maps[h], maps[h + 8]], axis=1))
+        for i, head in enumerate((h, h + 8)):
+            pairs[i] = pair[:, i * 128 : i * 128 + 128]
+            k, place = head // 4, head % 4
+            heads[k * 4 : k * 4 + 4, place * 128 : place * 128 + 128] = pairs[i, pl.ds(i, 4, stride=2), :]
     block = heads[...].astype(BF)
     for i in range(32):
         out_ref[i] = block
 
 
-def pack_kernel(xh_ref, xl_ref, gate_ref, up_ref, down_ref, ff0, ff1, ff2, ff3, fd_ref, send_fd_ref):
-    cuts = [slice(i * SIZE, (i + 1) * SIZE) for i in range(4)]
-    pad = jnp.zeros((WIDTH, DOWN - SIZE), BF)
-    for i, cut in enumerate(cuts):
+def target(xh_ref, xl_ref, r):
+    return 2 * (xh_ref[0] ^ (r >> 1)) + (xl_ref[0] ^ (r & 1))
+
+
+def pack_kernel(xh_ref, xl_ref, gate_ref, up_ref, proj_ref, residual_ref, gain_ref, carry_ref, *outs):
+    carry_ref[:, :2048] = proj_ref[...]
+    carry_ref[:, 2048:2304] = residual_ref[...]
+    carry_ref[:, 2304:] = gain_ref[...]
+    for i in range(4):
+        cut = slice(i * SIZE, (i + 1) * SIZE)
         block = jnp.concatenate([gate_ref[:, cut], up_ref[:, cut]], axis=1)
-        for r, out_ref in enumerate((ff0, ff1, ff2, ff3)):
-            target = 2 * (xl_ref[0] ^ (r & 1)) + (xh_ref[0] ^ (r >> 1))
-
-            @pl.when(target == i)
+        for r, out_ref in enumerate(outs):
+
+            @pl.when(target(xh_ref, xl_ref, r) == i)
             def _(out_ref=out_ref, block=block):
                 out_ref[...] = block
 
-    for half in range(2):
-        both = [down_ref[:, cuts[2 * half]], pad, down_ref[:, cuts[2 * half + 1]], pad]
-        both = jnp.concatenate(both, axis=1)
-
-        @pl.when(xl_ref[0] == half)
-        def _(both=both):
-            fd_ref[...] = both
-
-        @pl.when(xl_ref[0] != half)
-        def _(both=both):
-            send_fd_ref[...] = both
+
+def pack_down_kernel(xh_ref, xl_ref, down_ref, *outs):
+    for i in range(4):
+        block = down_ref[:, i * SIZE : (i + 1) * SIZE]
+        for r, out_ref in enumerate(outs):
+
+            @pl.when(target(xh_ref, xl_ref, r) == i)
+            def _(out_ref=out_ref, block=block):
+                out_ref[...] = block
 
 
 def rows_kernel(core_ref, y_ref, slot_ref, pick_ref, place_ref):
@@ -157,8 +162,8 @@
     nt = (((1,), (1,)), ((), ()))
     pick = pick_ref[...]
     unit = (lax.broadcasted_iota(jnp.int32, (16, 128), 1) == 0).astype(F32).astype(BF)
-    picked = lambda ref: lax.dot_general(pick, ref[:, :256], nt, preferred_element_type=F32)
-    gains = lambda ref: lax.dot_general(unit, ref[:, 256:], nt, preferred_element_type=F32)
+    picked = lambda ref: lax.dot_general(pick, ref[:, 2048:2304], nt, preferred_element_type=F32)
+    gains = lambda ref: lax.dot_general(unit, ref[:, 2304:], nt, preferred_element_type=F32)
     hidden = attended + jnp.concatenate([picked(own_ref), picked(other_ref)], axis=0)
     gain = jnp.concatenate([gains(own_ref), gains(other_ref)], axis=0)
     squares = jnp.sum(hidden * hidden, axis=1, keepdims=True)
@@ -177,7 +182,7 @@
 
 
 def gate_kernel(xh_ref, xl_ref, full_ref, *refs):
-    own_refs, other_refs, out_ref = refs[:4], refs[4:8], refs[8]
+    own_refs, other_refs, out_ref = refs[:4], refs[4:7], refs[7]
     lane = lax.broadcasted_iota(jnp.int32, (128, 128), 1)
     valid = lane < WIDTH
     none = jnp.zeros((128 - WIDTH, 384), BF)
@@ -195,7 +200,8 @@
     for n in range(0, 2 * SIZE, 384):
         total = jnp.zeros((128, 384), F32)
         for r in range(4):
-            both = [own_refs[r][:, n : n + 384], none, other_refs[r][:, n : n + 384], none]
+            k, at = divmod(r * 2 * SIZE + n, 4 * 384)
+            both = [own_refs[r][:, n : n + 384], none, other_refs[k][:, at : at + 384], none]
             total = total + dot(held[r], jnp.concatenate(both, axis=0))
         out_ref[:, :, n : n + 384] = total.astype(BF).reshape(8, 16, 384)
     high = squares.astype(BF).astype(F32)
@@ -212,28 +218,20 @@
     gate = total[:, :SIZE] * factor
     up = total[:, SIZE : 2 * SIZE] * factor
     units = (gate * jax.nn.sigmoid(gate) * up).astype(BF)
-    for i in range(16):
+    for i in range(8):
         out_ref[i] = units
 
 
 def down_kernel(
-    xl_ref, y_ref, own_ref, other_ref, w0, w1, hidden_ref, across_ref, place_ref, out_ref, total
+    xh_ref, xl_ref, y_ref, own_ref, other_ref, w0, w1, w2, w3, hidden_ref, across_ref, place_ref, out_ref, total
 ):
-    units = [
-        jnp.concatenate(
-            [own_ref[:, i].reshape(128, SIZE), other_ref[:, i].reshape(128, SIZE)], axis=0
-        )
-        for i in range(2)
-    ]
+    units = jnp.concatenate([own_ref[...].reshape(128, SIZE), other_ref[...].reshape(128, SIZE)], axis=0)
     place = place_ref[...]
     none = jnp.zeros((128 - WIDTH, SIZE), BF)
     nt = (((1,), (1,)), ((), ()))
-    for r, w in enumerate((w0, w1)):
-        part = jnp.zeros((256, 128), F32)
-        for i in range(2):
-            at = i * DOWN
-            wide = jnp.concatenate([w[:, at : at + SIZE], none], axis=0)
-            part = part + lax.dot_general(units[i], wide, nt, preferred_element_type=F32)
+    for r, w in enumerate((w0, w1, w2, w3)):
+        wide = jnp.concatenate([w[...], none], axis=0)
+        part = lax.dot_general(units, wide, nt, preferred_element_type=F32)
         if r == 0:
             total[...] = part
             at = pl.multiple_of(y_ref[0] * 16, 16)
@@ -241,7 +239,8 @@
             total[pl.ds(128 + at, 16), :] += across_ref[...]
             part = total[...]
         rows = dot(place, part.astype(BF)).astype(BF)
-        out_ref[pl.ds((xl_ref[0] ^ r) * 8, 8)] = rows.reshape(8, 32, 128)
+        x = 2 * (xh_ref[0] ^ (r >> 1)) + (xl_ref[0] ^ (r & 1))
+        out_ref[pl.ds(x * 8, 8)] = rows.reshape(8, 32, 128)
 
 
 def swap(value, axis="c"):
@@ -250,6 +249,10 @@
 
 def exchange(blocks, axes):
     return lax.all_to_all(blocks, axes, 0, 0, tiled=True)
+
+
+def diagonal(value):
+    return lax.ppermute(value, ("xh", "xl"), [(i, 3 - i) for i in range(4)])
 
 
 def local(
@@ -277,6 +280,7 @@
             pltpu.VMEM((576, 512), BF),
             pltpu.VMEM((16, 512, 128), BF),
             pltpu.VMEM((4, 64, 128), F32),
+            pltpu.VMEM((2, 8, 128), F32),
             pltpu.VMEM((16, 512), F32),
             pltpu.SemaphoreType.DMA((3,)),
         ],
@@ -289,24 +293,16 @@
     )
     rows = exchange(blocks, ("z", "xh", "xl"))
     gains = jnp.broadcast_to(norm_gain[:, None], (WIDTH, 128))
-    carry = jnp.concatenate([out_proj, residual, gains], axis=1)
-    carry_other = swap(carry)
-    tail, tail_other = carry[:, 2048:], carry_other[:, 2048:]
-
-    *ff, down_own, down_sent = call(
+    carry, *ff = call(
         pack_kernel,
-        [SMEM, SMEM, VMEM, VMEM, VMEM],
-        [shape((WIDTH, 2 * SIZE))] * 4 + [shape((WIDTH, 2 * DOWN))] * 2,
+        [SMEM] * 2 + [VMEM] * 5,
+        [shape((WIDTH, 2048 + 256 + 128))] + [shape((WIDTH, 2 * SIZE))] * 4,
         (),
         0,
         3_200_000,
-    )(xh, xl, w_gate, w_up, w_down)
-    ff = [
-        ff[0],
-        swap(ff[1], "xl"),
-        swap(ff[2], "xh"),
-        lax.ppermute(ff[3], ("xh", "xl"), [(i, 3 - i) for i in range(4)]),
-    ]
+    )(xh, xl, w_gate, w_up, out_proj, residual, gains)
+    carry_other = swap(carry)
+    ff = [ff[0], swap(ff[1], "xl"), swap(ff[2], "xh"), diagonal(ff[3])]
     rows, ff[0] = lax.optimization_barrier((rows, ff[0]))
     part = call(
         out_kernel,
@@ -316,43 +312,51 @@
         1_000_000,
         100_000,
     )(rows, out_proj, carry_other)
+    _, slot_of, w_down = lax.optimization_barrier((part, slot_of, w_down))
     pick, place = call(
         rows_kernel, [SMEM, SMEM, VMEM], [shape((16, 256)), shape((256, 256))], (), 0, 200_000
     )(core, tp, slot_of[None])
-    part, *ff = lax.optimization_barrier((exchange(part, "y"), *ff))
+    down = call(
+        pack_down_kernel, [SMEM, SMEM, VMEM], [shape((WIDTH, SIZE))] * 4, (), 0, 1_000_000
+    )(xh, xl, w_down)
+    _, _, ff = lax.optimization_barrier((pick, down, ff))
+    joined = jnp.concatenate
+    thirds = [
+        joined([ff[0], ff[1][:, :384]], axis=1),
+        joined([ff[1][:, 384:], ff[2][:, :768]], axis=1),
+        joined([ff[2][:, 768:], ff[3]], axis=1),
+    ]
+    part, ff, thirds, down, pick = lax.optimization_barrier(
+        (exchange(part, "y"), ff, thirds, down, pick)
+    )
     scaled, hidden = call(
         norm_kernel, [VMEM] * 4, [shape((32, 32, 128)), shape((32, 128), F32)], (), 0, 400_000
-    )(part, pick, tail, tail_other)
-    hidden, *ff = lax.optimization_barrier((hidden, *ff))
-    ff_other = [swap(w) for w in ff]
+    )(part, pick, carry, carry_other)
+    hidden, *thirds = lax.optimization_barrier((hidden, *thirds))
+    ff_other = [swap(w) for w in thirds]
     part = call(
-        gate_kernel, [SMEM] * 2 + [VMEM] * 9, shape((8, 16, 1280)), (), 300_000_000, 2_800_000
+        gate_kernel, [SMEM] * 2 + [VMEM] * 8, shape((8, 16, 1280)), (), 300_000_000, 2_800_000
     )(xh, xl, exchange(scaled, ("xh", "xl", "y")), *ff, *ff_other)
-    _, hidden, down_sent = lax.optimization_barrier((part, hidden, down_sent))
-    part, across, down_near = lax.optimization_barrier(
-        (exchange(part, "z"), swap(hidden[16:]), swap(down_sent, "xl"))
-    )
-    units = call(units_kernel, [VMEM], shape((16, 16, SIZE)), (), 0, 500_000)(part)
-    units = exchange(units, ("z", "xh"))
+    _, far, near = lax.optimization_barrier((part, down[2], down[1]))
+    part, far, near = lax.optimization_barrier(
+        (exchange(part, "z"), swap(far, "xh"), swap(near, "xl"))
+    )
+    units = call(units_kernel, [VMEM], shape((8, 16, SIZE)), (), 0, 500_000)(part)
+    _, hidden, cross = lax.optimization_barrier((units, hidden, down[3]))
+    units, across, cross = lax.optimization_barrier(
+        (exchange(units, "z"), swap(hidden[16:]), diagonal(cross))
+    )
+    down = (down[0], near, far, cross)
     part = call(
         down_kernel,
-        [SMEM] * 2 + [VMEM] * 7,
-        shape((16, 32, 128)),
+        [SMEM] * 3 + [VMEM] * 9,
+        shape((32, 32, 128)),
         [pltpu.VMEM((256, 128), F32)],
         200_000_000,
         1_600_000,
-    )(
-        xl,
-        tp,
-        units.reshape(8, 2, 16, SIZE),
-        swap(units).reshape(8, 2, 16, SIZE),
-        down_own,
-        down_near,
-        hidden,
-        across,
-        place,
-    )
-    return jnp.sum(exchange(part, ("xl", "y"))[:, :, :WIDTH].astype(F32), axis=0).astype(BF)
+    )(xh, xl, tp, units, swap(units), *down, hidden, across, place)
+    total = jnp.sum(exchange(part, ("xh", "xl", "y"))[:, :, :WIDTH].astype(F32), axis=0)
+    return total.astype(BF)
 
 
 def solution(mesh):

time: 131 us -> 130 us (level)
  blocking collectives: 34.8 us -> 19.1 us
  starting transfers between devices: 60.3 us -> 71.3 us
  waiting for transfers between devices: 20.4 us -> 22.3 us
    all_to_all x2 -> x1, blocking collectives: 34.8 us -> 19.1 us  [exchange(): return lax.all_to_all(blocks, axes, 0, 0, tiled=True)]
    all_to_all x4 -> x5, starting transfers between devices: 32.7 us -> 39 us  [exchange(): return lax.all_to_all(blocks, axes, 0, 0, tiled=True)]
    ppermute x1 -> x2, starting transfers between devices: 2.13 us -> 6.03 us  [diagonal(): return lax.ppermute(value, ('xh', 'xl'), [(i, 3 - i) for i in range(4)])]
    all_to_all x4 -> x5, waiting for transfers between devices: 8.41 us -> 11.9 us  [exchange(): return lax.all_to_all(blocks, axes, 0, 0, tiled=True)]
    ppermute x1 -> x2, waiting for transfers between devices: 4.77 us -> 1.73 us  [diagonal(): return lax.ppermute(value, ('xh', 'xl'), [(i, 3 - i) for i in range(4)])]
    ppermute x10, waiting for transfers between devices: 7.25 us -> 8.69 us  [swap(): return lax.ppermute(value, axis, [(0, 1), (1, 0)])]
    pallas_call x4 -> x5, Pallas kernels: 4.18 us -> 5.42 us  [the longest x1 1.48 us: local(): call(down_kernel, [SMEM] * 3 + [VMEM] * 9, shape((32, 32, 128)), [pltpu.V...]
  transfers between devices with their start and end apart: 15 -> 17, of which waited for: 9 -> 12; matrix products, arithmetic and copies ran while one was open for 1% -> 1% of each run, Pallas kernels for 2% -> 2%
where the time goes in v5:
time: 130 us; the launch traced here: 129 us
  starting transfers between devices  71.3 us (55%)
  waiting for transfers between devices  22.3 us (17%)
  blocking collectives  19.1 us (15%)
  Pallas kernels  11.6 us (9%)
  other arithmetic  2.36 us (2%)
    all_to_all x5, starting transfers between devices, exchange(): return lax.all_to_all(blocks, axes, 0, 0, tiled=True)  39 us
    ppermute x10, starting transfers between devices, swap(): return lax.ppermute(value, axis, [(0, 1), (1, 0)])  26.2 us
    all_to_all x1, blocking collectives, exchange(): return lax.all_to_all(blocks, axes, 0, 0, tiled=True)  19.1 us
    all_to_all x5, waiting for transfers between devices, exchange(): return lax.all_to_all(blocks, axes, 0, 0, tiled=True)  11.9 us
    ppermute x10, waiting for transfers between devices, swap(): return lax.ppermute(value, axis, [(0, 1), (1, 0)])  8.69 us
    ppermute x2, starting transfers between devices, diagonal(): return lax.ppermute(value, ('xh', 'xl'), [(i, 3 - i) for i in range(4)])  6.03 us
    pallas_call x1, Pallas kernels, local(): call(attention_kernel, [SMEM, HBM, VMEM, HBM, HBM], shape((32, 16, 512)),...  3.89 us
  transfers between devices with their start and end apart: 17, of which 12 were waited for; matrix products, arithmetic and copies ran while one was open for 1% of the time, Pallas kernels for 2%

profile of v5, /device:TPU:8, one launch (start us, length us, event | category | flops | bytes accessed | tf_op | source)
XLA Modules:
  0.0 129.0 jit_solution(3584647019311168562)
XLA Ops:
  0.7 3.9 %shard_map.118 = bf16[32,16,512]{2,1,0:T(8,128)(2,1)} custom-call(s32[1]{0:T(128)S(6)} %copy.13.len_ref, bf16[64,576]{1,0:T(8,128)(2,1)} %bitcast.19, bf16[4,576]{1,0:T(4,128)(2,1)} %bitcast.20, bf16[576,512]{1,0:T(8,128)(2,1)} %bitcast.18, bf16[16,512,128]{2,1,0:T(8,128)(2,1)} %maps_ref.1), custom_call_target="tpu_custom_call" | custom-call | flops 200000000 | bytes 4000000 | tf_op jit(solution)/shard_map/pallas_call | solution.py:274
  4.6 13.2 %all-to-all-start = ((bf16[32,16,512]{2,1,0:T(8,128)(2,1)}), bf16[32,16,512]{2,1,0:T(8,128)(2,1)S(1)}, u32[]{:S(2)}, u32[]{:S(2)}) async-start(bf16[32,16,512]{2,1,0:T(8,128)(2,1)} %shard_map.118), calls=%async_computation | async-start | bytes 1048576 | tf_op jit(solution)/shard_map/all_to_all | solution.py:251
  17.8 0.0 copy-start.11
  17.8 0.1 broadcast_in_dim.24.gain_ref
  17.9 1.4 %shard_map.119 = (bf16[112,2432]{1,0:T(8,128)(2,1)S(1)}, bf16[112,1152]{1,0:T(8,128)(2,1)S(1)}, bf16[112,1152]{1,0:T(8,128)(2,1)}, bf16[112,1152]{1,0:T(8,128)(2,1)}, bf16[112,1152]{1,0:T(8,128)(2,1)S(1)}) custom-call(s32[1]{0:T(128)} %bitcast.xh_ref, s32[1]{0:T(128)} %bitcast.1.xl_ref, bf16[112,2304]{1,0:T(8,128)(2,1)S(1)} %copy-done.1, ...), custom_call_target="tpu_custom_call" | custom-call | bytes 3200000 | tf_op jit(solution)/shard_map/pallas_call | solution.py:296
  19.3 1.9 %collective-permute-start = (bf16[112,2432]{1,0:T(8,128)(2,1)S(1)}, bf16[112,2432]{1,0:T(8,128)(2,1)S(1)}, u32[]{:S(2)}, u32[]{:S(2)}) collective-permute-start(bf16[112,2432]{1,0:T(8,128)(2,1)S(1)} %get-tuple-element.69.own_ref), channel_id=1, source_target_pairs={{0,8},{8,0},{1,9},{9,1},{2,10},{10,2},{3,11},{11,3},{4,12},{12,4},... | collective-permute-start | bytes 1634312 | tf_op jit(solution)/shard_map/ppermute | solution.py:247
  21.2 3.7 %collective-permute-start.1 = (bf16[112,1152]{1,0:T(8,128)(2,1)}, bf16[112,1152]{1,0:T(8,128)(2,1)S(1)}, u32[]{:S(2)}, u32[]{:S(2)}) collective-permute-start(bf16[112,1152]{1,0:T(8,128)(2,1)} %get-tuple-element.80), channel_id=1, source_target_pairs={{0,16},{16,0},{1,17},{17,1},{2,18},{18,2},{3,19},{19,3},{4,20},{20... | collective-permute-start | bytes 774152 | tf_op jit(solution)/shard_map/ppermute | solution.py:247
  25.0 4.6 %collective-permute-start.2 = (bf16[112,1152]{1,0:T(8,128)(2,1)}, bf16[112,1152]{1,0:T(8,128)(2,1)S(1)}, u32[]{:S(2)}, u32[]{:S(2)}) collective-permute-start(bf16[112,1152]{1,0:T(8,128)(2,1)} %get-tuple-element.81), channel_id=1, source_target_pairs={{0,32},{32,0},{1,33},{33,1},{2,34},{34,2},{3,35},{35,3},{4,36},{36... | collective-permute-start | bytes 774152 | tf_op jit(solution)/shard_map/ppermute | solution.py:247
  29.5 2.1 %collective-permute-start.3 = (bf16[112,1152]{1,0:T(8,128)(2,1)S(1)}, bf16[112,1152]{1,0:T(8,128)(2,1)S(1)}, u32[]{:S(2)}, u32[]{:S(2)}) collective-permute-start(bf16[112,1152]{1,0:T(8,128)(2,1)S(1)} %get-tuple-element.82), channel_id=1, source_target_pairs={{0,48},{16,32},{32,16},{48,0},{1,49},{17,33},{33,17},{49,1},{2,50}... | collective-permute-start | bytes 774152 | tf_op jit(solution)/shard_map/ppermute | solution.py:255
  31.7 3.9 %all-to-all-done.x_ref = bf16[32,16,512]{2,1,0:T(8,128)(2,1)S(1)} async-done(((bf16[32,16,512]{2,1,0:T(8,128)(2,1)}), bf16[32,16,512]{2,1,0:T(8,128)(2,1)S(1)}, u32[]{:S(2)}, u32[]{:S(2)}) %all-to-all-start) | async-done | bytes 524320 | tf_op jit(solution)/shard_map/all_to_all | solution.py:251
  35.6 0.0 collective-permute-done.other_ref
  35.6 1.2 shard_map.120
  36.7 7.5 %all-to-all-start.1 = ((bf16[8,32,128]{2,1,0:T(8,128)(2,1)}), bf16[8,32,128]{2,1,0:T(8,128)(2,1)S(1)}, u32[]{:S(2)}, u32[]{:S(2)}) async-start(bf16[8,32,128]{2,1,0:T(8,128)(2,1)} %shard_map.120), calls=%async_computation.1 | async-start | bytes 131072 | tf_op jit(solution)/shard_map/all_to_all | solution.py:251
  44.3 1.0 copy-done.3
  45.3 0.4 shard_map.122
  45.7 0.1 shard_map.121
  45.9 0.0 collective-permute-done.2.refs_2_
  45.9 0.5 collective-permute-done.3.refs_3_
  46.5 0.9 pad_maximum_fusion
  47.4 0.8 pad_maximum_fusion.1
  48.2 3.0 %all-to-all-done.1.part_ref = bf16[8,32,128]{2,1,0:T(8,128)(2,1)S(1)} async-done(((bf16[8,32,128]{2,1,0:T(8,128)(2,1)}), bf16[8,32,128]{2,1,0:T(8,128)(2,1)S(1)}, u32[]{:S(2)}, u32[]{:S(2)}) %all-to-all-start.1) | async-done | bytes 65568 | tf_op jit(solution)/shard_map/all_to_all | solution.py:251
  51.2 1.0 shard_map.123
  52.2 5.7 %all-to-all-start.2 = ((bf16[32,32,128]{2,1,0:T(8,128)(2,1)}), bf16[32,32,128]{2,1,0:T(8,128)(2,1)S(1)}, u32[]{:S(2)}, u32[]{:S(2)}) async-start(bf16[32,32,128]{2,1,0:T(8,128)(2,1)} %get-tuple-element.89), calls=%async_computation.2 | async-start | bytes 524288 | tf_op jit(solution)/shard_map/all_to_all | solution.py:251
  58.0 2.1 %collective-permute-start.4 = (bf16[112,1536]{1,0:T(8,128)(2,1)}, bf16[112,1536]{1,0:T(8,128)(2,1)S(1)}, u32[]{:S(2)}, u32[]{:S(2)}) collective-permute-start(bf16[112,1536]{1,0:T(8,128)(2,1)} %get-tuple-element.98), channel_id=1, source_target_pairs={{0,8},{8,0},{1,9},{9,1},{2,10},{10,2},{3,11},{11,3},{4,12},{12,4},... | collective-permute-start | bytes 1032200 | tf_op jit(solution)/shard_map/ppermute | solution.py:247
  60.1 2.4 %collective-permute-start.5 = (bf16[112,1536]{1,0:T(8,128)(2,1)}, bf16[112,1536]{1,0:T(8,128)(2,1)S(1)}, u32[]{:S(2)}, u32[]{:S(2)}) collective-permute-start(bf16[112,1536]{1,0:T(8,128)(2,1)} %pad_maximum_fusion.1), channel_id=1, source_target_pairs={{0,8},{8,0},{1,9},{9,1},{2,10},{10,2},{3,11},{11,3},{4,12},{12,4},... | collective-permute-start | bytes 1032200 | tf_op jit(solution)/shard_map/ppermute | solution.py:247
  62.5 1.9 %collective-permute-start.6 = (bf16[112,1536]{1,0:T(8,128)(2,1)}, bf16[112,1536]{1,0:T(8,128)(2,1)S(1)}, u32[]{:S(2)}, u32[]{:S(2)}) collective-permute-start(bf16[112,1536]{1,0:T(8,128)(2,1)} %get-tuple-element.100), channel_id=1, source_target_pairs={{0,8},{8,0},{1,9},{9,1},{2,10},{10,2},{3,11},{11,3},{4,12},{12,4},... | collective-permute-start | bytes 1032200 | tf_op jit(solution)/shard_map/ppermute | solution.py:247
  64.4 0.0 collective-permute-done.4.refs_4_
  64.4 1.8 %collective-permute-done.6.refs_6_ = bf16[112,1536]{1,0:T(8,128)(2,1)S(1)} collective-permute-done((bf16[112,1536]{1,0:T(8,128)(2,1)}, bf16[112,1536]{1,0:T(8,128)(2,1)S(1)}, u32[]{:S(2)}, u32[]{:S(2)}) %collective-permute-start.6) | collective-permute-done | bytes 344096 | tf_op jit(solution)/shard_map/ppermute | solution.py:247
  66.2 2.8 %all-to-all-done.2.full_ref = bf16[32,32,128]{2,1,0:T(8,128)(2,1)S(1)} async-done(((bf16[32,32,128]{2,1,0:T(8,128)(2,1)}), bf16[32,32,128]{2,1,0:T(8,128)(2,1)S(1)}, u32[]{:S(2)}, u32[]{:S(2)}) %all-to-all-start.2) | async-done | bytes 262176 | tf_op jit(solution)/shard_map/all_to_all | solution.py:251
  69.1 1.3 %shard_map.124 = bf16[8,16,1280]{2,1,0:T(8,128)(2,1)} custom-call(s32[1]{0:T(128)} %bitcast.xh_ref, s32[1]{0:T(128)} %bitcast.1.xl_ref, bf16[32,32,128]{2,1,0:T(8,128)(2,1)S(1)} %all-to-all-done.2.full_ref, bf16[112,1152]{1,0:T(8,128)(2,1)S(1)} %get-tuple-element.90.refs_0_, bf16[112,1152]{1,0:T(8,128)(2,1)S(1)} %collective-permute-done.1.refs_1_, ...), custom_call_target="tpu_custom_call" | custom-call | flops 300000000 | bytes 2800000 | tf_op jit(solution)/shard_map/pallas_call | solution.py:337
  70.4 6.3 %all-to-all-start.3 = ((bf16[8,16,1280]{2,1,0:T(8,128)(2,1)}), bf16[8,16,1280]{2,1,0:T(8,128)(2,1)S(1)}, u32[]{:S(2)}, u32[]{:S(2)}) async-start(bf16[8,16,1280]{2,1,0:T(8,128)(2,1)} %shard_map.124), calls=%async_computation.3 | async-start | bytes 655360 | tf_op jit(solution)/shard_map/all_to_all | solution.py:251
  76.7 3.2 %collective-permute-start.7 = (bf16[112,576]{1,0:T(8,128)(2,1)S(1)}, bf16[112,576]{1,0:T(8,128)(2,1)S(1)}, u32[]{:S(2)}, u32[]{:S(2)}) collective-permute-start(bf16[112,576]{1,0:T(8,128)(2,1)S(1)} %copy-done.10), channel_id=1, source_target_pairs={{0,32},{32,0},{1,33},{33,1},{2,34},{34,2},{3,35},{35,3},{4,36},{36... | collective-permute-start | bytes 387080 | tf_op jit(solution)/shard_map/ppermute | solution.py:247
  79.9 2.6 %collective-permute-start.8 = (bf16[112,576]{1,0:T(8,128)(2,1)S(1)}, bf16[112,576]{1,0:T(8,128)(2,1)S(1)}, u32[]{:S(2)}, u32[]{:S(2)}) collective-permute-start(bf16[112,576]{1,0:T(8,128)(2,1)S(1)} %copy-done.8), channel_id=1, source_target_pairs={{0,16},{16,0},{1,17},{17,1},{2,18},{18,2},{3,19},{19,3},{4,20},{20... | collective-permute-start | bytes 387080 | tf_op jit(solution)/shard_map/ppermute | solution.py:247
  82.6 3.5 %collective-permute-done.7.w2 = bf16[112,576]{1,0:T(8,128)(2,1)S(1)} collective-permute-done((bf16[112,576]{1,0:T(8,128)(2,1)S(1)}, bf16[112,576]{1,0:T(8,128)(2,1)S(1)}, u32[]{:S(2)}, u32[]{:S(2)}) %collective-permute-start.7) | collective-permute-done | bytes 129056 | tf_op jit(solution)/shard_map/ppermute | solution.py:247
  86.1 0.9 collective-permute-done.8.w1
  86.9 1.0 all-to-all-done.3.part_ref
  87.9 0.9 shard_map.125
  88.8 6.2 %all-to-all-start.4 = ((bf16[8,16,576]{2,1,0:T(8,128)(2,1)}), bf16[8,16,576]{2,1,0:T(8,128)(2,1)S(1)}, u32[]{:S(2)}, u32[]{:S(2)}) async-start(bf16[8,16,576]{2,1,0:T(8,128)(2,1)} %shard_map.125), calls=%async_computation.4 | async-start | bytes 327680 | tf_op jit(solution)/shard_map/all_to_all | solution.py:251
  95.0 3.9 %collective-permute-start.10 = (bf16[112,576]{1,0:T(8,128)(2,1)S(1)}, bf16[112,576]{1,0:T(8,128)(2,1)S(1)}, u32[]{:S(2)}, u32[]{:S(2)}) collective-permute-start(bf16[112,576]{1,0:T(8,128)(2,1)S(1)} %copy-done.6), channel_id=1, source_target_pairs={{0,48},{16,32},{32,16},{48,0},{1,49},{17,33},{33,17},{49,1},{2,50}... | collective-permute-start | bytes 387080 | tf_op jit(solution)/shard_map/ppermute | solution.py:255
  98.9 1.9 %collective-permute-start.9 = (f32[16,128]{1,0:T(8,128)S(1)}, f32[16,128]{1,0:T(8,128)S(1)}, u32[]{:S(2)}, u32[]{:S(2)}) collective-permute-start(f32[16,128]{1,0:T(8,128)S(1)} %slice.22), channel_id=1, source_target_pairs={{0,8},{8,0},{1,9},{9,1},{2,10},{10,2},{3,11},{11,3},{4,12},{12,4},... | collective-permute-start | bytes 24584 | tf_op jit(solution)/shard_map/ppermute | solution.py:247
  100.9 1.1 collective-permute-done.9.across_ref
  102.0 1.2 collective-permute-done.10.w3
  103.2 1.2 all-to-all-done.4.own_ref
  104.5 1.9 %collective-permute-start.11 = (bf16[8,16,576]{2,1,0:T(8,128)(2,1)S(1)}, bf16[8,16,576]{2,1,0:T(8,128)(2,1)S(1)}, u32[]{:S(2)}, u32[]{:S(2)}) collective-permute-start(bf16[8,16,576]{2,1,0:T(8,128)(2,1)S(1)} %all-to-all-done.4.own_ref), channel_id=1, source_target_pairs={{0,8},{8,0},{1,9},{9,1},{2,10},{10,2},{3,11},{11,3},{4,12},{12,4},... | collective-permute-start | bytes 442376 | tf_op jit(solution)/shard_map/ppermute | solution.py:247
  106.4 1.4 %collective-permute-done.11.other_ref = bf16[8,16,576]{2,1,0:T(8,128)(2,1)S(1)} collective-permute-done((bf16[8,16,576]{2,1,0:T(8,128)(2,1)S(1)}, bf16[8,16,576]{2,1,0:T(8,128)(2,1)S(1)}, u32[]{:S(2)}, u32[]{:S(2)}) %collective-permute-start.11) | collective-permute-done | bytes 147488 | tf_op jit(solution)/shard_map/ppermute | solution.py:247
  107.7 1.5 %shard_map.126 = bf16[32,32,128]{2,1,0:T(8,128)(2,1)S(1)} custom-call(s32[1]{0:T(128)} %bitcast.xh_ref, s32[1]{0:T(128)} %bitcast.1.xl_ref, s32[1]{0:T(128)} %bitcast.2.y_ref, bf16[8,16,576]{2,1,0:T(8,128)(2,1)S(1)} %all-to-all-done.4.own_ref, bf16[8,16,576]{2,1,0:T(8,128)(2,1)S(1)} %collective-permute-done.11.other_ref, ...), custom_call_target="tpu_custom_call" | custom-call | flops 200000000 | bytes 1600000 | tf_op jit(solution)/shard_map/pallas_call | solution.py:350
  109.2 19.1 %all_to_all.30 = bf16[32,32,128]{2,1,0:T(8,128)(2,1)S(1)} all-to-all(bf16[32,32,128]{2,1,0:T(8,128)(2,1)S(1)} %shard_map.126), channel_id=1, replica_groups=mesh['z'=8,'xh'=2,'xl'=2,'c'=2,'y'=8] {'xh','xl','y'}, dimensions={0} | all-to-all | bytes 524288 | tf_op jit(solution)/shard_map/all_to_all | solution.py:251
  128.4 0.7 slice_reduce_fusion
  (31 shorter events, 0.1 us)
Async XLA Ops:
  0.7 17.2 %copy-start.12 = (bf16[112]{0:T(256)(128)(2,1)S(1)}, bf16[112]{0:T(256)(128)(2,1)}, u32[]{:S(2)}) copy-start(bf16[112]{0:T(256)(128)(2,1)} %param.20) | copy-start | bytes 676
  0.7 17.2 %copy-start = (bf16[2048,112]{0,1:T(8,128)(2,1)S(1)}, bf16[2048,112]{0,1:T(8,128)(2,1)}, u32[]{:S(2)}) copy-start(bf16[2048,112]{0,1:T(8,128)(2,1)} %param.18) | copy-start | bytes 1376260
  0.7 17.2 %copy-start.1 = (bf16[112,2304]{1,0:T(8,128)(2,1)S(1)}, bf16[112,2304]{1,0:T(8,128)(2,1)}, u32[]{:S(2)}) copy-start(bf16[112,2304]{1,0:T(8,128)(2,1)} %gate_ref) | copy-start | bytes 1548292
  0.7 17.2 %copy-start.2 = (bf16[112,2304]{1,0:T(8,128)(2,1)S(1)}, bf16[112,2304]{1,0:T(8,128)(2,1)}, u32[]{:S(2)}) copy-start(bf16[112,2304]{1,0:T(8,128)(2,1)} %up_ref) | copy-start | bytes 1548292
  0.7 17.2 %copy-start.4 = (bf16[256,112]{0,1:T(8,128)(2,1)S(1)}, bf16[256,112]{0,1:T(8,128)(2,1)}, u32[]{:S(2)}) copy-start(bf16[256,112]{0,1:T(8,128)(2,1)} %param.19) | copy-start | bytes 172036
  4.6 31.0 %all-to-all-start = ((bf16[32,16,512]{2,1,0:T(8,128)(2,1)}), bf16[32,16,512]{2,1,0:T(8,128)(2,1)S(1)}, u32[]{:S(2)}, u32[]{:S(2)}) async-start(bf16[32,16,512]{2,1,0:T(8,128)(2,1)} %shard_map.118), calls=%async_computation | async-start | bytes 1048576 | tf_op jit(solution)/shard_map/all_to_all | solution.py:251
  17.8 28.0 %copy-start.11 = (s32[64]{0:T(128)S(1)}, s32[64]{0:T(128)}, u32[]{:S(2)}) copy-start(s32[64]{0:T(128)} %param.16) | copy-start | bytes 772
  19.3 16.3 %collective-permute-start = (bf16[112,2432]{1,0:T(8,128)(2,1)S(1)}, bf16[112,2432]{1,0:T(8,128)(2,1)S(1)}, u32[]{:S(2)}, u32[]{:S(2)}) collective-permute-start(bf16[112,2432]{1,0:T(8,128)(2,1)S(1)} %get-tuple-element.69.own_ref), channel_id=1, source_target_pairs={{0,8},{8,0},{1,9},{9,1},{2,10},{10,2},{3,11},{11,3},{4,12},{12,4},... | collective-permute-start | bytes 1634312 | tf_op jit(solution)/shard_map/ppermute | solution.py:247
  21.2 24.7 %collective-permute-start.1 = (bf16[112,1152]{1,0:T(8,128)(2,1)}, bf16[112,1152]{1,0:T(8,128)(2,1)S(1)}, u32[]{:S(2)}, u32[]{:S(2)}) collective-permute-start(bf16[112,1152]{1,0:T(8,128)(2,1)} %get-tuple-element.80), channel_id=1, source_target_pairs={{0,16},{16,0},{1,17},{17,1},{2,18},{18,2},{3,19},{19,3},{4,20},{20... | collective-permute-start | bytes 774152 | tf_op jit(solution)/shard_map/ppermute | solution.py:247
  25.0 21.0 %collective-permute-start.2 = (bf16[112,1152]{1,0:T(8,128)(2,1)}, bf16[112,1152]{1,0:T(8,128)(2,1)S(1)}, u32[]{:S(2)}, u32[]{:S(2)}) collective-permute-start(bf16[112,1152]{1,0:T(8,128)(2,1)} %get-tuple-element.81), channel_id=1, source_target_pairs={{0,32},{32,0},{1,33},{33,1},{2,34},{34,2},{3,35},{35,3},{4,36},{36... | collective-permute-start | bytes 774152 | tf_op jit(solution)/shard_map/ppermute | solution.py:247
  29.5 16.9 %collective-permute-start.3 = (bf16[112,1152]{1,0:T(8,128)(2,1)S(1)}, bf16[112,1152]{1,0:T(8,128)(2,1)S(1)}, u32[]{:S(2)}, u32[]{:S(2)}) collective-permute-start(bf16[112,1152]{1,0:T(8,128)(2,1)S(1)} %get-tuple-element.82), channel_id=1, source_target_pairs={{0,48},{16,32},{32,16},{48,0},{1,49},{17,33},{33,17},{49,1},{2,50}... | collective-permute-start | bytes 774152 | tf_op jit(solution)/shard_map/ppermute | solution.py:255
  36.7 14.5 %all-to-all-start.1 = ((bf16[8,32,128]{2,1,0:T(8,128)(2,1)}), bf16[8,32,128]{2,1,0:T(8,128)(2,1)S(1)}, u32[]{:S(2)}, u32[]{:S(2)}) async-start(bf16[8,32,128]{2,1,0:T(8,128)(2,1)} %shard_map.120), calls=%async_computation.1 | async-start | bytes 131072 | tf_op jit(solution)/shard_map/all_to_all | solution.py:251
  44.3 1.0 copy-start.3
  45.7 1.7 %copy-start.5 = (bf16[112,576]{1,0:T(8,128)(2,1)}, bf16[112,576]{1,0:T(8,128)(2,1)S(1)}, u32[]{:S(2)}) copy-start(bf16[112,576]{1,0:T(8,128)(2,1)S(1)} %get-tuple-element.109) | copy-start | bytes 387076
  45.7 1.7 %copy-start.7 = (bf16[112,576]{1,0:T(8,128)(2,1)}, bf16[112,576]{1,0:T(8,128)(2,1)S(1)}, u32[]{:S(2)}) copy-start(bf16[112,576]{1,0:T(8,128)(2,1)S(1)} %get-tuple-element.104) | copy-start | bytes 387076
  45.7 6.5 %copy-start.9 = (bf16[112,576]{1,0:T(8,128)(2,1)}, bf16[112,576]{1,0:T(8,128)(2,1)S(1)}, u32[]{:S(2)}) copy-start(bf16[112,576]{1,0:T(8,128)(2,1)S(1)} %get-tuple-element.103) | copy-start | bytes 387076
  52.2 27.7 %copy-start.8 = (bf16[112,576]{1,0:T(8,128)(2,1)S(1)}, bf16[112,576]{1,0:T(8,128)(2,1)}, u32[]{:S(2)}) copy-start(bf16[112,576]{1,0:T(8,128)(2,1)} %copy-done.7) | copy-start | bytes 387076
  52.2 24.5 %copy-start.10 = (bf16[112,576]{1,0:T(8,128)(2,1)S(1)}, bf16[112,576]{1,0:T(8,128)(2,1)}, u32[]{:S(2)}) copy-start(bf16[112,576]{1,0:T(8,128)(2,1)} %copy-done.9) | copy-start | bytes 387076
  52.2 16.8 %all-to-all-start.2 = ((bf16[32,32,128]{2,1,0:T(8,128)(2,1)}), bf16[32,32,128]{2,1,0:T(8,128)(2,1)S(1)}, u32[]{:S(2)}, u32[]{:S(2)}) async-start(bf16[32,32,128]{2,1,0:T(8,128)(2,1)} %get-tuple-element.89), calls=%async_computation.2 | async-start | bytes 524288 | tf_op jit(solution)/shard_map/all_to_all | solution.py:251
  58.0 37.0 %copy-start.6 = (bf16[112,576]{1,0:T(8,128)(2,1)S(1)}, bf16[112,576]{1,0:T(8,128)(2,1)}, u32[]{:S(2)}) copy-start(bf16[112,576]{1,0:T(8,128)(2,1)} %copy-done.5) | copy-start | bytes 387076
  58.0 6.4 %collective-permute-start.4 = (bf16[112,1536]{1,0:T(8,128)(2,1)}, bf16[112,1536]{1,0:T(8,128)(2,1)S(1)}, u32[]{:S(2)}, u32[]{:S(2)}) collective-permute-start(bf16[112,1536]{1,0:T(8,128)(2,1)} %get-tuple-element.98), channel_id=1, source_target_pairs={{0,8},{8,0},{1,9},{9,1},{2,10},{10,2},{3,11},{11,3},{4,12},{12,4},... | collective-permute-start | bytes 1032200 | tf_op jit(solution)/shard_map/ppermute | solution.py:247
  60.1 4.4 %collective-permute-start.5 = (bf16[112,1536]{1,0:T(8,128)(2,1)}, bf16[112,1536]{1,0:T(8,128)(2,1)S(1)}, u32[]{:S(2)}, u32[]{:S(2)}) collective-permute-start(bf16[112,1536]{1,0:T(8,128)(2,1)} %pad_maximum_fusion.1), channel_id=1, source_target_pairs={{0,8},{8,0},{1,9},{9,1},{2,10},{10,2},{3,11},{11,3},{4,12},{12,4},... | collective-permute-start | bytes 1032200 | tf_op jit(solution)/shard_map/ppermute | solution.py:247
  62.5 3.8 %collective-permute-start.6 = (bf16[112,1536]{1,0:T(8,128)(2,1)}, bf16[112,1536]{1,0:T(8,128)(2,1)S(1)}, u32[]{:S(2)}, u32[]{:S(2)}) collective-permute-start(bf16[112,1536]{1,0:T(8,128)(2,1)} %get-tuple-element.100), channel_id=1, source_target_pairs={{0,8},{8,0},{1,9},{9,1},{2,10},{10,2},{3,11},{11,3},{4,12},{12,4},... | collective-permute-start | bytes 1032200 | tf_op jit(solution)/shard_map/ppermute | solution.py:247
  70.4 17.5 %all-to-all-start.3 = ((bf16[8,16,1280]{2,1,0:T(8,128)(2,1)}), bf16[8,16,1280]{2,1,0:T(8,128)(2,1)S(1)}, u32[]{:S(2)}, u32[]{:S(2)}) async-start(bf16[8,16,1280]{2,1,0:T(8,128)(2,1)} %shard_map.124), calls=%async_computation.3 | async-start | bytes 655360 | tf_op jit(solution)/shard_map/all_to_all | solution.py:251
  76.7 9.3 %collective-permute-start.7 = (bf16[112,576]{1,0:T(8,128)(2,1)S(1)}, bf16[112,576]{1,0:T(8,128)(2,1)S(1)}, u32[]{:S(2)}, u32[]{:S(2)}) collective-permute-start(bf16[112,576]{1,0:T(8,128)(2,1)S(1)} %copy-done.10), channel_id=1, source_target_pairs={{0,32},{32,0},{1,33},{33,1},{2,34},{34,2},{3,35},{35,3},{4,36},{36... | collective-permute-start | bytes 387080 | tf_op jit(solution)/shard_map/ppermute | solution.py:247
  79.9 7.0 %collective-permute-start.8 = (bf16[112,576]{1,0:T(8,128)(2,1)S(1)}, bf16[112,576]{1,0:T(8,128)(2,1)S(1)}, u32[]{:S(2)}, u32[]{:S(2)}) collective-permute-start(bf16[112,576]{1,0:T(8,128)(2,1)S(1)} %copy-done.8), channel_id=1, source_target_pairs={{0,16},{16,0},{1,17},{17,1},{2,18},{18,2},{3,19},{19,3},{4,20},{20... | collective-permute-start | bytes 387080 | tf_op jit(solution)/shard_map/ppermute | solution.py:247
  88.8 15.7 %all-to-all-start.4 = ((bf16[8,16,576]{2,1,0:T(8,128)(2,1)}), bf16[8,16,576]{2,1,0:T(8,128)(2,1)S(1)}, u32[]{:S(2)}, u32[]{:S(2)}) async-start(bf16[8,16,576]{2,1,0:T(8,128)(2,1)} %shard_map.125), calls=%async_computation.4 | async-start | bytes 327680 | tf_op jit(solution)/shard_map/all_to_all | solution.py:251
  95.0 8.2 %collective-permute-start.10 = (bf16[112,576]{1,0:T(8,128)(2,1)S(1)}, bf16[112,576]{1,0:T(8,128)(2,1)S(1)}, u32[]{:S(2)}, u32[]{:S(2)}) collective-permute-start(bf16[112,576]{1,0:T(8,128)(2,1)S(1)} %copy-done.6), channel_id=1, source_target_pairs={{0,48},{16,32},{32,16},{48,0},{1,49},{17,33},{33,17},{49,1},{2,50}... | collective-permute-start | bytes 387080 | tf_op jit(solution)/shard_map/ppermute | solution.py:255
  98.9 3.1 %collective-permute-start.9 = (f32[16,128]{1,0:T(8,128)S(1)}, f32[16,128]{1,0:T(8,128)S(1)}, u32[]{:S(2)}, u32[]{:S(2)}) collective-permute-start(f32[16,128]{1,0:T(8,128)S(1)} %slice.22), channel_id=1, source_target_pairs={{0,8},{8,0},{1,9},{9,1},{2,10},{10,2},{3,11},{11,3},{4,12},{12,4},... | collective-permute-start | bytes 24584 | tf_op jit(solution)/shard_map/ppermute | solution.py:247
  104.5 3.3 %collective-permute-start.11 = (bf16[8,16,576]{2,1,0:T(8,128)(2,1)S(1)}, bf16[8,16,576]{2,1,0:T(8,128)(2,1)S(1)}, u32[]{:S(2)}, u32[]{:S(2)}) collective-permute-start(bf16[8,16,576]{2,1,0:T(8,128)(2,1)S(1)} %all-to-all-done.4.own_ref), channel_id=1, source_target_pairs={{0,8},{8,0},{1,9},{9,1},{2,10},{10,2},{3,11},{11,3},{4,12},{12,4},... | collective-permute-start | bytes 442376 | tf_op jit(solution)/shard_map/ppermute | solution.py:247

commit v6 on v5

--- a/solution.py
+++ b/solution.py
@@ -91,7 +91,7 @@
     return 2 * (xh_ref[0] ^ (r >> 1)) + (xl_ref[0] ^ (r & 1))
 
 
-def pack_kernel(xh_ref, xl_ref, gate_ref, up_ref, proj_ref, residual_ref, gain_ref, carry_ref, *outs):
+def pack_kernel(xh_ref, xl_ref, gate_ref, up_ref, down_ref, proj_ref, residual_ref, gain_ref, carry_ref, *outs):
     carry_ref[:, :2048] = proj_ref[...]
     carry_ref[:, 2048:2304] = residual_ref[...]
     carry_ref[:, 2304:] = gain_ref[...]
@@ -101,14 +101,16 @@
         for r, out_ref in enumerate(outs):
 
             @pl.when(target(xh_ref, xl_ref, r) == i)
-            def _(out_ref=out_ref, block=block):
-                out_ref[...] = block
+            def _(out_ref=out_ref, block=block, down=down_ref[:, cut] if r == 1 else None):
+                out_ref[:, : 2 * SIZE] = block
+                if down is not None:
+                    out_ref[:, 2 * SIZE :] = down
 
 
 def pack_down_kernel(xh_ref, xl_ref, down_ref, *outs):
     for i in range(4):
         block = down_ref[:, i * SIZE : (i + 1) * SIZE]
-        for r, out_ref in enumerate(outs):
+        for r, out_ref in zip((0, 2, 3), outs):
 
             @pl.when(target(xh_ref, xl_ref, r) == i)
             def _(out_ref=out_ref, block=block):
@@ -230,7 +232,7 @@
     none = jnp.zeros((128 - WIDTH, SIZE), BF)
     nt = (((1,), (1,)), ((), ()))
     for r, w in enumerate((w0, w1, w2, w3)):
-        wide = jnp.concatenate([w[...], none], axis=0)
+        wide = jnp.concatenate([w[:, w.shape[1] - SIZE :], none], axis=0)
         part = lax.dot_general(units, wide, nt, preferred_element_type=F32)
         if r == 0:
             total[...] = part
@@ -295,12 +297,13 @@
     gains = jnp.broadcast_to(norm_gain[:, None], (WIDTH, 128))
     carry, *ff = call(
         pack_kernel,
-        [SMEM] * 2 + [VMEM] * 5,
-        [shape((WIDTH, 2048 + 256 + 128))] + [shape((WIDTH, 2 * SIZE))] * 4,
+        [SMEM] * 2 + [VMEM] * 6,
+        [shape((WIDTH, 2048 + 256 + 128))]
+        + [shape((WIDTH, n * SIZE)) for n in (2, 3, 2, 2)],
         (),
         0,
         3_200_000,
-    )(xh, xl, w_gate, w_up, out_proj, residual, gains)
+    )(xh, xl, w_gate, w_up, w_down, out_proj, residual, gains)
     carry_other = swap(carry)
     ff = [ff[0], swap(ff[1], "xl"), swap(ff[2], "xh"), diagonal(ff[3])]
     rows, ff[0] = lax.optimization_barrier((rows, ff[0]))
@@ -317,13 +320,13 @@
         rows_kernel, [SMEM, SMEM, VMEM], [shape((16, 256)), shape((256, 256))], (), 0, 200_000
     )(core, tp, slot_of[None])
     down = call(
-        pack_down_kernel, [SMEM, SMEM, VMEM], [shape((WIDTH, SIZE))] * 4, (), 0, 1_000_000
+        pack_down_kernel, [SMEM, SMEM, VMEM], [shape((WIDTH, SIZE))] * 3, (), 0, 1_000_000
     )(xh, xl, w_down)
     _, _, ff = lax.optimization_barrier((pick, down, ff))
     joined = jnp.concatenate
     thirds = [
         joined([ff[0], ff[1][:, :384]], axis=1),
-        joined([ff[1][:, 384:], ff[2][:, :768]], axis=1),
+        joined([ff[1][:, 384 : 2 * SIZE], ff[2][:, :768]], axis=1),
         joined([ff[2][:, 768:], ff[3]], axis=1),
     ]
     part, ff, thirds, down, pick = lax.optimization_barrier(
@@ -337,16 +340,14 @@
     part = call(
         gate_kernel, [SMEM] * 2 + [VMEM] * 8, shape((8, 16, 1280)), (), 300_000_000, 2_800_000
     )(xh, xl, exchange(scaled, ("xh", "xl", "y")), *ff, *ff_other)
-    _, far, near = lax.optimization_barrier((part, down[2], down[1]))
-    part, far, near = lax.optimization_barrier(
-        (exchange(part, "z"), swap(far, "xh"), swap(near, "xl"))
+    _, hidden, far = lax.optimization_barrier((part, hidden, down[1]))
+    part, far, across = lax.optimization_barrier(
+        (exchange(part, "z"), swap(far, "xh"), swap(hidden[16:]))
     )
     units = call(units_kernel, [VMEM], shape((8, 16, SIZE)), (), 0, 500_000)(part)
-    _, hidden, cross = lax.optimization_barrier((units, hidden, down[3]))
-    units, across, cross = lax.optimization_barrier(
-        (exchange(units, "z"), swap(hidden[16:]), diagonal(cross))
-    )
-    down = (down[0], near, far, cross)
+    _, cross = lax.optimization_barrier((units, down[2]))
+    units, cross = lax.optimization_barrier((exchange(units, "z"), diagonal(cross)))
+    down = (down[0], ff[1], far, cross)
     part = call(
         down_kernel,
         [SMEM] * 3 + [VMEM] * 9,

time: 130 us -> 131 us (level)
  starting transfers between devices: 71.3 us -> 65.8 us
  waiting for transfers between devices: 22.3 us -> 27.1 us
  blocking collectives: 19.1 us -> 20.6 us
  Pallas kernels: 11.6 us -> 13 us
    ppermute x2, waiting for transfers between devices: 1.73 us -> 6.38 us  [diagonal(): return lax.ppermute(value, ('xh', 'xl'), [(i, 3 - i) for i in range(4)])]
    ppermute x10 -> x9, starting transfers between devices: 26.2 us -> 23.4 us  [swap(): return lax.ppermute(value, axis, [(0, 1), (1, 0)])]
    all_to_all x5, starting transfers between devices: 39 us -> 37.2 us  [exchange(): return lax.all_to_all(blocks, axes, 0, 0, tiled=True)]
    all_to_all x1, blocking collectives: 19.1 us -> 20.6 us  [exchange(): return lax.all_to_all(blocks, axes, 0, 0, tiled=True)]
    all_to_all x5, waiting for transfers between devices: 11.9 us -> 13.2 us  [exchange(): return lax.all_to_all(blocks, axes, 0, 0, tiled=True)]
    ppermute x10 -> x9, waiting for transfers between devices: 8.69 us -> 7.46 us  [swap(): return lax.ppermute(value, axis, [(0, 1), (1, 0)])]
  transfers between devices with their start and end apart: 17 -> 16, of which waited for: 12 -> 12; matrix products, arithmetic and copies ran while one was open for 1% -> 1% of each run, Pallas kernels for 2% -> 3%
where the time goes in v6:
time: 131 us; the launch traced here: 130 us
  starting transfers between devices  65.8 us (50%)
  waiting for transfers between devices  27.1 us (21%)
  blocking collectives  20.6 us (16%)
  Pallas kernels  13 us (10%)
  other arithmetic  2.37 us (2%)
    all_to_all x5, starting transfers between devices, exchange(): return lax.all_to_all(blocks, axes, 0, 0, tiled=True)  37.2 us
    ppermute x9, starting transfers between devices, swap(): return lax.ppermute(value, axis, [(0, 1), (1, 0)])  23.4 us
    all_to_all x1, blocking collectives, exchange(): return lax.all_to_all(blocks, axes, 0, 0, tiled=True)  20.6 us
    all_to_all x5, waiting for transfers between devices, exchange(): return lax.all_to_all(blocks, axes, 0, 0, tiled=True)  13.2 us
    ppermute x9, waiting for transfers between devices, swap(): return lax.ppermute(value, axis, [(0, 1), (1, 0)])  7.46 us
    ppermute x2, waiting for transfers between devices, diagonal(): return lax.ppermute(value, ('xh', 'xl'), [(i, 3 - i) for i in range(4)])  6.38 us
    ppermute x2, starting transfers between devices, diagonal(): return lax.ppermute(value, ('xh', 'xl'), [(i, 3 - i) for i in range(4)])  5.28 us
    pallas_call x1, Pallas kernels, local(): call(attention_kernel, [SMEM, HBM, VMEM, HBM, HBM], shape((32, 16, 512)),...  3.91 us
  transfers between devices with their start and end apart: 16, of which 12 were waited for; matrix products, arithmetic and copies ran while one was open for 1% of the time, Pallas kernels for 3%

profile of v6, /device:TPU:8, one launch (start us, length us, event | category | flops | bytes accessed | tf_op | source)
XLA Modules:
  0.0 130.0 jit_solution(8163171340170238061)
XLA Ops:
  0.7 3.9 %shard_map.118 = bf16[32,16,512]{2,1,0:T(8,128)(2,1)} custom-call(s32[1]{0:T(128)S(6)} %copy.13.len_ref, bf16[64,576]{1,0:T(8,128)(2,1)} %bitcast.20, bf16[4,576]{1,0:T(4,128)(2,1)} %bitcast.21, bf16[576,512]{1,0:T(8,128)(2,1)} %bitcast.19, bf16[16,512,128]{2,1,0:T(8,128)(2,1)} %maps_ref.1), custom_call_target="tpu_custom_call" | custom-call | flops 200000000 | bytes 4000000 | tf_op jit(solution)/shard_map/pallas_call | solution.py:276
  4.6 13.2 %all-to-all-start = ((bf16[32,16,512]{2,1,0:T(8,128)(2,1)}), bf16[32,16,512]{2,1,0:T(8,128)(2,1)S(1)}, u32[]{:S(2)}, u32[]{:S(2)}) async-start(bf16[32,16,512]{2,1,0:T(8,128)(2,1)} %shard_map.118), calls=%async_computation | async-start | bytes 1048576 | tf_op jit(solution)/shard_map/all_to_all | solution.py:253
  17.8 0.1 broadcast_in_dim.24.gain_ref
  18.0 0.0 copy-start.5
  18.0 1.8 %shard_map.119 = (bf16[112,2432]{1,0:T(8,128)(2,1)}, bf16[112,1152]{1,0:T(8,128)(2,1)S(1)}, bf16[112,1728]{1,0:T(8,128)(2,1)}, bf16[112,1152]{1,0:T(8,128)(2,1)}, bf16[112,1152]{1,0:T(8,128)(2,1)}) custom-call(s32[1]{0:T(128)} %bitcast.xh_ref, s32[1]{0:T(128)} %bitcast.1.xl_ref, bf16[112,2304]{1,0:T(8,128)(2,1)S(1)} %copy-done.2, ...), custom_call_target="tpu_custom_call" | custom-call | bytes 3200000 | tf_op jit(solution)/shard_map/pallas_call | solution.py:298
  19.8 1.9 %collective-permute-start = (bf16[112,2432]{1,0:T(8,128)(2,1)}, bf16[112,2432]{1,0:T(8,128)(2,1)S(1)}, u32[]{:S(2)}, u32[]{:S(2)}) collective-permute-start(bf16[112,2432]{1,0:T(8,128)(2,1)} %get-tuple-element.66.own_ref), channel_id=1, source_target_pairs={{0,8},{8,0},{1,9},{9,1},{2,10},{10,2},{3,11},{11,3},{4,12},{12,4},... | collective-permute-start | bytes 1634312 | tf_op jit(solution)/shard_map/ppermute | solution.py:249
  21.7 3.6 %collective-permute-start.1 = (bf16[112,1728]{1,0:T(8,128)(2,1)}, bf16[112,1728]{1,0:T(8,128)(2,1)S(1)}, u32[]{:S(2)}, u32[]{:S(2)}) collective-permute-start(bf16[112,1728]{1,0:T(8,128)(2,1)} %get-tuple-element.75), channel_id=1, source_target_pairs={{0,16},{16,0},{1,17},{17,1},{2,18},{18,2},{3,19},{19,3},{4,20},{20... | collective-permute-start | bytes 1161224 | tf_op jit(solution)/shard_map/ppermute | solution.py:249
  25.3 4.6 %collective-permute-start.2 = (bf16[112,1152]{1,0:T(8,128)(2,1)}, bf16[112,1152]{1,0:T(8,128)(2,1)S(1)}, u32[]{:S(2)}, u32[]{:S(2)}) collective-permute-start(bf16[112,1152]{1,0:T(8,128)(2,1)} %get-tuple-element.76), channel_id=1, source_target_pairs={{0,32},{32,0},{1,33},{33,1},{2,34},{34,2},{3,35},{35,3},{4,36},{36... | collective-permute-start | bytes 774152 | tf_op jit(solution)/shard_map/ppermute | solution.py:249
  29.9 2.2 %collective-permute-start.3 = (bf16[112,1152]{1,0:T(8,128)(2,1)}, bf16[112,1152]{1,0:T(8,128)(2,1)S(1)}, u32[]{:S(2)}, u32[]{:S(2)}) collective-permute-start(bf16[112,1152]{1,0:T(8,128)(2,1)} %get-tuple-element.77), channel_id=1, source_target_pairs={{0,48},{16,32},{32,16},{48,0},{1,49},{17,33},{33,17},{49,1},{2,50}... | collective-permute-start | bytes 774152 | tf_op jit(solution)/shard_map/ppermute | solution.py:257
  32.2 3.4 %all-to-all-done.x_ref = bf16[32,16,512]{2,1,0:T(8,128)(2,1)S(1)} async-done(((bf16[32,16,512]{2,1,0:T(8,128)(2,1)}), bf16[32,16,512]{2,1,0:T(8,128)(2,1)S(1)}, u32[]{:S(2)}, u32[]{:S(2)}) %all-to-all-start) | async-done | bytes 524320 | tf_op jit(solution)/shard_map/all_to_all | solution.py:253
  35.5 0.0 collective-permute-done.other_ref
  35.5 1.2 shard_map.120
  36.7 7.5 %all-to-all-start.1 = ((bf16[8,32,128]{2,1,0:T(8,128)(2,1)}), bf16[8,32,128]{2,1,0:T(8,128)(2,1)S(1)}, u32[]{:S(2)}, u32[]{:S(2)}) async-start(bf16[8,32,128]{2,1,0:T(8,128)(2,1)} %shard_map.120), calls=%async_computation.1 | async-start | bytes 131072 | tf_op jit(solution)/shard_map/all_to_all | solution.py:253
  44.2 0.2 shard_map.122
  44.5 0.0 copy-done.5
  44.5 0.1 shard_map.121
  44.6 1.0 collective-permute-done.2.refs_2_
  45.6 1.3 collective-permute-done.3.refs_3_
  46.8 0.0 collective-permute-done.1.refs_1_.w1
  46.9 0.9 pad_maximum_fusion
  47.8 0.8 pad_maximum_fusion.1
  48.6 2.5 %all-to-all-done.1.part_ref = bf16[8,32,128]{2,1,0:T(8,128)(2,1)S(1)} async-done(((bf16[8,32,128]{2,1,0:T(8,128)(2,1)}), bf16[8,32,128]{2,1,0:T(8,128)(2,1)S(1)}, u32[]{:S(2)}, u32[]{:S(2)}) %all-to-all-start.1) | async-done | bytes 65568 | tf_op jit(solution)/shard_map/all_to_all | solution.py:253
  51.2 2.1 %shard_map.123 = (bf16[32,32,128]{2,1,0:T(8,128)(2,1)}, f32[32,128]{1,0:T(8,128)S(1)}) custom-call(bf16[8,32,128]{2,1,0:T(8,128)(2,1)S(1)} %all-to-all-done.1.part_ref, bf16[16,256]{1,0:T(8,128)(2,1)S(1)} %get-tuple-element.83.pick_ref, bf16[112,2432]{1,0:T(8,128)(2,1)} %get-tuple-element.66.own_ref, bf16[112,2432]{1,0:T(8,128)(2,1)S(1)} %collective-permute-done.other_ref), custom_call_target="tpu_custom_call" | custom-call | bytes 400000 | tf_op jit(solution)/shard_map/pallas_call | solution.py:335
  53.2 5.3 %all-to-all-start.2 = ((bf16[32,32,128]{2,1,0:T(8,128)(2,1)}), bf16[32,32,128]{2,1,0:T(8,128)(2,1)S(1)}, u32[]{:S(2)}, u32[]{:S(2)}) async-start(bf16[32,32,128]{2,1,0:T(8,128)(2,1)} %get-tuple-element.84), calls=%async_computation.2 | async-start | bytes 524288 | tf_op jit(solution)/shard_map/all_to_all | solution.py:253
  58.5 1.9 %collective-permute-start.4 = (bf16[112,1536]{1,0:T(8,128)(2,1)}, bf16[112,1536]{1,0:T(8,128)(2,1)S(1)}, u32[]{:S(2)}, u32[]{:S(2)}) collective-permute-start(bf16[112,1536]{1,0:T(8,128)(2,1)} %get-tuple-element.93), channel_id=1, source_target_pairs={{0,8},{8,0},{1,9},{9,1},{2,10},{10,2},{3,11},{11,3},{4,12},{12,4},... | collective-permute-start | bytes 1032200 | tf_op jit(solution)/shard_map/ppermute | solution.py:249
  60.5 2.4 %collective-permute-start.5 = (bf16[112,1536]{1,0:T(8,128)(2,1)}, bf16[112,1536]{1,0:T(8,128)(2,1)S(1)}, u32[]{:S(2)}, u32[]{:S(2)}) collective-permute-start(bf16[112,1536]{1,0:T(8,128)(2,1)} %pad_maximum_fusion.1), channel_id=1, source_target_pairs={{0,8},{8,0},{1,9},{9,1},{2,10},{10,2},{3,11},{11,3},{4,12},{12,4},... | collective-permute-start | bytes 1032200 | tf_op jit(solution)/shard_map/ppermute | solution.py:249
  62.9 1.9 %collective-permute-start.6 = (bf16[112,1536]{1,0:T(8,128)(2,1)}, bf16[112,1536]{1,0:T(8,128)(2,1)S(1)}, u32[]{:S(2)}, u32[]{:S(2)}) collective-permute-start(bf16[112,1536]{1,0:T(8,128)(2,1)} %get-tuple-element.95), channel_id=1, source_target_pairs={{0,8},{8,0},{1,9},{9,1},{2,10},{10,2},{3,11},{11,3},{4,12},{12,4},... | collective-permute-start | bytes 1032200 | tf_op jit(solution)/shard_map/ppermute | solution.py:249
  64.8 0.0 collective-permute-done.4.refs_4_
  64.8 0.0 collective-permute-done.5.refs_5_
  64.8 1.8 %collective-permute-done.6.refs_6_ = bf16[112,1536]{1,0:T(8,128)(2,1)S(1)} collective-permute-done((bf16[112,1536]{1,0:T(8,128)(2,1)}, bf16[112,1536]{1,0:T(8,128)(2,1)S(1)}, u32[]{:S(2)}, u32[]{:S(2)}) %collective-permute-start.6) | collective-permute-done | bytes 344096 | tf_op jit(solution)/shard_map/ppermute | solution.py:249
  66.6 3.4 %all-to-all-done.2.full_ref = bf16[32,32,128]{2,1,0:T(8,128)(2,1)S(1)} async-done(((bf16[32,32,128]{2,1,0:T(8,128)(2,1)}), bf16[32,32,128]{2,1,0:T(8,128)(2,1)S(1)}, u32[]{:S(2)}, u32[]{:S(2)}) %all-to-all-start.2) | async-done | bytes 262176 | tf_op jit(solution)/shard_map/all_to_all | solution.py:253
  70.0 1.3 %shard_map.124 = bf16[8,16,1280]{2,1,0:T(8,128)(2,1)} custom-call(s32[1]{0:T(128)} %bitcast.xh_ref, s32[1]{0:T(128)} %bitcast.1.xl_ref, bf16[32,32,128]{2,1,0:T(8,128)(2,1)S(1)} %all-to-all-done.2.full_ref, bf16[112,1152]{1,0:T(8,128)(2,1)S(1)} %get-tuple-element.85.refs_0_, bf16[112,1728]{1,0:T(8,128)(2,1)S(1)} %collective-permute-done.1.refs_1_.w1, ...), custom_call_target="tpu_custom_call" | custom-call | flops 300000000 | bytes 2800000 | tf_op jit(solution)/shard_map/pallas_call | solution.py:340
  71.3 6.6 %all-to-all-start.3 = ((bf16[8,16,1280]{2,1,0:T(8,128)(2,1)}), bf16[8,16,1280]{2,1,0:T(8,128)(2,1)S(1)}, u32[]{:S(2)}, u32[]{:S(2)}) async-start(bf16[8,16,1280]{2,1,0:T(8,128)(2,1)} %shard_map.124), calls=%async_computation.3 | async-start | bytes 655360 | tf_op jit(solution)/shard_map/all_to_all | solution.py:253
  78.0 3.2 %collective-permute-start.7 = (bf16[112,576]{1,0:T(8,128)(2,1)S(1)}, bf16[112,576]{1,0:T(8,128)(2,1)S(1)}, u32[]{:S(2)}, u32[]{:S(2)}) collective-permute-start(bf16[112,576]{1,0:T(8,128)(2,1)S(1)} %get-tuple-element.98), channel_id=1, source_target_pairs={{0,32},{32,0},{1,33},{33,1},{2,34},{34,2},{3,35},{35,3},{4,36},{36... | collective-permute-start | bytes 387080 | tf_op jit(solution)/shard_map/ppermute | solution.py:249
  81.2 1.9 %collective-permute-start.8 = (f32[16,128]{1,0:T(8,128)S(1)}, f32[16,128]{1,0:T(8,128)S(1)}, u32[]{:S(2)}, u32[]{:S(2)}) collective-permute-start(f32[16,128]{1,0:T(8,128)S(1)} %slice.22), channel_id=1, source_target_pairs={{0,8},{8,0},{1,9},{9,1},{2,10},{10,2},{3,11},{11,3},{4,12},{12,4},... | collective-permute-start | bytes 24584 | tf_op jit(solution)/shard_map/ppermute | solution.py:249
  83.1 1.1 collective-permute-done.8.across_ref
  84.3 2.2 %collective-permute-done.7.w2 = bf16[112,576]{1,0:T(8,128)(2,1)S(1)} collective-permute-done((bf16[112,576]{1,0:T(8,128)(2,1)S(1)}, bf16[112,576]{1,0:T(8,128)(2,1)S(1)}, u32[]{:S(2)}, u32[]{:S(2)}) %collective-permute-start.7) | collective-permute-done | bytes 129056 | tf_op jit(solution)/shard_map/ppermute | solution.py:249
  86.5 2.7 %all-to-all-done.3.part_ref = bf16[8,16,1280]{2,1,0:T(8,128)(2,1)S(1)} async-done(((bf16[8,16,1280]{2,1,0:T(8,128)(2,1)}), bf16[8,16,1280]{2,1,0:T(8,128)(2,1)S(1)}, u32[]{:S(2)}, u32[]{:S(2)}) %all-to-all-start.3) | async-done | bytes 327712 | tf_op jit(solution)/shard_map/all_to_all | solution.py:253
  89.2 0.9 shard_map.125
  90.1 4.5 %all-to-all-start.4 = ((bf16[8,16,576]{2,1,0:T(8,128)(2,1)}), bf16[8,16,576]{2,1,0:T(8,128)(2,1)S(1)}, u32[]{:S(2)}, u32[]{:S(2)}) async-start(bf16[8,16,576]{2,1,0:T(8,128)(2,1)} %shard_map.125), calls=%async_computation.4 | async-start | bytes 327680 | tf_op jit(solution)/shard_map/all_to_all | solution.py:253
  94.6 3.1 %collective-permute-start.9 = (bf16[112,576]{1,0:T(8,128)(2,1)S(1)}, bf16[112,576]{1,0:T(8,128)(2,1)S(1)}, u32[]{:S(2)}, u32[]{:S(2)}) collective-permute-start(bf16[112,576]{1,0:T(8,128)(2,1)S(1)} %get-tuple-element.102), channel_id=1, source_target_pairs={{0,48},{16,32},{32,16},{48,0},{1,49},{17,33},{33,17},{49,1},{2,50}... | collective-permute-start | bytes 387080 | tf_op jit(solution)/shard_map/ppermute | solution.py:257
  97.6 5.1 %collective-permute-done.9.w3 = bf16[112,576]{1,0:T(8,128)(2,1)S(1)} collective-permute-done((bf16[112,576]{1,0:T(8,128)(2,1)S(1)}, bf16[112,576]{1,0:T(8,128)(2,1)S(1)}, u32[]{:S(2)}, u32[]{:S(2)}) %collective-permute-start.9) | collective-permute-done | bytes 129056 | tf_op jit(solution)/shard_map/ppermute | solution.py:257
  102.8 1.2 all-to-all-done.4.own_ref
  104.0 1.9 %collective-permute-start.10 = (bf16[8,16,576]{2,1,0:T(8,128)(2,1)S(1)}, bf16[8,16,576]{2,1,0:T(8,128)(2,1)S(1)}, u32[]{:S(2)}, u32[]{:S(2)}) collective-permute-start(bf16[8,16,576]{2,1,0:T(8,128)(2,1)S(1)} %all-to-all-done.4.own_ref), channel_id=1, source_target_pairs={{0,8},{8,0},{1,9},{9,1},{2,10},{10,2},{3,11},{11,3},{4,12},{12,4},... | collective-permute-start | bytes 442376 | tf_op jit(solution)/shard_map/ppermute | solution.py:249
  105.9 1.4 %collective-permute-done.10.other_ref = bf16[8,16,576]{2,1,0:T(8,128)(2,1)S(1)} collective-permute-done((bf16[8,16,576]{2,1,0:T(8,128)(2,1)S(1)}, bf16[8,16,576]{2,1,0:T(8,128)(2,1)S(1)}, u32[]{:S(2)}, u32[]{:S(2)}) %collective-permute-start.10) | collective-permute-done | bytes 147488 | tf_op jit(solution)/shard_map/ppermute | solution.py:249
  107.3 1.5 %shard_map.126 = bf16[32,32,128]{2,1,0:T(8,128)(2,1)S(1)} custom-call(s32[1]{0:T(128)} %bitcast.xh_ref, s32[1]{0:T(128)} %bitcast.1.xl_ref, s32[1]{0:T(128)} %bitcast.2.y_ref, bf16[8,16,576]{2,1,0:T(8,128)(2,1)S(1)} %all-to-all-done.4.own_ref, bf16[8,16,576]{2,1,0:T(8,128)(2,1)S(1)} %collective-permute-done.10.other_ref, ...), custom_call_target="tpu_custom_call" | custom-call | flops 200000000 | bytes 1600000 | tf_op jit(solution)/shard_map/pallas_call | solution.py:351
  108.8 20.6 %all_to_all.30 = bf16[32,32,128]{2,1,0:T(8,128)(2,1)S(1)} all-to-all(bf16[32,32,128]{2,1,0:T(8,128)(2,1)S(1)} %shard_map.126), channel_id=1, replica_groups=mesh['z'=8,'xh'=2,'xl'=2,'c'=2,'y'=8] {'xh','xl','y'}, dimensions={0} | all-to-all | bytes 524288 | tf_op jit(solution)/shard_map/all_to_all | solution.py:253
  129.4 0.7 slice_reduce_fusion
  (17 shorter events, 0.1 us)
Async XLA Ops:
  0.7 17.2 %copy-start.6 = (bf16[112]{0:T(256)(128)(2,1)S(1)}, bf16[112]{0:T(256)(128)(2,1)}, u32[]{:S(2)}) copy-start(bf16[112]{0:T(256)(128)(2,1)} %param.20) | copy-start | bytes 676
  0.7 17.3 %copy-start = (bf16[2304,112]{0,1:T(8,128)(2,1)S(1)}, bf16[2304,112]{0,1:T(8,128)(2,1)}, u32[]{:S(2)}) copy-start(bf16[2304,112]{0,1:T(8,128)(2,1)} %param.23) | copy-start | bytes 1548292
  0.7 17.3 %copy-start.1 = (bf16[2048,112]{0,1:T(8,128)(2,1)S(1)}, bf16[2048,112]{0,1:T(8,128)(2,1)}, u32[]{:S(2)}) copy-start(bf16[2048,112]{0,1:T(8,128)(2,1)} %param.18) | copy-start | bytes 1376260
  0.7 17.3 %copy-start.2 = (bf16[112,2304]{1,0:T(8,128)(2,1)S(1)}, bf16[112,2304]{1,0:T(8,128)(2,1)}, u32[]{:S(2)}) copy-start(bf16[112,2304]{1,0:T(8,128)(2,1)} %gate_ref) | copy-start | bytes 1548292
  0.7 17.3 %copy-start.3 = (bf16[112,2304]{1,0:T(8,128)(2,1)S(1)}, bf16[112,2304]{1,0:T(8,128)(2,1)}, u32[]{:S(2)}) copy-start(bf16[112,2304]{1,0:T(8,128)(2,1)} %up_ref) | copy-start | bytes 1548292
  0.7 17.3 %copy-start.4 = (bf16[256,112]{0,1:T(8,128)(2,1)S(1)}, bf16[256,112]{0,1:T(8,128)(2,1)}, u32[]{:S(2)}) copy-start(bf16[256,112]{0,1:T(8,128)(2,1)} %param.19) | copy-start | bytes 172036
  4.6 30.9 %all-to-all-start = ((bf16[32,16,512]{2,1,0:T(8,128)(2,1)}), bf16[32,16,512]{2,1,0:T(8,128)(2,1)S(1)}, u32[]{:S(2)}, u32[]{:S(2)}) async-start(bf16[32,16,512]{2,1,0:T(8,128)(2,1)} %shard_map.118), calls=%async_computation | async-start | bytes 1048576 | tf_op jit(solution)/shard_map/all_to_all | solution.py:253
  18.0 26.5 %copy-start.5 = (s32[64]{0:T(128)S(1)}, s32[64]{0:T(128)}, u32[]{:S(2)}) copy-start(s32[64]{0:T(128)} %param.16) | copy-start | bytes 772
  19.8 15.7 %collective-permute-start = (bf16[112,2432]{1,0:T(8,128)(2,1)}, bf16[112,2432]{1,0:T(8,128)(2,1)S(1)}, u32[]{:S(2)}, u32[]{:S(2)}) collective-permute-start(bf16[112,2432]{1,0:T(8,128)(2,1)} %get-tuple-element.66.own_ref), channel_id=1, source_target_pairs={{0,8},{8,0},{1,9},{9,1},{2,10},{10,2},{3,11},{11,3},{4,12},{12,4},... | collective-permute-start | bytes 1634312 | tf_op jit(solution)/shard_map/ppermute | solution.py:249
  21.7 25.1 %collective-permute-start.1 = (bf16[112,1728]{1,0:T(8,128)(2,1)}, bf16[112,1728]{1,0:T(8,128)(2,1)S(1)}, u32[]{:S(2)}, u32[]{:S(2)}) collective-permute-start(bf16[112,1728]{1,0:T(8,128)(2,1)} %get-tuple-element.75), channel_id=1, source_target_pairs={{0,16},{16,0},{1,17},{17,1},{2,18},{18,2},{3,19},{19,3},{4,20},{20... | collective-permute-start | bytes 1161224 | tf_op jit(solution)/shard_map/ppermute | solution.py:249
  25.3 20.2 %collective-permute-start.2 = (bf16[112,1152]{1,0:T(8,128)(2,1)}, bf16[112,1152]{1,0:T(8,128)(2,1)S(1)}, u32[]{:S(2)}, u32[]{:S(2)}) collective-permute-start(bf16[112,1152]{1,0:T(8,128)(2,1)} %get-tuple-element.76), channel_id=1, source_target_pairs={{0,32},{32,0},{1,33},{33,1},{2,34},{34,2},{3,35},{35,3},{4,36},{36... | collective-permute-start | bytes 774152 | tf_op jit(solution)/shard_map/ppermute | solution.py:249
  29.9 16.9 %collective-permute-start.3 = (bf16[112,1152]{1,0:T(8,128)(2,1)}, bf16[112,1152]{1,0:T(8,128)(2,1)S(1)}, u32[]{:S(2)}, u32[]{:S(2)}) collective-permute-start(bf16[112,1152]{1,0:T(8,128)(2,1)} %get-tuple-element.77), channel_id=1, source_target_pairs={{0,48},{16,32},{32,16},{48,0},{1,49},{17,33},{33,17},{49,1},{2,50}... | collective-permute-start | bytes 774152 | tf_op jit(solution)/shard_map/ppermute | solution.py:257
  36.7 14.5 %all-to-all-start.1 = ((bf16[8,32,128]{2,1,0:T(8,128)(2,1)}), bf16[8,32,128]{2,1,0:T(8,128)(2,1)S(1)}, u32[]{:S(2)}, u32[]{:S(2)}) async-start(bf16[8,32,128]{2,1,0:T(8,128)(2,1)} %shard_map.120), calls=%async_computation.1 | async-start | bytes 131072 | tf_op jit(solution)/shard_map/all_to_all | solution.py:253
  53.2 16.8 %all-to-all-start.2 = ((bf16[32,32,128]{2,1,0:T(8,128)(2,1)}), bf16[32,32,128]{2,1,0:T(8,128)(2,1)S(1)}, u32[]{:S(2)}, u32[]{:S(2)}) async-start(bf16[32,32,128]{2,1,0:T(8,128)(2,1)} %get-tuple-element.84), calls=%async_computation.2 | async-start | bytes 524288 | tf_op jit(solution)/shard_map/all_to_all | solution.py:253
  58.5 6.3 %collective-permute-start.4 = (bf16[112,1536]{1,0:T(8,128)(2,1)}, bf16[112,1536]{1,0:T(8,128)(2,1)S(1)}, u32[]{:S(2)}, u32[]{:S(2)}) collective-permute-start(bf16[112,1536]{1,0:T(8,128)(2,1)} %get-tuple-element.93), channel_id=1, source_target_pairs={{0,8},{8,0},{1,9},{9,1},{2,10},{10,2},{3,11},{11,3},{4,12},{12,4},... | collective-permute-start | bytes 1032200 | tf_op jit(solution)/shard_map/ppermute | solution.py:249
  60.5 4.4 %collective-permute-start.5 = (bf16[112,1536]{1,0:T(8,128)(2,1)}, bf16[112,1536]{1,0:T(8,128)(2,1)S(1)}, u32[]{:S(2)}, u32[]{:S(2)}) collective-permute-start(bf16[112,1536]{1,0:T(8,128)(2,1)} %pad_maximum_fusion.1), channel_id=1, source_target_pairs={{0,8},{8,0},{1,9},{9,1},{2,10},{10,2},{3,11},{11,3},{4,12},{12,4},... | collective-permute-start | bytes 1032200 | tf_op jit(solution)/shard_map/ppermute | solution.py:249
  62.9 3.8 %collective-permute-start.6 = (bf16[112,1536]{1,0:T(8,128)(2,1)}, bf16[112,1536]{1,0:T(8,128)(2,1)S(1)}, u32[]{:S(2)}, u32[]{:S(2)}) collective-permute-start(bf16[112,1536]{1,0:T(8,128)(2,1)} %get-tuple-element.95), channel_id=1, source_target_pairs={{0,8},{8,0},{1,9},{9,1},{2,10},{10,2},{3,11},{11,3},{4,12},{12,4},... | collective-permute-start | bytes 1032200 | tf_op jit(solution)/shard_map/ppermute | solution.py:249
  71.3 17.8 %all-to-all-start.3 = ((bf16[8,16,1280]{2,1,0:T(8,128)(2,1)}), bf16[8,16,1280]{2,1,0:T(8,128)(2,1)S(1)}, u32[]{:S(2)}, u32[]{:S(2)}) async-start(bf16[8,16,1280]{2,1,0:T(8,128)(2,1)} %shard_map.124), calls=%async_computation.3 | async-start | bytes 655360 | tf_op jit(solution)/shard_map/all_to_all | solution.py:253
  78.0 8.5 %collective-permute-start.7 = (bf16[112,576]{1,0:T(8,128)(2,1)S(1)}, bf16[112,576]{1,0:T(8,128)(2,1)S(1)}, u32[]{:S(2)}, u32[]{:S(2)}) collective-permute-start(bf16[112,576]{1,0:T(8,128)(2,1)S(1)} %get-tuple-element.98), channel_id=1, source_target_pairs={{0,32},{32,0},{1,33},{33,1},{2,34},{34,2},{3,35},{35,3},{4,36},{36... | collective-permute-start | bytes 387080 | tf_op jit(solution)/shard_map/ppermute | solution.py:249
  81.2 3.1 %collective-permute-start.8 = (f32[16,128]{1,0:T(8,128)S(1)}, f32[16,128]{1,0:T(8,128)S(1)}, u32[]{:S(2)}, u32[]{:S(2)}) collective-permute-start(f32[16,128]{1,0:T(8,128)S(1)} %slice.22), channel_id=1, source_target_pairs={{0,8},{8,0},{1,9},{9,1},{2,10},{10,2},{3,11},{11,3},{4,12},{12,4},... | collective-permute-start | bytes 24584 | tf_op jit(solution)/shard_map/ppermute | solution.py:249
  90.1 13.9 %all-to-all-start.4 = ((bf16[8,16,576]{2,1,0:T(8,128)(2,1)}), bf16[8,16,576]{2,1,0:T(8,128)(2,1)S(1)}, u32[]{:S(2)}, u32[]{:S(2)}) async-start(bf16[8,16,576]{2,1,0:T(8,128)(2,1)} %shard_map.125), calls=%async_computation.4 | async-start | bytes 327680 | tf_op jit(solution)/shard_map/all_to_all | solution.py:253
  94.6 8.2 %collective-permute-start.9 = (bf16[112,576]{1,0:T(8,128)(2,1)S(1)}, bf16[112,576]{1,0:T(8,128)(2,1)S(1)}, u32[]{:S(2)}, u32[]{:S(2)}) collective-permute-start(bf16[112,576]{1,0:T(8,128)(2,1)S(1)} %get-tuple-element.102), channel_id=1, source_target_pairs={{0,48},{16,32},{32,16},{48,0},{1,49},{17,33},{33,17},{49,1},{2,50}... | collective-permute-start | bytes 387080 | tf_op jit(solution)/shard_map/ppermute | solution.py:257
  104.0 3.3 %collective-permute-start.10 = (bf16[8,16,576]{2,1,0:T(8,128)(2,1)S(1)}, bf16[8,16,576]{2,1,0:T(8,128)(2,1)S(1)}, u32[]{:S(2)}, u32[]{:S(2)}) collective-permute-start(bf16[8,16,576]{2,1,0:T(8,128)(2,1)S(1)} %all-to-all-done.4.own_ref), channel_id=1, source_target_pairs={{0,8},{8,0},{1,9},{9,1},{2,10},{10,2},{3,11},{11,3},{4,12},{12,4},... | collective-permute-start | bytes 442376 | tf_op jit(solution)/shard_map/ppermute | solution.py:249

commit v7 on v6

--- a/solution.py
+++ b/solution.py
@@ -164,8 +164,8 @@
     nt = (((1,), (1,)), ((), ()))
     pick = pick_ref[...]
     unit = (lax.broadcasted_iota(jnp.int32, (16, 128), 1) == 0).astype(F32).astype(BF)
-    picked = lambda ref: lax.dot_general(pick, ref[:, 2048:2304], nt, preferred_element_type=F32)
-    gains = lambda ref: lax.dot_general(unit, ref[:, 2304:], nt, preferred_element_type=F32)
+    picked = lambda ref: lax.dot_general(pick, ref[:, :256], nt, preferred_element_type=F32)
+    gains = lambda ref: lax.dot_general(unit, ref[:, 256:], nt, preferred_element_type=F32)
     hidden = attended + jnp.concatenate([picked(own_ref), picked(other_ref)], axis=0)
     gain = jnp.concatenate([gains(own_ref), gains(other_ref)], axis=0)
     squares = jnp.sum(hidden * hidden, axis=1, keepdims=True)
@@ -315,7 +315,10 @@
         1_000_000,
         100_000,
     )(rows, out_proj, carry_other)
-    _, slot_of, w_down = lax.optimization_barrier((part, slot_of, w_down))
+    _, slot_of, w_down, tail, tail_other = lax.optimization_barrier(
+        (part, slot_of, w_down, carry, carry_other)
+    )
+    tail, tail_other = tail[:, 2048:], tail_other[:, 2048:]
     pick, place = call(
         rows_kernel, [SMEM, SMEM, VMEM], [shape((16, 256)), shape((256, 256))], (), 0, 200_000
     )(core, tp, slot_of[None])
@@ -329,24 +332,24 @@
         joined([ff[1][:, 384 : 2 * SIZE], ff[2][:, :768]], axis=1),
         joined([ff[2][:, 768:], ff[3]], axis=1),
     ]
-    part, ff, thirds, down, pick = lax.optimization_barrier(
-        (exchange(part, "y"), ff, thirds, down, pick)
+    part, ff, thirds, down, pick, tail, tail_other = lax.optimization_barrier(
+        (exchange(part, "y"), ff, thirds, down, pick, tail, tail_other)
     )
     scaled, hidden = call(
         norm_kernel, [VMEM] * 4, [shape((32, 32, 128)), shape((32, 128), F32)], (), 0, 400_000
-    )(part, pick, carry, carry_other)
+    )(part, pick, tail, tail_other)
     hidden, *thirds = lax.optimization_barrier((hidden, *thirds))
     ff_other = [swap(w) for w in thirds]
     part = call(
         gate_kernel, [SMEM] * 2 + [VMEM] * 8, shape((8, 16, 1280)), (), 300_000_000, 2_800_000
     )(xh, xl, exchange(scaled, ("xh", "xl", "y")), *ff, *ff_other)
-    _, hidden, far = lax.optimization_barrier((part, hidden, down[1]))
-    part, far, across = lax.optimization_barrier(
-        (exchange(part, "z"), swap(far, "xh"), swap(hidden[16:]))
+    _, far, cross = lax.optimization_barrier((part, down[1], down[2]))
+    part, far, cross = lax.optimization_barrier(
+        (exchange(part, "z"), swap(far, "xh"), diagonal(cross))
     )
     units = call(units_kernel, [VMEM], shape((8, 16, SIZE)), (), 0, 500_000)(part)
-    _, cross = lax.optimization_barrier((units, down[2]))
-    units, cross = lax.optimization_barrier((exchange(units, "z"), diagonal(cross)))
+    _, hidden = lax.optimization_barrier((units, hidden))
+    units, across = lax.optimization_barrier((exchange(units, "z"), swap(hidden[16:])))
     down = (down[0], ff[1], far, cross)
     part = call(
         down_kernel,

time: 131 us -> 133 us (1.015)
  starting transfers between devices: 65.8 us -> 70.1 us
  waiting for transfers between devices: 27.1 us -> 25.7 us
    all_to_all x5, starting transfers between devices: 37.2 us -> 40.6 us  [exchange(): return lax.all_to_all(blocks, axes, 0, 0, tiled=True)]
    ppermute x2, waiting for transfers between devices: 6.38 us -> 4.08 us  [diagonal(): return lax.ppermute(value, ('xh', 'xl'), [(i, 3 - i) for i in range(4)])]
    all_to_all x5, waiting for transfers between devices: 13.2 us -> 14.9 us  [exchange(): return lax.all_to_all(blocks, axes, 0, 0, tiled=True)]
  transfers between devices with their start and end apart: 16 -> 16, of which waited for: 12 -> 11; matrix products, arithmetic and copies ran while one was open for 1% -> 2% of each run, Pallas kernels for 3% -> 3%
where the time goes in v7:
time: 133 us; the launch traced here: 132 us
  starting transfers between devices  70.1 us (53%)
  waiting for transfers between devices  25.7 us (19%)
  blocking collectives  19.6 us (15%)
  Pallas kernels  12 us (9%)
  other arithmetic  2.36 us (2%)
    all_to_all x5, starting transfers between devices, exchange(): return lax.all_to_all(blocks, axes, 0, 0, tiled=True)  40.6 us
    ppermute x9, starting transfers between devices, swap(): return lax.ppermute(value, axis, [(0, 1), (1, 0)])  23.4 us
    all_to_all x1, blocking collectives, exchange(): return lax.all_to_all(blocks, axes, 0, 0, tiled=True)  19.6 us
    all_to_all x5, waiting for transfers between devices, exchange(): return lax.all_to_all(blocks, axes, 0, 0, tiled=True)  14.9 us
    ppermute x9, waiting for transfers between devices, swap(): return lax.ppermute(value, axis, [(0, 1), (1, 0)])  6.74 us
    ppermute x2, starting transfers between devices, diagonal(): return lax.ppermute(value, ('xh', 'xl'), [(i, 3 - i) for i in range(4)])  6.1 us
    ppermute x2, waiting for transfers between devices, diagonal(): return lax.ppermute(value, ('xh', 'xl'), [(i, 3 - i) for i in range(4)])  4.08 us
    pallas_call x1, Pallas kernels, local(): call(attention_kernel, [SMEM, HBM, VMEM, HBM, HBM], shape((32, 16, 512)),...  3.93 us
  transfers between devices with their start and end apart: 16, of which 11 were waited for; matrix products, arithmetic and copies ran while one was open for 2% of the time, Pallas kernels for 3%

profile of v7, /device:TPU:8, one launch (start us, length us, event | category | flops | bytes accessed | tf_op | source)
XLA Modules:
  0.0 131.8 jit_solution(8606634540153998011)
XLA Ops:
  0.7 3.9 %shard_map.118 = bf16[32,16,512]{2,1,0:T(8,128)(2,1)} custom-call(s32[1]{0:T(128)S(6)} %copy.13.len_ref, bf16[64,576]{1,0:T(8,128)(2,1)} %bitcast.20, bf16[4,576]{1,0:T(4,128)(2,1)} %bitcast.21, bf16[576,512]{1,0:T(8,128)(2,1)} %bitcast.19, bf16[16,512,128]{2,1,0:T(8,128)(2,1)} %maps_ref.1), custom_call_target="tpu_custom_call" | custom-call | flops 200000000 | bytes 4000000 | tf_op jit(solution)/shard_map/pallas_call | solution.py:276
  4.6 13.2 %all-to-all-start = ((bf16[32,16,512]{2,1,0:T(8,128)(2,1)}), bf16[32,16,512]{2,1,0:T(8,128)(2,1)S(1)}, u32[]{:S(2)}, u32[]{:S(2)}) async-start(bf16[32,16,512]{2,1,0:T(8,128)(2,1)} %shard_map.118), calls=%async_computation | async-start | bytes 1048576 | tf_op jit(solution)/shard_map/all_to_all | solution.py:253
  17.9 0.1 broadcast_in_dim.24.gain_ref
  18.0 0.0 copy-start.7
  18.0 1.8 %shard_map.119 = (bf16[112,2432]{1,0:T(8,128)(2,1)}, bf16[112,1152]{1,0:T(8,128)(2,1)S(1)}, bf16[112,1728]{1,0:T(8,128)(2,1)}, bf16[112,1152]{1,0:T(8,128)(2,1)}, bf16[112,1152]{1,0:T(8,128)(2,1)}) custom-call(s32[1]{0:T(128)} %bitcast.xh_ref, s32[1]{0:T(128)} %bitcast.1.xl_ref, bf16[112,2304]{1,0:T(8,128)(2,1)S(1)} %copy-done.2, ...), custom_call_target="tpu_custom_call" | custom-call | bytes 3200000 | tf_op jit(solution)/shard_map/pallas_call | solution.py:298
  19.8 1.9 %collective-permute-start = (bf16[112,2432]{1,0:T(8,128)(2,1)}, bf16[112,2432]{1,0:T(8,128)(2,1)S(1)}, u32[]{:S(2)}, u32[]{:S(2)}) collective-permute-start(bf16[112,2432]{1,0:T(8,128)(2,1)} %get-tuple-element.86), channel_id=1, source_target_pairs={{0,8},{8,0},{1,9},{9,1},{2,10},{10,2},{3,11},{11,3},{4,12},{12,4},... | collective-permute-start | bytes 1634312 | tf_op jit(solution)/shard_map/ppermute | solution.py:249
  21.7 3.6 %collective-permute-start.1 = (bf16[112,1728]{1,0:T(8,128)(2,1)}, bf16[112,1728]{1,0:T(8,128)(2,1)S(1)}, u32[]{:S(2)}, u32[]{:S(2)}) collective-permute-start(bf16[112,1728]{1,0:T(8,128)(2,1)} %get-tuple-element.79), channel_id=1, source_target_pairs={{0,16},{16,0},{1,17},{17,1},{2,18},{18,2},{3,19},{19,3},{4,20},{20... | collective-permute-start | bytes 1161224 | tf_op jit(solution)/shard_map/ppermute | solution.py:249
  25.3 4.6 %collective-permute-start.2 = (bf16[112,1152]{1,0:T(8,128)(2,1)}, bf16[112,1152]{1,0:T(8,128)(2,1)S(1)}, u32[]{:S(2)}, u32[]{:S(2)}) collective-permute-start(bf16[112,1152]{1,0:T(8,128)(2,1)} %get-tuple-element.80), channel_id=1, source_target_pairs={{0,32},{32,0},{1,33},{33,1},{2,34},{34,2},{3,35},{35,3},{4,36},{36... | collective-permute-start | bytes 774152 | tf_op jit(solution)/shard_map/ppermute | solution.py:249
  29.9 2.2 %collective-permute-start.3 = (bf16[112,1152]{1,0:T(8,128)(2,1)}, bf16[112,1152]{1,0:T(8,128)(2,1)S(1)}, u32[]{:S(2)}, u32[]{:S(2)}) collective-permute-start(bf16[112,1152]{1,0:T(8,128)(2,1)} %get-tuple-element.81), channel_id=1, source_target_pairs={{0,48},{16,32},{32,16},{48,0},{1,49},{17,33},{33,17},{49,1},{2,50}... | collective-permute-start | bytes 774152 | tf_op jit(solution)/shard_map/ppermute | solution.py:257
  32.2 3.4 %all-to-all-done.x_ref = bf16[32,16,512]{2,1,0:T(8,128)(2,1)S(1)} async-done(((bf16[32,16,512]{2,1,0:T(8,128)(2,1)}), bf16[32,16,512]{2,1,0:T(8,128)(2,1)S(1)}, u32[]{:S(2)}, u32[]{:S(2)}) %all-to-all-start) | async-done | bytes 524320 | tf_op jit(solution)/shard_map/all_to_all | solution.py:253
  35.5 0.0 collective-permute-done.other_ref
  35.5 1.2 shard_map.120
  36.7 7.5 %all-to-all-start.1 = ((bf16[8,32,128]{2,1,0:T(8,128)(2,1)}), bf16[8,32,128]{2,1,0:T(8,128)(2,1)S(1)}, u32[]{:S(2)}, u32[]{:S(2)}) async-start(bf16[8,32,128]{2,1,0:T(8,128)(2,1)} %shard_map.120), calls=%async_computation.1 | async-start | bytes 131072 | tf_op jit(solution)/shard_map/all_to_all | solution.py:253
  44.3 0.2 shard_map.122
  44.5 0.1 shard_map.121
  44.6 0.9 collective-permute-done.2.refs_2_
  45.6 1.3 collective-permute-done.3.refs_3_
  46.8 0.0 collective-permute-done.1.refs_1_.w1
  46.9 0.9 pad_maximum_fusion
  47.9 0.8 pad_maximum_fusion.1
  48.6 0.9 slice.28.own_ref
  49.5 1.6 %all-to-all-done.1.part_ref = bf16[8,32,128]{2,1,0:T(8,128)(2,1)S(1)} async-done(((bf16[8,32,128]{2,1,0:T(8,128)(2,1)}), bf16[8,32,128]{2,1,0:T(8,128)(2,1)S(1)}, u32[]{:S(2)}, u32[]{:S(2)}) %all-to-all-start.1) | async-done | bytes 65568 | tf_op jit(solution)/shard_map/all_to_all | solution.py:253
  51.2 1.0 shard_map.123
  52.2 6.1 %all-to-all-start.2 = ((bf16[32,32,128]{2,1,0:T(8,128)(2,1)}), bf16[32,32,128]{2,1,0:T(8,128)(2,1)S(1)}, u32[]{:S(2)}, u32[]{:S(2)}) async-start(bf16[32,32,128]{2,1,0:T(8,128)(2,1)} %get-tuple-element.92), calls=%async_computation.2 | async-start | bytes 524288 | tf_op jit(solution)/shard_map/all_to_all | solution.py:253
  58.3 1.9 %collective-permute-start.4 = (bf16[112,1536]{1,0:T(8,128)(2,1)}, bf16[112,1536]{1,0:T(8,128)(2,1)S(1)}, u32[]{:S(2)}, u32[]{:S(2)}) collective-permute-start(bf16[112,1536]{1,0:T(8,128)(2,1)} %get-tuple-element.101), channel_id=1, source_target_pairs={{0,8},{8,0},{1,9},{9,1},{2,10},{10,2},{3,11},{11,3},{4,12},{12,4},... | collective-permute-start | bytes 1032200 | tf_op jit(solution)/shard_map/ppermute | solution.py:249
  60.2 2.4 %collective-permute-start.5 = (bf16[112,1536]{1,0:T(8,128)(2,1)}, bf16[112,1536]{1,0:T(8,128)(2,1)S(1)}, u32[]{:S(2)}, u32[]{:S(2)}) collective-permute-start(bf16[112,1536]{1,0:T(8,128)(2,1)} %pad_maximum_fusion.1), channel_id=1, source_target_pairs={{0,8},{8,0},{1,9},{9,1},{2,10},{10,2},{3,11},{11,3},{4,12},{12,4},... | collective-permute-start | bytes 1032200 | tf_op jit(solution)/shard_map/ppermute | solution.py:249
  62.6 1.9 %collective-permute-start.6 = (bf16[112,1536]{1,0:T(8,128)(2,1)}, bf16[112,1536]{1,0:T(8,128)(2,1)S(1)}, u32[]{:S(2)}, u32[]{:S(2)}) collective-permute-start(bf16[112,1536]{1,0:T(8,128)(2,1)} %get-tuple-element.103), channel_id=1, source_target_pairs={{0,8},{8,0},{1,9},{9,1},{2,10},{10,2},{3,11},{11,3},{4,12},{12,4},... | collective-permute-start | bytes 1032200 | tf_op jit(solution)/shard_map/ppermute | solution.py:249
  64.5 0.0 collective-permute-done.4.refs_4_
  64.6 0.0 collective-permute-done.5.refs_5_
  64.6 1.8 %collective-permute-done.6.refs_6_ = bf16[112,1536]{1,0:T(8,128)(2,1)S(1)} collective-permute-done((bf16[112,1536]{1,0:T(8,128)(2,1)}, bf16[112,1536]{1,0:T(8,128)(2,1)S(1)}, u32[]{:S(2)}, u32[]{:S(2)}) %collective-permute-start.6) | collective-permute-done | bytes 344096 | tf_op jit(solution)/shard_map/ppermute | solution.py:249
  66.4 3.5 %all-to-all-done.2.full_ref = bf16[32,32,128]{2,1,0:T(8,128)(2,1)S(1)} async-done(((bf16[32,32,128]{2,1,0:T(8,128)(2,1)}), bf16[32,32,128]{2,1,0:T(8,128)(2,1)S(1)}, u32[]{:S(2)}, u32[]{:S(2)}) %all-to-all-start.2) | async-done | bytes 262176 | tf_op jit(solution)/shard_map/all_to_all | solution.py:253
  69.9 1.3 %shard_map.124 = bf16[8,16,1280]{2,1,0:T(8,128)(2,1)} custom-call(s32[1]{0:T(128)} %bitcast.xh_ref, s32[1]{0:T(128)} %bitcast.1.xl_ref, bf16[32,32,128]{2,1,0:T(8,128)(2,1)S(1)} %all-to-all-done.2.full_ref, bf16[112,1152]{1,0:T(8,128)(2,1)S(1)} %get-tuple-element.93.refs_0_, bf16[112,1728]{1,0:T(8,128)(2,1)S(1)} %collective-permute-done.1.refs_1_.w1, ...), custom_call_target="tpu_custom_call" | custom-call | flops 300000000 | bytes 2800000 | tf_op jit(solution)/shard_map/pallas_call | solution.py:343
  71.2 6.6 %all-to-all-start.3 = ((bf16[8,16,1280]{2,1,0:T(8,128)(2,1)}), bf16[8,16,1280]{2,1,0:T(8,128)(2,1)S(1)}, u32[]{:S(2)}, u32[]{:S(2)}) async-start(bf16[8,16,1280]{2,1,0:T(8,128)(2,1)} %shard_map.124), calls=%async_computation.3 | async-start | bytes 655360 | tf_op jit(solution)/shard_map/all_to_all | solution.py:253
  77.9 3.2 %collective-permute-start.7 = (bf16[112,576]{1,0:T(8,128)(2,1)S(1)}, bf16[112,576]{1,0:T(8,128)(2,1)S(1)}, u32[]{:S(2)}, u32[]{:S(2)}) collective-permute-start(bf16[112,576]{1,0:T(8,128)(2,1)S(1)} %copy-done.6), channel_id=1, source_target_pairs={{0,32},{32,0},{1,33},{33,1},{2,34},{34,2},{3,35},{35,3},{4,36},{36... | collective-permute-start | bytes 387080 | tf_op jit(solution)/shard_map/ppermute | solution.py:249
  81.1 3.9 %collective-permute-start.8 = (bf16[112,576]{1,0:T(8,128)(2,1)S(1)}, bf16[112,576]{1,0:T(8,128)(2,1)S(1)}, u32[]{:S(2)}, u32[]{:S(2)}) collective-permute-start(bf16[112,576]{1,0:T(8,128)(2,1)S(1)} %get-tuple-element.107), channel_id=1, source_target_pairs={{0,48},{16,32},{32,16},{48,0},{1,49},{17,33},{33,17},{49,1},{2,50}... | collective-permute-start | bytes 387080 | tf_op jit(solution)/shard_map/ppermute | solution.py:257
  85.0 1.5 %collective-permute-done.7.w2 = bf16[112,576]{1,0:T(8,128)(2,1)S(1)} collective-permute-done((bf16[112,576]{1,0:T(8,128)(2,1)S(1)}, bf16[112,576]{1,0:T(8,128)(2,1)S(1)}, u32[]{:S(2)}, u32[]{:S(2)}) %collective-permute-start.7) | collective-permute-done | bytes 129056 | tf_op jit(solution)/shard_map/ppermute | solution.py:249
  86.5 2.8 %collective-permute-done.8.w3 = bf16[112,576]{1,0:T(8,128)(2,1)S(1)} collective-permute-done((bf16[112,576]{1,0:T(8,128)(2,1)S(1)}, bf16[112,576]{1,0:T(8,128)(2,1)S(1)}, u32[]{:S(2)}, u32[]{:S(2)}) %collective-permute-start.8) | collective-permute-done | bytes 129056 | tf_op jit(solution)/shard_map/ppermute | solution.py:257
  89.3 0.0 all-to-all-done.3.part_ref
  89.3 0.9 shard_map.125
  90.2 7.2 %all-to-all-start.4 = ((bf16[8,16,576]{2,1,0:T(8,128)(2,1)}), bf16[8,16,576]{2,1,0:T(8,128)(2,1)S(1)}, u32[]{:S(2)}, u32[]{:S(2)}) async-start(bf16[8,16,576]{2,1,0:T(8,128)(2,1)} %shard_map.125), calls=%async_computation.4 | async-start | bytes 327680 | tf_op jit(solution)/shard_map/all_to_all | solution.py:253
  97.4 1.9 %collective-permute-start.9 = (f32[16,128]{1,0:T(8,128)S(1)}, f32[16,128]{1,0:T(8,128)S(1)}, u32[]{:S(2)}, u32[]{:S(2)}) collective-permute-start(f32[16,128]{1,0:T(8,128)S(1)} %slice.30), channel_id=1, source_target_pairs={{0,8},{8,0},{1,9},{9,1},{2,10},{10,2},{3,11},{11,3},{4,12},{12,4},... | collective-permute-start | bytes 24584 | tf_op jit(solution)/shard_map/ppermute | solution.py:249
  99.3 1.1 collective-permute-done.9.across_ref
  100.5 6.4 %all-to-all-done.4.own_ref = bf16[8,16,576]{2,1,0:T(8,128)(2,1)S(1)} async-done(((bf16[8,16,576]{2,1,0:T(8,128)(2,1)}), bf16[8,16,576]{2,1,0:T(8,128)(2,1)S(1)}, u32[]{:S(2)}, u32[]{:S(2)}) %all-to-all-start.4) | async-done | bytes 147488 | tf_op jit(solution)/shard_map/all_to_all | solution.py:253
  106.8 1.9 %collective-permute-start.10 = (bf16[8,16,576]{2,1,0:T(8,128)(2,1)S(1)}, bf16[8,16,576]{2,1,0:T(8,128)(2,1)S(1)}, u32[]{:S(2)}, u32[]{:S(2)}) collective-permute-start(bf16[8,16,576]{2,1,0:T(8,128)(2,1)S(1)} %all-to-all-done.4.own_ref), channel_id=1, source_target_pairs={{0,8},{8,0},{1,9},{9,1},{2,10},{10,2},{3,11},{11,3},{4,12},{12,4},... | collective-permute-start | bytes 442376 | tf_op jit(solution)/shard_map/ppermute | solution.py:249
  108.7 1.4 %collective-permute-done.10.other_ref = bf16[8,16,576]{2,1,0:T(8,128)(2,1)S(1)} collective-permute-done((bf16[8,16,576]{2,1,0:T(8,128)(2,1)S(1)}, bf16[8,16,576]{2,1,0:T(8,128)(2,1)S(1)}, u32[]{:S(2)}, u32[]{:S(2)}) %collective-permute-start.10) | collective-permute-done | bytes 147488 | tf_op jit(solution)/shard_map/ppermute | solution.py:249
  110.1 1.5 %shard_map.126 = bf16[32,32,128]{2,1,0:T(8,128)(2,1)S(1)} custom-call(s32[1]{0:T(128)} %bitcast.xh_ref, s32[1]{0:T(128)} %bitcast.1.xl_ref, s32[1]{0:T(128)} %bitcast.2.y_ref, bf16[8,16,576]{2,1,0:T(8,128)(2,1)S(1)} %all-to-all-done.4.own_ref, bf16[8,16,576]{2,1,0:T(8,128)(2,1)S(1)} %collective-permute-done.10.other_ref, ...), custom_call_target="tpu_custom_call" | custom-call | flops 200000000 | bytes 1600000 | tf_op jit(solution)/shard_map/pallas_call | solution.py:354
  111.6 19.6 %all_to_all.30 = bf16[32,32,128]{2,1,0:T(8,128)(2,1)S(1)} all-to-all(bf16[32,32,128]{2,1,0:T(8,128)(2,1)S(1)} %shard_map.126), channel_id=1, replica_groups=mesh['z'=8,'xh'=2,'xl'=2,'c'=2,'y'=8] {'xh','xl','y'}, dimensions={0} | all-to-all | bytes 524288 | tf_op jit(solution)/shard_map/all_to_all | solution.py:253
  131.1 0.7 slice_reduce_fusion
  (23 shorter events, 0.1 us)
Async XLA Ops:
  0.7 17.2 %copy-start.8 = (bf16[112]{0:T(256)(128)(2,1)S(1)}, bf16[112]{0:T(256)(128)(2,1)}, u32[]{:S(2)}) copy-start(bf16[112]{0:T(256)(128)(2,1)} %param.20) | copy-start | bytes 676
  0.7 17.3 %copy-start = (bf16[2304,112]{0,1:T(8,128)(2,1)S(1)}, bf16[2304,112]{0,1:T(8,128)(2,1)}, u32[]{:S(2)}) copy-start(bf16[2304,112]{0,1:T(8,128)(2,1)} %param.23) | copy-start | bytes 1548292
  0.7 17.3 %copy-start.1 = (bf16[2048,112]{0,1:T(8,128)(2,1)S(1)}, bf16[2048,112]{0,1:T(8,128)(2,1)}, u32[]{:S(2)}) copy-start(bf16[2048,112]{0,1:T(8,128)(2,1)} %param.18) | copy-start | bytes 1376260
  0.7 17.3 %copy-start.2 = (bf16[112,2304]{1,0:T(8,128)(2,1)S(1)}, bf16[112,2304]{1,0:T(8,128)(2,1)}, u32[]{:S(2)}) copy-start(bf16[112,2304]{1,0:T(8,128)(2,1)} %gate_ref) | copy-start | bytes 1548292
  0.7 17.3 %copy-start.3 = (bf16[112,2304]{1,0:T(8,128)(2,1)S(1)}, bf16[112,2304]{1,0:T(8,128)(2,1)}, u32[]{:S(2)}) copy-start(bf16[112,2304]{1,0:T(8,128)(2,1)} %up_ref) | copy-start | bytes 1548292
  0.7 17.3 %copy-start.4 = (bf16[256,112]{0,1:T(8,128)(2,1)S(1)}, bf16[256,112]{0,1:T(8,128)(2,1)}, u32[]{:S(2)}) copy-start(bf16[256,112]{0,1:T(8,128)(2,1)} %param.19) | copy-start | bytes 172036
  4.6 30.9 %all-to-all-start = ((bf16[32,16,512]{2,1,0:T(8,128)(2,1)}), bf16[32,16,512]{2,1,0:T(8,128)(2,1)S(1)}, u32[]{:S(2)}, u32[]{:S(2)}) async-start(bf16[32,16,512]{2,1,0:T(8,128)(2,1)} %shard_map.118), calls=%async_computation | async-start | bytes 1048576 | tf_op jit(solution)/shard_map/all_to_all | solution.py:253
  18.0 26.5 %copy-start.7 = (s32[64]{0:T(128)S(1)}, s32[64]{0:T(128)}, u32[]{:S(2)}) copy-start(s32[64]{0:T(128)} %param.16) | copy-start | bytes 772
  19.8 15.8 %collective-permute-start = (bf16[112,2432]{1,0:T(8,128)(2,1)}, bf16[112,2432]{1,0:T(8,128)(2,1)S(1)}, u32[]{:S(2)}, u32[]{:S(2)}) collective-permute-start(bf16[112,2432]{1,0:T(8,128)(2,1)} %get-tuple-element.86), channel_id=1, source_target_pairs={{0,8},{8,0},{1,9},{9,1},{2,10},{10,2},{3,11},{11,3},{4,12},{12,4},... | collective-permute-start | bytes 1634312 | tf_op jit(solution)/shard_map/ppermute | solution.py:249
  21.7 25.1 %collective-permute-start.1 = (bf16[112,1728]{1,0:T(8,128)(2,1)}, bf16[112,1728]{1,0:T(8,128)(2,1)S(1)}, u32[]{:S(2)}, u32[]{:S(2)}) collective-permute-start(bf16[112,1728]{1,0:T(8,128)(2,1)} %get-tuple-element.79), channel_id=1, source_target_pairs={{0,16},{16,0},{1,17},{17,1},{2,18},{18,2},{3,19},{19,3},{4,20},{20... | collective-permute-start | bytes 1161224 | tf_op jit(solution)/shard_map/ppermute | solution.py:249
  25.3 20.2 %collective-permute-start.2 = (bf16[112,1152]{1,0:T(8,128)(2,1)}, bf16[112,1152]{1,0:T(8,128)(2,1)S(1)}, u32[]{:S(2)}, u32[]{:S(2)}) collective-permute-start(bf16[112,1152]{1,0:T(8,128)(2,1)} %get-tuple-element.80), channel_id=1, source_target_pairs={{0,32},{32,0},{1,33},{33,1},{2,34},{34,2},{3,35},{35,3},{4,36},{36... | collective-permute-start | bytes 774152 | tf_op jit(solution)/shard_map/ppermute | solution.py:249
  29.9 16.9 %collective-permute-start.3 = (bf16[112,1152]{1,0:T(8,128)(2,1)}, bf16[112,1152]{1,0:T(8,128)(2,1)S(1)}, u32[]{:S(2)}, u32[]{:S(2)}) collective-permute-start(bf16[112,1152]{1,0:T(8,128)(2,1)} %get-tuple-element.81), channel_id=1, source_target_pairs={{0,48},{16,32},{32,16},{48,0},{1,49},{17,33},{33,17},{49,1},{2,50}... | collective-permute-start | bytes 774152 | tf_op jit(solution)/shard_map/ppermute | solution.py:257
  36.7 14.5 %all-to-all-start.1 = ((bf16[8,32,128]{2,1,0:T(8,128)(2,1)}), bf16[8,32,128]{2,1,0:T(8,128)(2,1)S(1)}, u32[]{:S(2)}, u32[]{:S(2)}) async-start(bf16[8,32,128]{2,1,0:T(8,128)(2,1)} %shard_map.120), calls=%async_computation.1 | async-start | bytes 131072 | tf_op jit(solution)/shard_map/all_to_all | solution.py:253
  44.5 3.4 %copy-start.5 = (bf16[112,576]{1,0:T(8,128)(2,1)}, bf16[112,576]{1,0:T(8,128)(2,1)S(1)}, u32[]{:S(2)}) copy-start(bf16[112,576]{1,0:T(8,128)(2,1)S(1)} %get-tuple-element.106) | copy-start | bytes 387076
  51.2 26.7 %copy-start.6 = (bf16[112,576]{1,0:T(8,128)(2,1)S(1)}, bf16[112,576]{1,0:T(8,128)(2,1)}, u32[]{:S(2)}) copy-start(bf16[112,576]{1,0:T(8,128)(2,1)} %copy-done.5) | copy-start | bytes 387076
  52.2 17.7 %all-to-all-start.2 = ((bf16[32,32,128]{2,1,0:T(8,128)(2,1)}), bf16[32,32,128]{2,1,0:T(8,128)(2,1)S(1)}, u32[]{:S(2)}, u32[]{:S(2)}) async-start(bf16[32,32,128]{2,1,0:T(8,128)(2,1)} %get-tuple-element.92), calls=%async_computation.2 | async-start | bytes 524288 | tf_op jit(solution)/shard_map/all_to_all | solution.py:253
  58.3 6.3 %collective-permute-start.4 = (bf16[112,1536]{1,0:T(8,128)(2,1)}, bf16[112,1536]{1,0:T(8,128)(2,1)S(1)}, u32[]{:S(2)}, u32[]{:S(2)}) collective-permute-start(bf16[112,1536]{1,0:T(8,128)(2,1)} %get-tuple-element.101), channel_id=1, source_target_pairs={{0,8},{8,0},{1,9},{9,1},{2,10},{10,2},{3,11},{11,3},{4,12},{12,4},... | collective-permute-start | bytes 1032200 | tf_op jit(solution)/shard_map/ppermute | solution.py:249
  60.2 4.4 %collective-permute-start.5 = (bf16[112,1536]{1,0:T(8,128)(2,1)}, bf16[112,1536]{1,0:T(8,128)(2,1)S(1)}, u32[]{:S(2)}, u32[]{:S(2)}) collective-permute-start(bf16[112,1536]{1,0:T(8,128)(2,1)} %pad_maximum_fusion.1), channel_id=1, source_target_pairs={{0,8},{8,0},{1,9},{9,1},{2,10},{10,2},{3,11},{11,3},{4,12},{12,4},... | collective-permute-start | bytes 1032200 | tf_op jit(solution)/shard_map/ppermute | solution.py:249
  62.6 3.8 %collective-permute-start.6 = (bf16[112,1536]{1,0:T(8,128)(2,1)}, bf16[112,1536]{1,0:T(8,128)(2,1)S(1)}, u32[]{:S(2)}, u32[]{:S(2)}) collective-permute-start(bf16[112,1536]{1,0:T(8,128)(2,1)} %get-tuple-element.103), channel_id=1, source_target_pairs={{0,8},{8,0},{1,9},{9,1},{2,10},{10,2},{3,11},{11,3},{4,12},{12,4},... | collective-permute-start | bytes 1032200 | tf_op jit(solution)/shard_map/ppermute | solution.py:249
  71.2 18.1 %all-to-all-start.3 = ((bf16[8,16,1280]{2,1,0:T(8,128)(2,1)}), bf16[8,16,1280]{2,1,0:T(8,128)(2,1)S(1)}, u32[]{:S(2)}, u32[]{:S(2)}) async-start(bf16[8,16,1280]{2,1,0:T(8,128)(2,1)} %shard_map.124), calls=%async_computation.3 | async-start | bytes 655360 | tf_op jit(solution)/shard_map/all_to_all | solution.py:253
  77.9 8.6 %collective-permute-start.7 = (bf16[112,576]{1,0:T(8,128)(2,1)S(1)}, bf16[112,576]{1,0:T(8,128)(2,1)S(1)}, u32[]{:S(2)}, u32[]{:S(2)}) collective-permute-start(bf16[112,576]{1,0:T(8,128)(2,1)S(1)} %copy-done.6), channel_id=1, source_target_pairs={{0,32},{32,0},{1,33},{33,1},{2,34},{34,2},{3,35},{35,3},{4,36},{36... | collective-permute-start | bytes 387080 | tf_op jit(solution)/shard_map/ppermute | solution.py:249
  81.1 8.2 %collective-permute-start.8 = (bf16[112,576]{1,0:T(8,128)(2,1)S(1)}, bf16[112,576]{1,0:T(8,128)(2,1)S(1)}, u32[]{:S(2)}, u32[]{:S(2)}) collective-permute-start(bf16[112,576]{1,0:T(8,128)(2,1)S(1)} %get-tuple-element.107), channel_id=1, source_target_pairs={{0,48},{16,32},{32,16},{48,0},{1,49},{17,33},{33,17},{49,1},{2,50}... | collective-permute-start | bytes 387080 | tf_op jit(solution)/shard_map/ppermute | solution.py:257
  90.2 16.6 %all-to-all-start.4 = ((bf16[8,16,576]{2,1,0:T(8,128)(2,1)}), bf16[8,16,576]{2,1,0:T(8,128)(2,1)S(1)}, u32[]{:S(2)}, u32[]{:S(2)}) async-start(bf16[8,16,576]{2,1,0:T(8,128)(2,1)} %shard_map.125), calls=%async_computation.4 | async-start | bytes 327680 | tf_op jit(solution)/shard_map/all_to_all | solution.py:253
  97.4 3.1 %collective-permute-start.9 = (f32[16,128]{1,0:T(8,128)S(1)}, f32[16,128]{1,0:T(8,128)S(1)}, u32[]{:S(2)}, u32[]{:S(2)}) collective-permute-start(f32[16,128]{1,0:T(8,128)S(1)} %slice.30), channel_id=1, source_target_pairs={{0,8},{8,0},{1,9},{9,1},{2,10},{10,2},{3,11},{11,3},{4,12},{12,4},... | collective-permute-start | bytes 24584 | tf_op jit(solution)/shard_map/ppermute | solution.py:249
  106.8 3.3 %collective-permute-start.10 = (bf16[8,16,576]{2,1,0:T(8,128)(2,1)S(1)}, bf16[8,16,576]{2,1,0:T(8,128)(2,1)S(1)}, u32[]{:S(2)}, u32[]{:S(2)}) collective-permute-start(bf16[8,16,576]{2,1,0:T(8,128)(2,1)S(1)} %all-to-all-done.4.own_ref), channel_id=1, source_target_pairs={{0,8},{8,0},{1,9},{9,1},{2,10},{10,2},{3,11},{11,3},{4,12},{12,4},... | collective-permute-start | bytes 442376 | tf_op jit(solution)/shard_map/ppermute | solution.py:249

commit v8 on v7

--- a/solution.py
+++ b/solution.py
@@ -121,8 +121,7 @@
     iota = lambda dims, axis: lax.broadcasted_iota(jnp.int32, dims, axis)
     slot = slot_ref[...].astype(F32)
     col = iota((256, 256), 1)
-    core = jnp.where(col < 128, core_ref[0], 1 - core_ref[0])
-    held = (col & 31) * 8 + core * 4 + ((col >> 5) & 3)
+    held = (col & 31) * 8 + (col >> 7) * 4 + ((col >> 5) & 3)
     spread = (iota((256, 64), 0) >> 2) == iota((256, 64), 1)
     of_row = jnp.sum(jnp.where(spread, slot, 0.0), axis=1, keepdims=True).astype(jnp.int32)
     place = (of_row * 4 + (iota((256, 256), 0) & 3)) == held
@@ -220,14 +219,14 @@
     gate = total[:, :SIZE] * factor
     up = total[:, SIZE : 2 * SIZE] * factor
     units = (gate * jax.nn.sigmoid(gate) * up).astype(BF)
-    for i in range(8):
+    for i in range(16):
         out_ref[i] = units
 
 
 def down_kernel(
-    xh_ref, xl_ref, y_ref, own_ref, other_ref, w0, w1, w2, w3, hidden_ref, across_ref, place_ref, out_ref, total
+    xh_ref, xl_ref, core_ref, y_ref, units_ref, w0, w1, w2, w3, hidden_ref, across_ref, place_ref, out_ref, total
 ):
-    units = jnp.concatenate([own_ref[...].reshape(128, SIZE), other_ref[...].reshape(128, SIZE)], axis=0)
+    units = jnp.concatenate([units_ref[:, i].reshape(128, SIZE) for i in range(2)], axis=0)
     place = place_ref[...]
     none = jnp.zeros((128 - WIDTH, SIZE), BF)
     nt = (((1,), (1,)), ((), ()))
@@ -236,9 +235,10 @@
         part = lax.dot_general(units, wide, nt, preferred_element_type=F32)
         if r == 0:
             total[...] = part
-            at = pl.multiple_of(y_ref[0] * 16, 16)
-            total[pl.ds(at, 16), :] += hidden_ref[0:16, :]
-            total[pl.ds(128 + at, 16), :] += across_ref[...]
+            here = pl.multiple_of(core_ref[0] * 128 + y_ref[0] * 16, 16)
+            total[pl.ds(here, 16), :] += hidden_ref[0:16, :]
+            there = pl.multiple_of((1 - core_ref[0]) * 128 + y_ref[0] * 16, 16)
+            total[pl.ds(there, 16), :] += across_ref[...]
             part = total[...]
         rows = dot(place, part.astype(BF)).astype(BF)
         x = 2 * (xh_ref[0] ^ (r >> 1)) + (xl_ref[0] ^ (r & 1))
@@ -343,22 +343,22 @@
     part = call(
         gate_kernel, [SMEM] * 2 + [VMEM] * 8, shape((8, 16, 1280)), (), 300_000_000, 2_800_000
     )(xh, xl, exchange(scaled, ("xh", "xl", "y")), *ff, *ff_other)
-    _, far, cross = lax.optimization_barrier((part, down[1], down[2]))
-    part, far, cross = lax.optimization_barrier(
-        (exchange(part, "z"), swap(far, "xh"), diagonal(cross))
-    )
-    units = call(units_kernel, [VMEM], shape((8, 16, SIZE)), (), 0, 500_000)(part)
-    _, hidden = lax.optimization_barrier((units, hidden))
-    units, across = lax.optimization_barrier((exchange(units, "z"), swap(hidden[16:])))
+    _, hidden, far = lax.optimization_barrier((part, hidden, down[1]))
+    part, far, across = lax.optimization_barrier(
+        (exchange(part, "z"), swap(far, "xh"), swap(hidden[16:]))
+    )
+    units = call(units_kernel, [VMEM], shape((16, 16, SIZE)), (), 0, 500_000)(part)
+    _, cross = lax.optimization_barrier((units, down[2]))
+    units, cross = lax.optimization_barrier((exchange(units, ("z", "c")), diagonal(cross)))
     down = (down[0], ff[1], far, cross)
     part = call(
         down_kernel,
-        [SMEM] * 3 + [VMEM] * 9,
+        [SMEM] * 4 + [VMEM] * 8,
         shape((32, 32, 128)),
         [pltpu.VMEM((256, 128), F32)],
         200_000_000,
         1_600_000,
-    )(xh, xl, tp, units, swap(units), *down, hidden, across, place)
+    )(xh, xl, core, tp, units.reshape(8, 2, 16, SIZE), *down, hidden, across, place)
     total = jnp.sum(exchange(part, ("xh", "xl", "y"))[:, :, :WIDTH].astype(F32), axis=0)
     return total.astype(BF)
 

time: 133 us -> 131 us (0.985)
  starting transfers between devices: 70.1 us -> 64.8 us
  waiting for transfers between devices: 25.7 us -> 27.9 us
    ppermute x2, waiting for transfers between devices: 4.08 us -> 7.37 us  [diagonal(): return lax.ppermute(value, ('xh', 'xl'), [(i, 3 - i) for i in range(4)])]
    all_to_all x5, starting transfers between devices: 40.6 us -> 38.1 us  [exchange(): return lax.all_to_all(blocks, axes, 0, 0, tiled=True)]
    ppermute x9 -> x8, starting transfers between devices: 23.4 us -> 21.5 us  [swap(): return lax.ppermute(value, axis, [(0, 1), (1, 0)])]
    ppermute x9 -> x8, waiting for transfers between devices: 6.74 us -> 6.08 us  [swap(): return lax.ppermute(value, axis, [(0, 1), (1, 0)])]
  transfers between devices with their start and end apart: 16 -> 15, of which waited for: 11 -> 11; matrix products, arithmetic and copies ran while one was open for 2% -> 2% of each run, Pallas kernels for 3% -> 3%
where the time goes in v8:
time: 131 us; the launch traced here: 130 us
  starting transfers between devices  64.8 us (49%)
  waiting for transfers between devices  27.9 us (21%)
  blocking collectives  20.8 us (16%)
  Pallas kernels  12.1 us (9%)
  other arithmetic  2.36 us (2%)
    all_to_all x5, starting transfers between devices, exchange(): return lax.all_to_all(blocks, axes, 0, 0, tiled=True)  38.1 us
    ppermute x8, starting transfers between devices, swap(): return lax.ppermute(value, axis, [(0, 1), (1, 0)])  21.5 us
    all_to_all x1, blocking collectives, exchange(): return lax.all_to_all(blocks, axes, 0, 0, tiled=True)  20.8 us
    all_to_all x5, waiting for transfers between devices, exchange(): return lax.all_to_all(blocks, axes, 0, 0, tiled=True)  14.4 us
    ppermute x2, waiting for transfers between devices, diagonal(): return lax.ppermute(value, ('xh', 'xl'), [(i, 3 - i) for i in range(4)])  7.37 us
    ppermute x8, waiting for transfers between devices, swap(): return lax.ppermute(value, axis, [(0, 1), (1, 0)])  6.08 us
    ppermute x2, starting transfers between devices, diagonal(): return lax.ppermute(value, ('xh', 'xl'), [(i, 3 - i) for i in range(4)])  5.29 us
    pallas_call x1, Pallas kernels, local(): call(attention_kernel, [SMEM, HBM, VMEM, HBM, HBM], shape((32, 16, 512)),...  3.93 us
  transfers between devices with their start and end apart: 15, of which 11 were waited for; matrix products, arithmetic and copies ran while one was open for 2% of the time, Pallas kernels for 3%

profile of v8, /device:TPU:8, one launch (start us, length us, event | category | flops | bytes accessed | tf_op | source)
XLA Modules:
  0.0 130.0 jit_solution(3452460556947410668)
XLA Ops:
  0.7 0.0 copy-start.8
  0.7 3.9 %shard_map.118 = bf16[32,16,512]{2,1,0:T(8,128)(2,1)} custom-call(s32[1]{0:T(128)S(6)} %copy.13.len_ref, bf16[64,576]{1,0:T(8,128)(2,1)} %bitcast.22, bf16[4,576]{1,0:T(4,128)(2,1)} %bitcast.23, bf16[576,512]{1,0:T(8,128)(2,1)} %bitcast.21, bf16[16,512,128]{2,1,0:T(8,128)(2,1)} %maps_ref.1), custom_call_target="tpu_custom_call" | custom-call | flops 200000000 | bytes 4000000 | tf_op jit(solution)/shard_map/pallas_call | solution.py:276
  4.6 13.2 %all-to-all-start = ((bf16[32,16,512]{2,1,0:T(8,128)(2,1)}), bf16[32,16,512]{2,1,0:T(8,128)(2,1)S(1)}, u32[]{:S(2)}, u32[]{:S(2)}) async-start(bf16[32,16,512]{2,1,0:T(8,128)(2,1)} %shard_map.118), calls=%async_computation | async-start | bytes 1048576 | tf_op jit(solution)/shard_map/all_to_all | solution.py:253
  17.8 0.0 copy-done.8
  17.9 0.1 broadcast_in_dim.25.gain_ref
  18.0 0.0 copy-start.7
  18.0 1.8 %shard_map.119 = (bf16[112,2432]{1,0:T(8,128)(2,1)}, bf16[112,1152]{1,0:T(8,128)(2,1)S(1)}, bf16[112,1728]{1,0:T(8,128)(2,1)}, bf16[112,1152]{1,0:T(8,128)(2,1)}, bf16[112,1152]{1,0:T(8,128)(2,1)}) custom-call(s32[1]{0:T(128)} %bitcast.xh_ref, s32[1]{0:T(128)} %bitcast.1.xl_ref, bf16[112,2304]{1,0:T(8,128)(2,1)S(1)} %copy-done.2, ...), custom_call_target="tpu_custom_call" | custom-call | bytes 3200000 | tf_op jit(solution)/shard_map/pallas_call | solution.py:298
  19.8 1.9 %collective-permute-start = (bf16[112,2432]{1,0:T(8,128)(2,1)}, bf16[112,2432]{1,0:T(8,128)(2,1)S(1)}, u32[]{:S(2)}, u32[]{:S(2)}) collective-permute-start(bf16[112,2432]{1,0:T(8,128)(2,1)} %get-tuple-element.86), channel_id=1, source_target_pairs={{0,8},{8,0},{1,9},{9,1},{2,10},{10,2},{3,11},{11,3},{4,12},{12,4},... | collective-permute-start | bytes 1634312 | tf_op jit(solution)/shard_map/ppermute | solution.py:249
  21.7 3.6 %collective-permute-start.1 = (bf16[112,1728]{1,0:T(8,128)(2,1)}, bf16[112,1728]{1,0:T(8,128)(2,1)S(1)}, u32[]{:S(2)}, u32[]{:S(2)}) collective-permute-start(bf16[112,1728]{1,0:T(8,128)(2,1)} %get-tuple-element.79), channel_id=1, source_target_pairs={{0,16},{16,0},{1,17},{17,1},{2,18},{18,2},{3,19},{19,3},{4,20},{20... | collective-permute-start | bytes 1161224 | tf_op jit(solution)/shard_map/ppermute | solution.py:249
  25.3 4.6 %collective-permute-start.2 = (bf16[112,1152]{1,0:T(8,128)(2,1)}, bf16[112,1152]{1,0:T(8,128)(2,1)S(1)}, u32[]{:S(2)}, u32[]{:S(2)}) collective-permute-start(bf16[112,1152]{1,0:T(8,128)(2,1)} %get-tuple-element.80), channel_id=1, source_target_pairs={{0,32},{32,0},{1,33},{33,1},{2,34},{34,2},{3,35},{35,3},{4,36},{36... | collective-permute-start | bytes 774152 | tf_op jit(solution)/shard_map/ppermute | solution.py:249
  29.9 2.2 %collective-permute-start.3 = (bf16[112,1152]{1,0:T(8,128)(2,1)}, bf16[112,1152]{1,0:T(8,128)(2,1)S(1)}, u32[]{:S(2)}, u32[]{:S(2)}) collective-permute-start(bf16[112,1152]{1,0:T(8,128)(2,1)} %get-tuple-element.81), channel_id=1, source_target_pairs={{0,48},{16,32},{32,16},{48,0},{1,49},{17,33},{33,17},{49,1},{2,50}... | collective-permute-start | bytes 774152 | tf_op jit(solution)/shard_map/ppermute | solution.py:257
  32.2 3.4 %all-to-all-done.x_ref = bf16[32,16,512]{2,1,0:T(8,128)(2,1)S(1)} async-done(((bf16[32,16,512]{2,1,0:T(8,128)(2,1)}), bf16[32,16,512]{2,1,0:T(8,128)(2,1)S(1)}, u32[]{:S(2)}, u32[]{:S(2)}) %all-to-all-start) | async-done | bytes 524320 | tf_op jit(solution)/shard_map/all_to_all | solution.py:253
  35.5 0.0 collective-permute-done.other_ref
  35.5 1.2 shard_map.120
  36.7 7.5 %all-to-all-start.1 = ((bf16[8,32,128]{2,1,0:T(8,128)(2,1)}), bf16[8,32,128]{2,1,0:T(8,128)(2,1)S(1)}, u32[]{:S(2)}, u32[]{:S(2)}) async-start(bf16[8,32,128]{2,1,0:T(8,128)(2,1)} %shard_map.120), calls=%async_computation.1 | async-start | bytes 131072 | tf_op jit(solution)/shard_map/all_to_all | solution.py:253
  44.3 0.2 shard_map.122
  44.5 0.1 shard_map.121
  44.6 0.9 collective-permute-done.2.refs_2_
  45.6 1.3 collective-permute-done.3.refs_3_
  46.8 0.0 collective-permute-done.1.refs_1_.w1
  46.9 0.9 pad_maximum_fusion
  47.9 0.8 pad_maximum_fusion.1
  48.6 0.9 slice.28.own_ref
  49.5 1.6 %all-to-all-done.1.part_ref = bf16[8,32,128]{2,1,0:T(8,128)(2,1)S(1)} async-done(((bf16[8,32,128]{2,1,0:T(8,128)(2,1)}), bf16[8,32,128]{2,1,0:T(8,128)(2,1)S(1)}, u32[]{:S(2)}, u32[]{:S(2)}) %all-to-all-start.1) | async-done | bytes 65568 | tf_op jit(solution)/shard_map/all_to_all | solution.py:253
  51.2 1.0 shard_map.123
  52.2 6.1 %all-to-all-start.2 = ((bf16[32,32,128]{2,1,0:T(8,128)(2,1)}), bf16[32,32,128]{2,1,0:T(8,128)(2,1)S(1)}, u32[]{:S(2)}, u32[]{:S(2)}) async-start(bf16[32,32,128]{2,1,0:T(8,128)(2,1)} %get-tuple-element.92), calls=%async_computation.2 | async-start | bytes 524288 | tf_op jit(solution)/shard_map/all_to_all | solution.py:253
  58.3 1.9 %collective-permute-start.4 = (bf16[112,1536]{1,0:T(8,128)(2,1)}, bf16[112,1536]{1,0:T(8,128)(2,1)S(1)}, u32[]{:S(2)}, u32[]{:S(2)}) collective-permute-start(bf16[112,1536]{1,0:T(8,128)(2,1)} %get-tuple-element.101), channel_id=1, source_target_pairs={{0,8},{8,0},{1,9},{9,1},{2,10},{10,2},{3,11},{11,3},{4,12},{12,4},... | collective-permute-start | bytes 1032200 | tf_op jit(solution)/shard_map/ppermute | solution.py:249
  60.2 2.4 %collective-permute-start.5 = (bf16[112,1536]{1,0:T(8,128)(2,1)}, bf16[112,1536]{1,0:T(8,128)(2,1)S(1)}, u32[]{:S(2)}, u32[]{:S(2)}) collective-permute-start(bf16[112,1536]{1,0:T(8,128)(2,1)} %pad_maximum_fusion.1), channel_id=1, source_target_pairs={{0,8},{8,0},{1,9},{9,1},{2,10},{10,2},{3,11},{11,3},{4,12},{12,4},... | collective-permute-start | bytes 1032200 | tf_op jit(solution)/shard_map/ppermute | solution.py:249
  62.6 1.9 %collective-permute-start.6 = (bf16[112,1536]{1,0:T(8,128)(2,1)}, bf16[112,1536]{1,0:T(8,128)(2,1)S(1)}, u32[]{:S(2)}, u32[]{:S(2)}) collective-permute-start(bf16[112,1536]{1,0:T(8,128)(2,1)} %get-tuple-element.103), channel_id=1, source_target_pairs={{0,8},{8,0},{1,9},{9,1},{2,10},{10,2},{3,11},{11,3},{4,12},{12,4},... | collective-permute-start | bytes 1032200 | tf_op jit(solution)/shard_map/ppermute | solution.py:249
  64.5 0.0 collective-permute-done.4.refs_4_
  64.6 0.0 collective-permute-done.5.refs_5_
  64.6 1.8 %collective-permute-done.6.refs_6_ = bf16[112,1536]{1,0:T(8,128)(2,1)S(1)} collective-permute-done((bf16[112,1536]{1,0:T(8,128)(2,1)}, bf16[112,1536]{1,0:T(8,128)(2,1)S(1)}, u32[]{:S(2)}, u32[]{:S(2)}) %collective-permute-start.6) | collective-permute-done | bytes 344096 | tf_op jit(solution)/shard_map/ppermute | solution.py:249
  66.4 3.5 %all-to-all-done.2.full_ref = bf16[32,32,128]{2,1,0:T(8,128)(2,1)S(1)} async-done(((bf16[32,32,128]{2,1,0:T(8,128)(2,1)}), bf16[32,32,128]{2,1,0:T(8,128)(2,1)S(1)}, u32[]{:S(2)}, u32[]{:S(2)}) %all-to-all-start.2) | async-done | bytes 262176 | tf_op jit(solution)/shard_map/all_to_all | solution.py:253
  69.9 1.3 %shard_map.124 = bf16[8,16,1280]{2,1,0:T(8,128)(2,1)} custom-call(s32[1]{0:T(128)} %bitcast.xh_ref, s32[1]{0:T(128)} %bitcast.1.xl_ref, bf16[32,32,128]{2,1,0:T(8,128)(2,1)S(1)} %all-to-all-done.2.full_ref, bf16[112,1152]{1,0:T(8,128)(2,1)S(1)} %get-tuple-element.93.refs_0_, bf16[112,1728]{1,0:T(8,128)(2,1)S(1)} %collective-permute-done.1.refs_1_.w1, ...), custom_call_target="tpu_custom_call" | custom-call | flops 300000000 | bytes 2800000 | tf_op jit(solution)/shard_map/pallas_call | solution.py:343
  71.2 6.6 %all-to-all-start.3 = ((bf16[8,16,1280]{2,1,0:T(8,128)(2,1)}), bf16[8,16,1280]{2,1,0:T(8,128)(2,1)S(1)}, u32[]{:S(2)}, u32[]{:S(2)}) async-start(bf16[8,16,1280]{2,1,0:T(8,128)(2,1)} %shard_map.124), calls=%async_computation.3 | async-start | bytes 655360 | tf_op jit(solution)/shard_map/all_to_all | solution.py:253
  77.9 3.2 %collective-permute-start.7 = (bf16[112,576]{1,0:T(8,128)(2,1)S(1)}, bf16[112,576]{1,0:T(8,128)(2,1)S(1)}, u32[]{:S(2)}, u32[]{:S(2)}) collective-permute-start(bf16[112,576]{1,0:T(8,128)(2,1)S(1)} %copy-done.6), channel_id=1, source_target_pairs={{0,32},{32,0},{1,33},{33,1},{2,34},{34,2},{3,35},{35,3},{4,36},{36... | collective-permute-start | bytes 387080 | tf_op jit(solution)/shard_map/ppermute | solution.py:249
  81.1 1.9 %collective-permute-start.8 = (f32[16,128]{1,0:T(8,128)S(1)}, f32[16,128]{1,0:T(8,128)S(1)}, u32[]{:S(2)}, u32[]{:S(2)}) collective-permute-start(f32[16,128]{1,0:T(8,128)S(1)} %slice.30), channel_id=1, source_target_pairs={{0,8},{8,0},{1,9},{9,1},{2,10},{10,2},{3,11},{11,3},{4,12},{12,4},... | collective-permute-start | bytes 24584 | tf_op jit(solution)/shard_map/ppermute | solution.py:249
  83.0 1.1 collective-permute-done.8.across_ref
  84.2 2.2 %collective-permute-done.7.w2 = bf16[112,576]{1,0:T(8,128)(2,1)S(1)} collective-permute-done((bf16[112,576]{1,0:T(8,128)(2,1)S(1)}, bf16[112,576]{1,0:T(8,128)(2,1)S(1)}, u32[]{:S(2)}, u32[]{:S(2)}) %collective-permute-start.7) | collective-permute-done | bytes 129056 | tf_op jit(solution)/shard_map/ppermute | solution.py:249
  86.4 2.7 %all-to-all-done.3.part_ref = bf16[8,16,1280]{2,1,0:T(8,128)(2,1)S(1)} async-done(((bf16[8,16,1280]{2,1,0:T(8,128)(2,1)}), bf16[8,16,1280]{2,1,0:T(8,128)(2,1)S(1)}, u32[]{:S(2)}, u32[]{:S(2)}) %all-to-all-start.3) | async-done | bytes 327712 | tf_op jit(solution)/shard_map/all_to_all | solution.py:253
  89.0 1.0 shard_map.125
  90.0 4.6 %all-to-all-start.4 = ((bf16[16,16,576]{2,1,0:T(8,128)(2,1)}), bf16[16,16,576]{2,1,0:T(8,128)(2,1)S(1)}, u32[]{:S(2)}, u32[]{:S(2)}) async-start(bf16[16,16,576]{2,1,0:T(8,128)(2,1)} %shard_map.125), calls=%async_computation.4 | async-start | bytes 655360 | tf_op jit(solution)/shard_map/all_to_all | solution.py:253
  94.7 3.1 %collective-permute-start.9 = (bf16[112,576]{1,0:T(8,128)(2,1)S(1)}, bf16[112,576]{1,0:T(8,128)(2,1)S(1)}, u32[]{:S(2)}, u32[]{:S(2)}) collective-permute-start(bf16[112,576]{1,0:T(8,128)(2,1)S(1)} %get-tuple-element.110), channel_id=1, source_target_pairs={{0,48},{16,32},{32,16},{48,0},{1,49},{17,33},{33,17},{49,1},{2,50}... | collective-permute-start | bytes 387080 | tf_op jit(solution)/shard_map/ppermute | solution.py:257
  97.7 6.1 %collective-permute-done.9.w3 = bf16[112,576]{1,0:T(8,128)(2,1)S(1)} collective-permute-done((bf16[112,576]{1,0:T(8,128)(2,1)S(1)}, bf16[112,576]{1,0:T(8,128)(2,1)S(1)}, u32[]{:S(2)}, u32[]{:S(2)}) %collective-permute-start.9) | collective-permute-done | bytes 129056 | tf_op jit(solution)/shard_map/ppermute | solution.py:257
  103.9 3.2 %all-to-all-done.4 = bf16[16,16,576]{2,1,0:T(8,128)(2,1)S(1)} async-done(((bf16[16,16,576]{2,1,0:T(8,128)(2,1)}), bf16[16,16,576]{2,1,0:T(8,128)(2,1)S(1)}, u32[]{:S(2)}, u32[]{:S(2)}) %all-to-all-start.4) | async-done | bytes 294944 | tf_op jit(solution)/shard_map/all_to_all | solution.py:253
  107.0 1.5 %shard_map.126 = bf16[32,32,128]{2,1,0:T(8,128)(2,1)S(1)} custom-call(s32[1]{0:T(128)} %bitcast.xh_ref, s32[1]{0:T(128)} %bitcast.1.xl_ref, s32[1]{0:T(128)} %bitcast.2.core_ref, s32[1]{0:T(128)} %bitcast.3.y_ref, bf16[8,2,16,576]{3,2,1,0:T(8,128)(2,1)S(1)} %bitcast.18, bf16[112,576]{1,0:T(8,128)(2,1)S(1)} %get-tuple-element.112.w0, ...), custom_call_target="tpu_custom_call" | custom-call | flops 200000000 | bytes 1600000 | tf_op jit(solution)/shard_map/pallas_call | solution.py:354
  108.5 20.8 %all_to_all.30 = bf16[32,32,128]{2,1,0:T(8,128)(2,1)S(1)} all-to-all(bf16[32,32,128]{2,1,0:T(8,128)(2,1)S(1)} %shard_map.126), channel_id=1, replica_groups=mesh['z'=8,'xh'=2,'xl'=2,'c'=2,'y'=8] {'xh','xl','y'}, dimensions={0} | all-to-all | bytes 524288 | tf_op jit(solution)/shard_map/all_to_all | solution.py:253
  129.3 0.7 slice_reduce_fusion
  (21 shorter events, 0.1 us)
Async XLA Ops:
  0.7 17.2 %copy-start.8 = (bf16[112]{0:T(256)(128)(2,1)S(1)}, bf16[112]{0:T(256)(128)(2,1)}, u32[]{:S(2)}) copy-start(bf16[112]{0:T(256)(128)(2,1)} %param.20) | copy-start | bytes 676
  0.7 17.3 %copy-start = (bf16[2304,112]{0,1:T(8,128)(2,1)S(1)}, bf16[2304,112]{0,1:T(8,128)(2,1)}, u32[]{:S(2)}) copy-start(bf16[2304,112]{0,1:T(8,128)(2,1)} %param.23) | copy-start | bytes 1548292
  0.7 17.3 %copy-start.1 = (bf16[2048,112]{0,1:T(8,128)(2,1)S(1)}, bf16[2048,112]{0,1:T(8,128)(2,1)}, u32[]{:S(2)}) copy-start(bf16[2048,112]{0,1:T(8,128)(2,1)} %param.18) | copy-start | bytes 1376260
  0.7 17.3 %copy-start.2 = (bf16[112,2304]{1,0:T(8,128)(2,1)S(1)}, bf16[112,2304]{1,0:T(8,128)(2,1)}, u32[]{:S(2)}) copy-start(bf16[112,2304]{1,0:T(8,128)(2,1)} %gate_ref) | copy-start | bytes 1548292
  0.7 17.3 %copy-start.3 = (bf16[112,2304]{1,0:T(8,128)(2,1)S(1)}, bf16[112,2304]{1,0:T(8,128)(2,1)}, u32[]{:S(2)}) copy-start(bf16[112,2304]{1,0:T(8,128)(2,1)} %up_ref) | copy-start | bytes 1548292
  0.7 17.3 %copy-start.4 = (bf16[256,112]{0,1:T(8,128)(2,1)S(1)}, bf16[256,112]{0,1:T(8,128)(2,1)}, u32[]{:S(2)}) copy-start(bf16[256,112]{0,1:T(8,128)(2,1)} %param.19) | copy-start | bytes 172036
  4.6 30.9 %all-to-all-start = ((bf16[32,16,512]{2,1,0:T(8,128)(2,1)}), bf16[32,16,512]{2,1,0:T(8,128)(2,1)S(1)}, u32[]{:S(2)}, u32[]{:S(2)}) async-start(bf16[32,16,512]{2,1,0:T(8,128)(2,1)} %shard_map.118), calls=%async_computation | async-start | bytes 1048576 | tf_op jit(solution)/shard_map/all_to_all | solution.py:253
  18.0 26.5 %copy-start.7 = (s32[64]{0:T(128)S(1)}, s32[64]{0:T(128)}, u32[]{:S(2)}) copy-start(s32[64]{0:T(128)} %param.16) | copy-start | bytes 772
  19.8 15.8 %collective-permute-start = (bf16[112,2432]{1,0:T(8,128)(2,1)}, bf16[112,2432]{1,0:T(8,128)(2,1)S(1)}, u32[]{:S(2)}, u32[]{:S(2)}) collective-permute-start(bf16[112,2432]{1,0:T(8,128)(2,1)} %get-tuple-element.86), channel_id=1, source_target_pairs={{0,8},{8,0},{1,9},{9,1},{2,10},{10,2},{3,11},{11,3},{4,12},{12,4},... | collective-permute-start | bytes 1634312 | tf_op jit(solution)/shard_map/ppermute | solution.py:249
  21.7 25.1 %collective-permute-start.1 = (bf16[112,1728]{1,0:T(8,128)(2,1)}, bf16[112,1728]{1,0:T(8,128)(2,1)S(1)}, u32[]{:S(2)}, u32[]{:S(2)}) collective-permute-start(bf16[112,1728]{1,0:T(8,128)(2,1)} %get-tuple-element.79), channel_id=1, source_target_pairs={{0,16},{16,0},{1,17},{17,1},{2,18},{18,2},{3,19},{19,3},{4,20},{20... | collective-permute-start | bytes 1161224 | tf_op jit(solution)/shard_map/ppermute | solution.py:249
  25.3 20.2 %collective-permute-start.2 = (bf16[112,1152]{1,0:T(8,128)(2,1)}, bf16[112,1152]{1,0:T(8,128)(2,1)S(1)}, u32[]{:S(2)}, u32[]{:S(2)}) collective-permute-start(bf16[112,1152]{1,0:T(8,128)(2,1)} %get-tuple-element.80), channel_id=1, source_target_pairs={{0,32},{32,0},{1,33},{33,1},{2,34},{34,2},{3,35},{35,3},{4,36},{36... | collective-permute-start | bytes 774152 | tf_op jit(solution)/shard_map/ppermute | solution.py:249
  29.9 16.9 %collective-permute-start.3 = (bf16[112,1152]{1,0:T(8,128)(2,1)}, bf16[112,1152]{1,0:T(8,128)(2,1)S(1)}, u32[]{:S(2)}, u32[]{:S(2)}) collective-permute-start(bf16[112,1152]{1,0:T(8,128)(2,1)} %get-tuple-element.81), channel_id=1, source_target_pairs={{0,48},{16,32},{32,16},{48,0},{1,49},{17,33},{33,17},{49,1},{2,50}... | collective-permute-start | bytes 774152 | tf_op jit(solution)/shard_map/ppermute | solution.py:257
  36.7 14.5 %all-to-all-start.1 = ((bf16[8,32,128]{2,1,0:T(8,128)(2,1)}), bf16[8,32,128]{2,1,0:T(8,128)(2,1)S(1)}, u32[]{:S(2)}, u32[]{:S(2)}) async-start(bf16[8,32,128]{2,1,0:T(8,128)(2,1)} %shard_map.120), calls=%async_computation.1 | async-start | bytes 131072 | tf_op jit(solution)/shard_map/all_to_all | solution.py:253
  44.5 3.4 %copy-start.5 = (bf16[112,576]{1,0:T(8,128)(2,1)}, bf16[112,576]{1,0:T(8,128)(2,1)S(1)}, u32[]{:S(2)}) copy-start(bf16[112,576]{1,0:T(8,128)(2,1)S(1)} %get-tuple-element.106) | copy-start | bytes 387076
  51.2 26.7 %copy-start.6 = (bf16[112,576]{1,0:T(8,128)(2,1)S(1)}, bf16[112,576]{1,0:T(8,128)(2,1)}, u32[]{:S(2)}) copy-start(bf16[112,576]{1,0:T(8,128)(2,1)} %copy-done.5) | copy-start | bytes 387076
  52.2 17.7 %all-to-all-start.2 = ((bf16[32,32,128]{2,1,0:T(8,128)(2,1)}), bf16[32,32,128]{2,1,0:T(8,128)(2,1)S(1)}, u32[]{:S(2)}, u32[]{:S(2)}) async-start(bf16[32,32,128]{2,1,0:T(8,128)(2,1)} %get-tuple-element.92), calls=%async_computation.2 | async-start | bytes 524288 | tf_op jit(solution)/shard_map/all_to_all | solution.py:253
  58.3 6.3 %collective-permute-start.4 = (bf16[112,1536]{1,0:T(8,128)(2,1)}, bf16[112,1536]{1,0:T(8,128)(2,1)S(1)}, u32[]{:S(2)}, u32[]{:S(2)}) collective-permute-start(bf16[112,1536]{1,0:T(8,128)(2,1)} %get-tuple-element.101), channel_id=1, source_target_pairs={{0,8},{8,0},{1,9},{9,1},{2,10},{10,2},{3,11},{11,3},{4,12},{12,4},... | collective-permute-start | bytes 1032200 | tf_op jit(solution)/shard_map/ppermute | solution.py:249
  60.2 4.4 %collective-permute-start.5 = (bf16[112,1536]{1,0:T(8,128)(2,1)}, bf16[112,1536]{1,0:T(8,128)(2,1)S(1)}, u32[]{:S(2)}, u32[]{:S(2)}) collective-permute-start(bf16[112,1536]{1,0:T(8,128)(2,1)} %pad_maximum_fusion.1), channel_id=1, source_target_pairs={{0,8},{8,0},{1,9},{9,1},{2,10},{10,2},{3,11},{11,3},{4,12},{12,4},... | collective-permute-start | bytes 1032200 | tf_op jit(solution)/shard_map/ppermute | solution.py:249
  62.6 3.8 %collective-permute-start.6 = (bf16[112,1536]{1,0:T(8,128)(2,1)}, bf16[112,1536]{1,0:T(8,128)(2,1)S(1)}, u32[]{:S(2)}, u32[]{:S(2)}) collective-permute-start(bf16[112,1536]{1,0:T(8,128)(2,1)} %get-tuple-element.103), channel_id=1, source_target_pairs={{0,8},{8,0},{1,9},{9,1},{2,10},{10,2},{3,11},{11,3},{4,12},{12,4},... | collective-permute-start | bytes 1032200 | tf_op jit(solution)/shard_map/ppermute | solution.py:249
  71.2 17.8 %all-to-all-start.3 = ((bf16[8,16,1280]{2,1,0:T(8,128)(2,1)}), bf16[8,16,1280]{2,1,0:T(8,128)(2,1)S(1)}, u32[]{:S(2)}, u32[]{:S(2)}) async-start(bf16[8,16,1280]{2,1,0:T(8,128)(2,1)} %shard_map.124), calls=%async_computation.3 | async-start | bytes 655360 | tf_op jit(solution)/shard_map/all_to_all | solution.py:253
  77.9 8.5 %collective-permute-start.7 = (bf16[112,576]{1,0:T(8,128)(2,1)S(1)}, bf16[112,576]{1,0:T(8,128)(2,1)S(1)}, u32[]{:S(2)}, u32[]{:S(2)}) collective-permute-start(bf16[112,576]{1,0:T(8,128)(2,1)S(1)} %copy-done.6), channel_id=1, source_target_pairs={{0,32},{32,0},{1,33},{33,1},{2,34},{34,2},{3,35},{35,3},{4,36},{36... | collective-permute-start | bytes 387080 | tf_op jit(solution)/shard_map/ppermute | solution.py:249
  81.1 3.1 %collective-permute-start.8 = (f32[16,128]{1,0:T(8,128)S(1)}, f32[16,128]{1,0:T(8,128)S(1)}, u32[]{:S(2)}, u32[]{:S(2)}) collective-permute-start(f32[16,128]{1,0:T(8,128)S(1)} %slice.30), channel_id=1, source_target_pairs={{0,8},{8,0},{1,9},{9,1},{2,10},{10,2},{3,11},{11,3},{4,12},{12,4},... | collective-permute-start | bytes 24584 | tf_op jit(solution)/shard_map/ppermute | solution.py:249
  90.0 17.0 %all-to-all-start.4 = ((bf16[16,16,576]{2,1,0:T(8,128)(2,1)}), bf16[16,16,576]{2,1,0:T(8,128)(2,1)S(1)}, u32[]{:S(2)}, u32[]{:S(2)}) async-start(bf16[16,16,576]{2,1,0:T(8,128)(2,1)} %shard_map.125), calls=%async_computation.4 | async-start | bytes 655360 | tf_op jit(solution)/shard_map/all_to_all | solution.py:253
  94.7 9.2 %collective-permute-start.9 = (bf16[112,576]{1,0:T(8,128)(2,1)S(1)}, bf16[112,576]{1,0:T(8,128)(2,1)S(1)}, u32[]{:S(2)}, u32[]{:S(2)}) collective-permute-start(bf16[112,576]{1,0:T(8,128)(2,1)S(1)} %get-tuple-element.110), channel_id=1, source_target_pairs={{0,48},{16,32},{32,16},{48,0},{1,49},{17,33},{33,17},{49,1},{2,50}... | collective-permute-start | bytes 387080 | tf_op jit(solution)/shard_map/ppermute | solution.py:257

commit v9 on v8

--- a/solution.py
+++ b/solution.py
@@ -305,7 +305,9 @@
         3_200_000,
     )(xh, xl, w_gate, w_up, w_down, out_proj, residual, gains)
     carry_other = swap(carry)
-    ff = [ff[0], swap(ff[1], "xl"), swap(ff[2], "xh"), diagonal(ff[3])]
+    far = swap(ff[2], "xh")
+    cross = diagonal(ff[3])
+    ff = [ff[0], swap(ff[1], "xl"), far, cross]
     rows, ff[0] = lax.optimization_barrier((rows, ff[0]))
     part = call(
         out_kernel,
@@ -325,7 +327,8 @@
     down = call(
         pack_down_kernel, [SMEM, SMEM, VMEM], [shape((WIDTH, SIZE))] * 3, (), 0, 1_000_000
     )(xh, xl, w_down)
-    _, _, ff = lax.optimization_barrier((pick, down, ff))
+    *ff, _, _ = lax.optimization_barrier((*ff[::-1], pick, down))
+    ff = ff[::-1]
     joined = jnp.concatenate
     thirds = [
         joined([ff[0], ff[1][:, :384]], axis=1),

time: 131 us -> 129 us (0.985)
  starting transfers between devices: 64.8 us -> 62.2 us
  waiting for transfers between devices: 27.9 us -> 29.4 us
    all_to_all x5, waiting for transfers between devices: 14.4 us -> 17.4 us  [exchange(): return lax.all_to_all(blocks, axes, 0, 0, tiled=True)]
    all_to_all x5, starting transfers between devices: 38.1 us -> 35.7 us  [exchange(): return lax.all_to_all(blocks, axes, 0, 0, tiled=True)]
    ppermute x8, starting transfers between devices: 21.5 us -> 19.4 us  [swap(): return lax.ppermute(value, axis, [(0, 1), (1, 0)])]
    ppermute x2, starting transfers between devices: 5.29 us -> 7.11 us  [diagonal(): return lax.ppermute(value, ('xh', 'xl'), [(i, 3 - i) for i in range(4)])]
  transfers between devices with their start and end apart: 15 -> 15, of which waited for: 11 -> 10; matrix products, arithmetic and copies ran while one was open for 2% -> 2% of each run, Pallas kernels for 3% -> 3%
where the time goes in v9:
time: 129 us; the launch traced here: 128 us
  starting transfers between devices  62.2 us (48%)
  waiting for transfers between devices  29.4 us (23%)
  blocking collectives  19.9 us (15%)
  Pallas kernels  12.1 us (9%)
  other arithmetic  2.36 us (2%)
    all_to_all x5, starting transfers between devices, exchange(): return lax.all_to_all(blocks, axes, 0, 0, tiled=True)  35.7 us
    all_to_all x1, blocking collectives, exchange(): return lax.all_to_all(blocks, axes, 0, 0, tiled=True)  19.9 us
    ppermute x8, starting transfers between devices, swap(): return lax.ppermute(value, axis, [(0, 1), (1, 0)])  19.4 us
    all_to_all x5, waiting for transfers between devices, exchange(): return lax.all_to_all(blocks, axes, 0, 0, tiled=True)  17.4 us
    ppermute x2, starting transfers between devices, diagonal(): return lax.ppermute(value, ('xh', 'xl'), [(i, 3 - i) for i in range(4)])  7.11 us
    ppermute x2, waiting for transfers between devices, diagonal(): return lax.ppermute(value, ('xh', 'xl'), [(i, 3 - i) for i in range(4)])  6.13 us
    ppermute x8, waiting for transfers between devices, swap(): return lax.ppermute(value, axis, [(0, 1), (1, 0)])  5.87 us
    pallas_call x1, Pallas kernels, local(): call(attention_kernel, [SMEM, HBM, VMEM, HBM, HBM], shape((32, 16, 512)),...  3.93 us
  transfers between devices with their start and end apart: 15, of which 10 were waited for; matrix products, arithmetic and copies ran while one was open for 2% of the time, Pallas kernels for 3%

profile of v9, /device:TPU:8, one launch (start us, length us, event | category | flops | bytes accessed | tf_op | source)
XLA Modules:
  0.0 128.0 jit_solution(28767780034742741)
XLA Ops:
  0.7 3.9 %shard_map.118 = bf16[32,16,512]{2,1,0:T(8,128)(2,1)} custom-call(s32[1]{0:T(128)S(6)} %copy.13.len_ref, bf16[64,576]{1,0:T(8,128)(2,1)} %bitcast.22, bf16[4,576]{1,0:T(4,128)(2,1)} %bitcast.23, bf16[576,512]{1,0:T(8,128)(2,1)} %bitcast.21, bf16[16,512,128]{2,1,0:T(8,128)(2,1)} %maps_ref.1), custom_call_target="tpu_custom_call" | custom-call | flops 200000000 | bytes 4000000 | tf_op jit(solution)/shard_map/pallas_call | solution.py:276
  4.6 13.2 %all-to-all-start = ((bf16[32,16,512]{2,1,0:T(8,128)(2,1)}), bf16[32,16,512]{2,1,0:T(8,128)(2,1)S(1)}, u32[]{:S(2)}, u32[]{:S(2)}) async-start(bf16[32,16,512]{2,1,0:T(8,128)(2,1)} %shard_map.118), calls=%async_computation | async-start | bytes 1048576 | tf_op jit(solution)/shard_map/all_to_all | solution.py:253
  17.8 0.0 copy-done.8
  17.9 0.1 broadcast_in_dim.25.gain_ref
  18.0 0.0 copy-start.7
  18.0 1.8 %shard_map.119 = (bf16[112,2432]{1,0:T(8,128)(2,1)}, bf16[112,1152]{1,0:T(8,128)(2,1)S(1)}, bf16[112,1728]{1,0:T(8,128)(2,1)}, bf16[112,1152]{1,0:T(8,128)(2,1)}, bf16[112,1152]{1,0:T(8,128)(2,1)}) custom-call(s32[1]{0:T(128)} %bitcast.xh_ref, s32[1]{0:T(128)} %bitcast.1.xl_ref, bf16[112,2304]{1,0:T(8,128)(2,1)S(1)} %copy-done.2, ...), custom_call_target="tpu_custom_call" | custom-call | bytes 3200000 | tf_op jit(solution)/shard_map/pallas_call | solution.py:298
  19.8 1.9 %collective-permute-start = (bf16[112,2432]{1,0:T(8,128)(2,1)}, bf16[112,2432]{1,0:T(8,128)(2,1)S(1)}, u32[]{:S(2)}, u32[]{:S(2)}) collective-permute-start(bf16[112,2432]{1,0:T(8,128)(2,1)} %get-tuple-element.86), channel_id=1, source_target_pairs={{0,8},{8,0},{1,9},{9,1},{2,10},{10,2},{3,11},{11,3},{4,12},{12,4},... | collective-permute-start | bytes 1634312 | tf_op jit(solution)/shard_map/ppermute | solution.py:249
  21.7 3.6 %collective-permute-start.3 = (bf16[112,1728]{1,0:T(8,128)(2,1)}, bf16[112,1728]{1,0:T(8,128)(2,1)S(1)}, u32[]{:S(2)}, u32[]{:S(2)}) collective-permute-start(bf16[112,1728]{1,0:T(8,128)(2,1)} %get-tuple-element.73), channel_id=1, source_target_pairs={{0,16},{16,0},{1,17},{17,1},{2,18},{18,2},{3,19},{19,3},{4,20},{20... | collective-permute-start | bytes 1161224 | tf_op jit(solution)/shard_map/ppermute | solution.py:249
  25.3 4.0 %collective-permute-start.1 = (bf16[112,1152]{1,0:T(8,128)(2,1)}, bf16[112,1152]{1,0:T(8,128)(2,1)S(1)}, u32[]{:S(2)}, u32[]{:S(2)}) collective-permute-start(bf16[112,1152]{1,0:T(8,128)(2,1)} %get-tuple-element.71), channel_id=1, source_target_pairs={{0,48},{16,32},{32,16},{48,0},{1,49},{17,33},{33,17},{49,1},{2,50}... | collective-permute-start | bytes 774152 | tf_op jit(solution)/shard_map/ppermute | solution.py:257
  29.4 2.5 %collective-permute-start.2 = (bf16[112,1152]{1,0:T(8,128)(2,1)}, bf16[112,1152]{1,0:T(8,128)(2,1)S(1)}, u32[]{:S(2)}, u32[]{:S(2)}) collective-permute-start(bf16[112,1152]{1,0:T(8,128)(2,1)} %get-tuple-element.72), channel_id=1, source_target_pairs={{0,32},{32,0},{1,33},{33,1},{2,34},{34,2},{3,35},{35,3},{4,36},{36... | collective-permute-start | bytes 774152 | tf_op jit(solution)/shard_map/ppermute | solution.py:249
  31.9 3.8 %all-to-all-done.x_ref = bf16[32,16,512]{2,1,0:T(8,128)(2,1)S(1)} async-done(((bf16[32,16,512]{2,1,0:T(8,128)(2,1)}), bf16[32,16,512]{2,1,0:T(8,128)(2,1)S(1)}, u32[]{:S(2)}, u32[]{:S(2)}) %all-to-all-start) | async-done | bytes 524320 | tf_op jit(solution)/shard_map/all_to_all | solution.py:253
  35.6 0.0 collective-permute-done.other_ref
  35.6 1.2 shard_map.120
  36.8 7.5 %all-to-all-start.1 = ((bf16[8,32,128]{2,1,0:T(8,128)(2,1)}), bf16[8,32,128]{2,1,0:T(8,128)(2,1)S(1)}, u32[]{:S(2)}, u32[]{:S(2)}) async-start(bf16[8,32,128]{2,1,0:T(8,128)(2,1)} %shard_map.120), calls=%async_computation.1 | async-start | bytes 131072 | tf_op jit(solution)/shard_map/all_to_all | solution.py:253
  44.3 0.2 shard_map.122
  44.6 0.1 shard_map.121
  44.7 0.0 collective-permute-done.1.refs_3_
  44.8 0.7 collective-permute-done.2.refs_2_
  45.5 0.0 collective-permute-done.3.refs_1_.w1
  45.6 0.9 pad_maximum_fusion
  46.5 0.0 copy-done.5
  46.5 0.8 pad_maximum_fusion.1
  47.2 0.9 slice.28.own_ref
  48.2 3.1 %all-to-all-done.1.part_ref = bf16[8,32,128]{2,1,0:T(8,128)(2,1)S(1)} async-done(((bf16[8,32,128]{2,1,0:T(8,128)(2,1)}), bf16[8,32,128]{2,1,0:T(8,128)(2,1)S(1)}, u32[]{:S(2)}, u32[]{:S(2)}) %all-to-all-start.1) | async-done | bytes 65568 | tf_op jit(solution)/shard_map/all_to_all | solution.py:253
  51.3 1.0 shard_map.123
  52.3 5.4 %all-to-all-start.2 = ((bf16[32,32,128]{2,1,0:T(8,128)(2,1)}), bf16[32,32,128]{2,1,0:T(8,128)(2,1)S(1)}, u32[]{:S(2)}, u32[]{:S(2)}) async-start(bf16[32,32,128]{2,1,0:T(8,128)(2,1)} %get-tuple-element.92), calls=%async_computation.2 | async-start | bytes 524288 | tf_op jit(solution)/shard_map/all_to_all | solution.py:253
  57.6 1.9 %collective-permute-start.4 = (bf16[112,1536]{1,0:T(8,128)(2,1)}, bf16[112,1536]{1,0:T(8,128)(2,1)S(1)}, u32[]{:S(2)}, u32[]{:S(2)}) collective-permute-start(bf16[112,1536]{1,0:T(8,128)(2,1)} %get-tuple-element.101), channel_id=1, source_target_pairs={{0,8},{8,0},{1,9},{9,1},{2,10},{10,2},{3,11},{11,3},{4,12},{12,4},... | collective-permute-start | bytes 1032200 | tf_op jit(solution)/shard_map/ppermute | solution.py:249
  59.6 2.4 %collective-permute-start.5 = (bf16[112,1536]{1,0:T(8,128)(2,1)}, bf16[112,1536]{1,0:T(8,128)(2,1)S(1)}, u32[]{:S(2)}, u32[]{:S(2)}) collective-permute-start(bf16[112,1536]{1,0:T(8,128)(2,1)} %pad_maximum_fusion.1), channel_id=1, source_target_pairs={{0,8},{8,0},{1,9},{9,1},{2,10},{10,2},{3,11},{11,3},{4,12},{12,4},... | collective-permute-start | bytes 1032200 | tf_op jit(solution)/shard_map/ppermute | solution.py:249
  62.0 1.9 %collective-permute-start.6 = (bf16[112,1536]{1,0:T(8,128)(2,1)}, bf16[112,1536]{1,0:T(8,128)(2,1)S(1)}, u32[]{:S(2)}, u32[]{:S(2)}) collective-permute-start(bf16[112,1536]{1,0:T(8,128)(2,1)} %get-tuple-element.103), channel_id=1, source_target_pairs={{0,8},{8,0},{1,9},{9,1},{2,10},{10,2},{3,11},{11,3},{4,12},{12,4},... | collective-permute-start | bytes 1032200 | tf_op jit(solution)/shard_map/ppermute | solution.py:249
  63.9 0.0 collective-permute-done.4.refs_4_
  63.9 0.0 collective-permute-done.5.refs_5_
  63.9 1.8 %collective-permute-done.6.refs_6_ = bf16[112,1536]{1,0:T(8,128)(2,1)S(1)} collective-permute-done((bf16[112,1536]{1,0:T(8,128)(2,1)}, bf16[112,1536]{1,0:T(8,128)(2,1)S(1)}, u32[]{:S(2)}, u32[]{:S(2)}) %collective-permute-start.6) | collective-permute-done | bytes 344096 | tf_op jit(solution)/shard_map/ppermute | solution.py:249
  65.7 3.6 %all-to-all-done.2.full_ref = bf16[32,32,128]{2,1,0:T(8,128)(2,1)S(1)} async-done(((bf16[32,32,128]{2,1,0:T(8,128)(2,1)}), bf16[32,32,128]{2,1,0:T(8,128)(2,1)S(1)}, u32[]{:S(2)}, u32[]{:S(2)}) %all-to-all-start.2) | async-done | bytes 262176 | tf_op jit(solution)/shard_map/all_to_all | solution.py:253
  69.3 1.3 %shard_map.124 = bf16[8,16,1280]{2,1,0:T(8,128)(2,1)} custom-call(s32[1]{0:T(128)} %bitcast.xh_ref, s32[1]{0:T(128)} %bitcast.1.xl_ref, bf16[32,32,128]{2,1,0:T(8,128)(2,1)S(1)} %all-to-all-done.2.full_ref, bf16[112,1152]{1,0:T(8,128)(2,1)S(1)} %get-tuple-element.93.refs_0_, bf16[112,1728]{1,0:T(8,128)(2,1)S(1)} %collective-permute-done.3.refs_1_.w1, ...), custom_call_target="tpu_custom_call" | custom-call | flops 300000000 | bytes 2800000 | tf_op jit(solution)/shard_map/pallas_call | solution.py:346
  70.6 6.1 %all-to-all-start.3 = ((bf16[8,16,1280]{2,1,0:T(8,128)(2,1)}), bf16[8,16,1280]{2,1,0:T(8,128)(2,1)S(1)}, u32[]{:S(2)}, u32[]{:S(2)}) async-start(bf16[8,16,1280]{2,1,0:T(8,128)(2,1)} %shard_map.124), calls=%async_computation.3 | async-start | bytes 655360 | tf_op jit(solution)/shard_map/all_to_all | solution.py:253
  76.7 3.2 %collective-permute-start.7 = (bf16[112,576]{1,0:T(8,128)(2,1)S(1)}, bf16[112,576]{1,0:T(8,128)(2,1)S(1)}, u32[]{:S(2)}, u32[]{:S(2)}) collective-permute-start(bf16[112,576]{1,0:T(8,128)(2,1)S(1)} %copy-done.6), channel_id=1, source_target_pairs={{0,32},{32,0},{1,33},{33,1},{2,34},{34,2},{3,35},{35,3},{4,36},{36... | collective-permute-start | bytes 387080 | tf_op jit(solution)/shard_map/ppermute | solution.py:249
  80.0 1.9 %collective-permute-start.8 = (f32[16,128]{1,0:T(8,128)S(1)}, f32[16,128]{1,0:T(8,128)S(1)}, u32[]{:S(2)}, u32[]{:S(2)}) collective-permute-start(f32[16,128]{1,0:T(8,128)S(1)} %slice.30), channel_id=1, source_target_pairs={{0,8},{8,0},{1,9},{9,1},{2,10},{10,2},{3,11},{11,3},{4,12},{12,4},... | collective-permute-start | bytes 24584 | tf_op jit(solution)/shard_map/ppermute | solution.py:249
  81.9 1.1 collective-permute-done.8.across_ref
  83.0 2.2 %collective-permute-done.7.w2 = bf16[112,576]{1,0:T(8,128)(2,1)S(1)} collective-permute-done((bf16[112,576]{1,0:T(8,128)(2,1)S(1)}, bf16[112,576]{1,0:T(8,128)(2,1)S(1)}, u32[]{:S(2)}, u32[]{:S(2)}) %collective-permute-start.7) | collective-permute-done | bytes 129056 | tf_op jit(solution)/shard_map/ppermute | solution.py:249
  85.2 3.7 %all-to-all-done.3.part_ref = bf16[8,16,1280]{2,1,0:T(8,128)(2,1)S(1)} async-done(((bf16[8,16,1280]{2,1,0:T(8,128)(2,1)}), bf16[8,16,1280]{2,1,0:T(8,128)(2,1)S(1)}, u32[]{:S(2)}, u32[]{:S(2)}) %all-to-all-start.3) | async-done | bytes 327712 | tf_op jit(solution)/shard_map/all_to_all | solution.py:253
  89.0 1.0 shard_map.125
  89.9 3.6 %all-to-all-start.4 = ((bf16[16,16,576]{2,1,0:T(8,128)(2,1)}), bf16[16,16,576]{2,1,0:T(8,128)(2,1)S(1)}, u32[]{:S(2)}, u32[]{:S(2)}) async-start(bf16[16,16,576]{2,1,0:T(8,128)(2,1)} %shard_map.125), calls=%async_computation.4 | async-start | bytes 655360 | tf_op jit(solution)/shard_map/all_to_all | solution.py:253
  93.5 3.1 %collective-permute-start.9 = (bf16[112,576]{1,0:T(8,128)(2,1)S(1)}, bf16[112,576]{1,0:T(8,128)(2,1)S(1)}, u32[]{:S(2)}, u32[]{:S(2)}) collective-permute-start(bf16[112,576]{1,0:T(8,128)(2,1)S(1)} %get-tuple-element.110), channel_id=1, source_target_pairs={{0,48},{16,32},{32,16},{48,0},{1,49},{17,33},{33,17},{49,1},{2,50}... | collective-permute-start | bytes 387080 | tf_op jit(solution)/shard_map/ppermute | solution.py:257
  96.6 6.1 %collective-permute-done.9.w3 = bf16[112,576]{1,0:T(8,128)(2,1)S(1)} collective-permute-done((bf16[112,576]{1,0:T(8,128)(2,1)S(1)}, bf16[112,576]{1,0:T(8,128)(2,1)S(1)}, u32[]{:S(2)}, u32[]{:S(2)}) %collective-permute-start.9) | collective-permute-done | bytes 129056 | tf_op jit(solution)/shard_map/ppermute | solution.py:257
  102.7 3.2 %all-to-all-done.4 = bf16[16,16,576]{2,1,0:T(8,128)(2,1)S(1)} async-done(((bf16[16,16,576]{2,1,0:T(8,128)(2,1)}), bf16[16,16,576]{2,1,0:T(8,128)(2,1)S(1)}, u32[]{:S(2)}, u32[]{:S(2)}) %all-to-all-start.4) | async-done | bytes 294944 | tf_op jit(solution)/shard_map/all_to_all | solution.py:253
  105.9 1.5 %shard_map.126 = bf16[32,32,128]{2,1,0:T(8,128)(2,1)S(1)} custom-call(s32[1]{0:T(128)} %bitcast.xh_ref, s32[1]{0:T(128)} %bitcast.1.xl_ref, s32[1]{0:T(128)} %bitcast.2.core_ref, s32[1]{0:T(128)} %bitcast.3.y_ref, bf16[8,2,16,576]{3,2,1,0:T(8,128)(2,1)S(1)} %bitcast.18, bf16[112,576]{1,0:T(8,128)(2,1)S(1)} %get-tuple-element.112.w0, ...), custom_call_target="tpu_custom_call" | custom-call | flops 200000000 | bytes 1600000 | tf_op jit(solution)/shard_map/pallas_call | solution.py:357
  107.4 19.9 %all_to_all.30 = bf16[32,32,128]{2,1,0:T(8,128)(2,1)S(1)} all-to-all(bf16[32,32,128]{2,1,0:T(8,128)(2,1)S(1)} %shard_map.126), channel_id=1, replica_groups=mesh['z'=8,'xh'=2,'xl'=2,'c'=2,'y'=8] {'xh','xl','y'}, dimensions={0} | all-to-all | bytes 524288 | tf_op jit(solution)/shard_map/all_to_all | solution.py:253
  127.3 0.7 slice_reduce_fusion
  (21 shorter events, 0.1 us)
Async XLA Ops:
  0.7 17.2 %copy-start.8 = (bf16[112]{0:T(256)(128)(2,1)S(1)}, bf16[112]{0:T(256)(128)(2,1)}, u32[]{:S(2)}) copy-start(bf16[112]{0:T(256)(128)(2,1)} %param.20) | copy-start | bytes 676
  0.7 17.3 %copy-start = (bf16[2304,112]{0,1:T(8,128)(2,1)S(1)}, bf16[2304,112]{0,1:T(8,128)(2,1)}, u32[]{:S(2)}) copy-start(bf16[2304,112]{0,1:T(8,128)(2,1)} %param.23) | copy-start | bytes 1548292
  0.7 17.3 %copy-start.1 = (bf16[2048,112]{0,1:T(8,128)(2,1)S(1)}, bf16[2048,112]{0,1:T(8,128)(2,1)}, u32[]{:S(2)}) copy-start(bf16[2048,112]{0,1:T(8,128)(2,1)} %param.18) | copy-start | bytes 1376260
  0.7 17.3 %copy-start.2 = (bf16[112,2304]{1,0:T(8,128)(2,1)S(1)}, bf16[112,2304]{1,0:T(8,128)(2,1)}, u32[]{:S(2)}) copy-start(bf16[112,2304]{1,0:T(8,128)(2,1)} %gate_ref) | copy-start | bytes 1548292
  0.7 17.3 %copy-start.3 = (bf16[112,2304]{1,0:T(8,128)(2,1)S(1)}, bf16[112,2304]{1,0:T(8,128)(2,1)}, u32[]{:S(2)}) copy-start(bf16[112,2304]{1,0:T(8,128)(2,1)} %up_ref) | copy-start | bytes 1548292
  0.7 17.3 %copy-start.4 = (bf16[256,112]{0,1:T(8,128)(2,1)S(1)}, bf16[256,112]{0,1:T(8,128)(2,1)}, u32[]{:S(2)}) copy-start(bf16[256,112]{0,1:T(8,128)(2,1)} %param.19) | copy-start | bytes 172036
  4.6 31.0 %all-to-all-start = ((bf16[32,16,512]{2,1,0:T(8,128)(2,1)}), bf16[32,16,512]{2,1,0:T(8,128)(2,1)S(1)}, u32[]{:S(2)}, u32[]{:S(2)}) async-start(bf16[32,16,512]{2,1,0:T(8,128)(2,1)} %shard_map.118), calls=%async_computation | async-start | bytes 1048576 | tf_op jit(solution)/shard_map/all_to_all | solution.py:253
  18.0 26.6 %copy-start.7 = (s32[64]{0:T(128)S(1)}, s32[64]{0:T(128)}, u32[]{:S(2)}) copy-start(s32[64]{0:T(128)} %param.16) | copy-start | bytes 772
  19.8 15.8 %collective-permute-start = (bf16[112,2432]{1,0:T(8,128)(2,1)}, bf16[112,2432]{1,0:T(8,128)(2,1)S(1)}, u32[]{:S(2)}, u32[]{:S(2)}) collective-permute-start(bf16[112,2432]{1,0:T(8,128)(2,1)} %get-tuple-element.86), channel_id=1, source_target_pairs={{0,8},{8,0},{1,9},{9,1},{2,10},{10,2},{3,11},{11,3},{4,12},{12,4},... | collective-permute-start | bytes 1634312 | tf_op jit(solution)/shard_map/ppermute | solution.py:249
  21.7 23.8 %collective-permute-start.3 = (bf16[112,1728]{1,0:T(8,128)(2,1)}, bf16[112,1728]{1,0:T(8,128)(2,1)S(1)}, u32[]{:S(2)}, u32[]{:S(2)}) collective-permute-start(bf16[112,1728]{1,0:T(8,128)(2,1)} %get-tuple-element.73), channel_id=1, source_target_pairs={{0,16},{16,0},{1,17},{17,1},{2,18},{18,2},{3,19},{19,3},{4,20},{20... | collective-permute-start | bytes 1161224 | tf_op jit(solution)/shard_map/ppermute | solution.py:249
  25.3 19.4 %collective-permute-start.1 = (bf16[112,1152]{1,0:T(8,128)(2,1)}, bf16[112,1152]{1,0:T(8,128)(2,1)S(1)}, u32[]{:S(2)}, u32[]{:S(2)}) collective-permute-start(bf16[112,1152]{1,0:T(8,128)(2,1)} %get-tuple-element.71), channel_id=1, source_target_pairs={{0,48},{16,32},{32,16},{48,0},{1,49},{17,33},{33,17},{49,1},{2,50}... | collective-permute-start | bytes 774152 | tf_op jit(solution)/shard_map/ppermute | solution.py:257
  29.4 16.1 %collective-permute-start.2 = (bf16[112,1152]{1,0:T(8,128)(2,1)}, bf16[112,1152]{1,0:T(8,128)(2,1)S(1)}, u32[]{:S(2)}, u32[]{:S(2)}) collective-permute-start(bf16[112,1152]{1,0:T(8,128)(2,1)} %get-tuple-element.72), channel_id=1, source_target_pairs={{0,32},{32,0},{1,33},{33,1},{2,34},{34,2},{3,35},{35,3},{4,36},{36... | collective-permute-start | bytes 774152 | tf_op jit(solution)/shard_map/ppermute | solution.py:249
  36.8 14.5 %all-to-all-start.1 = ((bf16[8,32,128]{2,1,0:T(8,128)(2,1)}), bf16[8,32,128]{2,1,0:T(8,128)(2,1)S(1)}, u32[]{:S(2)}, u32[]{:S(2)}) async-start(bf16[8,32,128]{2,1,0:T(8,128)(2,1)} %shard_map.120), calls=%async_computation.1 | async-start | bytes 131072 | tf_op jit(solution)/shard_map/all_to_all | solution.py:253
  44.6 1.9 %copy-start.5 = (bf16[112,576]{1,0:T(8,128)(2,1)}, bf16[112,576]{1,0:T(8,128)(2,1)S(1)}, u32[]{:S(2)}) copy-start(bf16[112,576]{1,0:T(8,128)(2,1)S(1)} %get-tuple-element.106) | copy-start | bytes 387076
  51.3 25.5 %copy-start.6 = (bf16[112,576]{1,0:T(8,128)(2,1)S(1)}, bf16[112,576]{1,0:T(8,128)(2,1)}, u32[]{:S(2)}) copy-start(bf16[112,576]{1,0:T(8,128)(2,1)} %copy-done.5) | copy-start | bytes 387076
  52.3 17.0 %all-to-all-start.2 = ((bf16[32,32,128]{2,1,0:T(8,128)(2,1)}), bf16[32,32,128]{2,1,0:T(8,128)(2,1)S(1)}, u32[]{:S(2)}, u32[]{:S(2)}) async-start(bf16[32,32,128]{2,1,0:T(8,128)(2,1)} %get-tuple-element.92), calls=%async_computation.2 | async-start | bytes 524288 | tf_op jit(solution)/shard_map/all_to_all | solution.py:253
  57.6 6.3 %collective-permute-start.4 = (bf16[112,1536]{1,0:T(8,128)(2,1)}, bf16[112,1536]{1,0:T(8,128)(2,1)S(1)}, u32[]{:S(2)}, u32[]{:S(2)}) collective-permute-start(bf16[112,1536]{1,0:T(8,128)(2,1)} %get-tuple-element.101), channel_id=1, source_target_pairs={{0,8},{8,0},{1,9},{9,1},{2,10},{10,2},{3,11},{11,3},{4,12},{12,4},... | collective-permute-start | bytes 1032200 | tf_op jit(solution)/shard_map/ppermute | solution.py:249
  59.6 4.4 %collective-permute-start.5 = (bf16[112,1536]{1,0:T(8,128)(2,1)}, bf16[112,1536]{1,0:T(8,128)(2,1)S(1)}, u32[]{:S(2)}, u32[]{:S(2)}) collective-permute-start(bf16[112,1536]{1,0:T(8,128)(2,1)} %pad_maximum_fusion.1), channel_id=1, source_target_pairs={{0,8},{8,0},{1,9},{9,1},{2,10},{10,2},{3,11},{11,3},{4,12},{12,4},... | collective-permute-start | bytes 1032200 | tf_op jit(solution)/shard_map/ppermute | solution.py:249
  62.0 3.8 %collective-permute-start.6 = (bf16[112,1536]{1,0:T(8,128)(2,1)}, bf16[112,1536]{1,0:T(8,128)(2,1)S(1)}, u32[]{:S(2)}, u32[]{:S(2)}) collective-permute-start(bf16[112,1536]{1,0:T(8,128)(2,1)} %get-tuple-element.103), channel_id=1, source_target_pairs={{0,8},{8,0},{1,9},{9,1},{2,10},{10,2},{3,11},{11,3},{4,12},{12,4},... | collective-permute-start | bytes 1032200 | tf_op jit(solution)/shard_map/ppermute | solution.py:249
  70.6 18.3 %all-to-all-start.3 = ((bf16[8,16,1280]{2,1,0:T(8,128)(2,1)}), bf16[8,16,1280]{2,1,0:T(8,128)(2,1)S(1)}, u32[]{:S(2)}, u32[]{:S(2)}) async-start(bf16[8,16,1280]{2,1,0:T(8,128)(2,1)} %shard_map.124), calls=%async_computation.3 | async-start | bytes 655360 | tf_op jit(solution)/shard_map/all_to_all | solution.py:253
  76.7 8.5 %collective-permute-start.7 = (bf16[112,576]{1,0:T(8,128)(2,1)S(1)}, bf16[112,576]{1,0:T(8,128)(2,1)S(1)}, u32[]{:S(2)}, u32[]{:S(2)}) collective-permute-start(bf16[112,576]{1,0:T(8,128)(2,1)S(1)} %copy-done.6), channel_id=1, source_target_pairs={{0,32},{32,0},{1,33},{33,1},{2,34},{34,2},{3,35},{35,3},{4,36},{36... | collective-permute-start | bytes 387080 | tf_op jit(solution)/shard_map/ppermute | solution.py:249
  80.0 3.1 %collective-permute-start.8 = (f32[16,128]{1,0:T(8,128)S(1)}, f32[16,128]{1,0:T(8,128)S(1)}, u32[]{:S(2)}, u32[]{:S(2)}) collective-permute-start(f32[16,128]{1,0:T(8,128)S(1)} %slice.30), channel_id=1, source_target_pairs={{0,8},{8,0},{1,9},{9,1},{2,10},{10,2},{3,11},{11,3},{4,12},{12,4},... | collective-permute-start | bytes 24584 | tf_op jit(solution)/shard_map/ppermute | solution.py:249
  89.9 16.0 %all-to-all-start.4 = ((bf16[16,16,576]{2,1,0:T(8,128)(2,1)}), bf16[16,16,576]{2,1,0:T(8,128)(2,1)S(1)}, u32[]{:S(2)}, u32[]{:S(2)}) async-start(bf16[16,16,576]{2,1,0:T(8,128)(2,1)} %shard_map.125), calls=%async_computation.4 | async-start | bytes 655360 | tf_op jit(solution)/shard_map/all_to_all | solution.py:253
  93.5 9.2 %collective-permute-start.9 = (bf16[112,576]{1,0:T(8,128)(2,1)S(1)}, bf16[112,576]{1,0:T(8,128)(2,1)S(1)}, u32[]{:S(2)}, u32[]{:S(2)}) collective-permute-start(bf16[112,576]{1,0:T(8,128)(2,1)S(1)} %get-tuple-element.110), channel_id=1, source_target_pairs={{0,48},{16,32},{32,16},{48,0},{1,49},{17,33},{33,17},{49,1},{2,50}... | collective-permute-start | bytes 387080 | tf_op jit(solution)/shard_map/ppermute | solution.py:257
